TPU v7x, 128 devices: a whole 4x4x4 slice. The times are simulated.
128 devices in a mesh: seq: 64 (over z, y, x), mp: 2 (over core).
Axes of the slice: x: 4, y: 4, z: 4, core: 2. Of those that a mesh axis runs over, the one named last changes fastest.
Arguments:
- tokens: bfloat16 [16384, 2048], P('seq'), may hold values from -6 to 6
- cotangent: bfloat16 [16384, 2048], P('seq'), may hold values from -6 to 6
- starts: int32 [16384], P('seq'), may hold values from 0 to 1, as said below
- valid: int32 [16384], P('seq'), may hold values 0 or 1
- w_rec: bfloat16 [2048, 2, 2560], P('seq', None, 'mp'), may hold values from -0.125 to 0.125
- w_out: bfloat16 [2560, 2048], P('mp', 'seq'), may hold values from -0.25 to 0.25
- w_mlp: bfloat16 [2048, 2, 6144], P('seq', None, 'mp'), may hold values from -0.125 to 0.125
- w_down: bfloat16 [6144, 2048], P('mp', 'seq'), may hold values from -0.15625 to 0.15625
- lru_gates: bfloat16 [2, 10, 256, 256], P(None, 'mp'), may hold values from -0.375 to 0.375
- lru_bias: float32 [2, 2560], P(None, 'mp'), may hold values from -4 to 4
- lam: float32 [2560], P('mp'), may hold values from 4 to 16
- conv_w: float32 [4, 2560], P(None, 'mp'), may hold values from -3 to 3
- conv_b: float32 [2560], P('mp'), may hold values from -2 to 2
- gain_rec: float32 [2048], replicated, may hold values from 0.1 to 1.9
- gain_mlp: float32 [2048], replicated, may hold values from 0.1 to 1.9
- h_init: float32 [2560], P('mp'), may hold values from -5 to 5
- conv_state: float32 [3, 2560], P(None, 'mp'), may hold values from -5 to 5
Outputs:
- result: bfloat16 [16384, 2048], P('seq')
- rms_rec: float32 [16384], P('seq')
- rms_mlp: float32 [16384], P('seq')
- grad_tokens: float32 [16384, 2048], P('seq')
- grad_w_rec: float32 [2048, 2, 2560], P('seq', None, 'mp')
- grad_w_out: float32 [2560, 2048], P('mp', 'seq')
- grad_w_mlp: float32 [2048, 2, 6144], P('seq', None, 'mp')
- grad_w_down: float32 [6144, 2048], P('mp', 'seq')
- grad_lru_gates: float32 [2, 10, 256, 256], P(None, 'mp')
- grad_lru_bias: float32 [2, 2560], P(None, 'mp')
- grad_lam: float32 [2560], P('mp')
- grad_conv_w: float32 [4, 2560], P(None, 'mp')
- conv_bias_gradient: float32 [2560], P('mp')
- grad_gain_rec: float32 [2048], replicated
- grad_gain_mlp: float32 [2048], replicated
- grad_h_init: float32 [2560], P('mp')
- grad_conv_state: float32 [3, 2560], P(None, 'mp')
Inputs may be any that keep to these rules, and one draw needn't show every extreme that they name: `starts`: 1 at exactly two tokens: one among the first 256 tokens but not the very first, one among the last 256; 0 elsewhere.
All inputs are finite; a program needn't handle non-finite values. No bound on the sum of `valid` on one device may be relied on, other than what follows from the above.
Results may differ from a plain program's by a relative error of at most 0.018.
Values may be sent and summed in bfloat16 or wider, within the bound.
A program may use at most 448 MiB of HBM per device.

v0:
```python
import jax
import jax.numpy as jnp
from jax import lax
from jax.sharding import PartitionSpec as P

D = 2048
CONV = 4


EPSILON = 1e-06


def from_behind(block, axis, distance):
    devices = range(lax.axis_size(axis))
    route = [(i - distance, i) for i in devices if i - distance in devices]
    return lax.ppermute(block, axis, route)


def carried_in(value, axis, join, neutral, backward):
    count, mine = (lax.axis_size(axis), lax.axis_index(axis))
    pieces = jax.tree.map(lambda part: lax.all_gather(part, axis), value)
    if backward:
        pieces = jax.tree.map(lambda part: part[::-1], pieces)
        mine = count - 1 - mine
    running = jax.tree.map(
        lambda part, zero: jnp.full_like(part, 0) + jnp.asarray(zero, part.dtype), value, neutral
    )

    def lap(position, running):
        longer = join(running, jax.tree.map(lambda part: part[position], pieces))
        return jax.tree.map(lambda new, old: jnp.where(position < mine, new, old), longer, running)

    return lax.fori_loop(0, count - 1, lap, running)


def rms_norm(values):
    mean_sq = jnp.mean(values * values, axis=-1, keepdims=True)
    inverse = lax.rsqrt(mean_sq + EPSILON)
    return (values * inverse, inverse, jnp.sqrt(mean_sq[:, 0] + EPSILON))


def rms_back(grad_normed, normed, inverse, scales):
    grad_hat = grad_normed * scales
    inner_mean = jnp.mean(grad_hat * normed, axis=-1, keepdims=True)
    return (inverse * (grad_hat - normed * inner_mean), jnp.sum(grad_normed * normed, axis=0))


def linear_recurrence_scan(decay_multipliers, scan_increments):

    def merge_pairs(earlier, later):
        return (earlier[0] * later[0], later[1] + later[0] * earlier[1])

    return lax.associative_scan(merge_pairs, (decay_multipliers, scan_increments), axis=0)


def chain_combine(earlier, later):
    return (earlier[0] * later[0], later[1] + later[0] * earlier[1])


def fold_rows(weight, fold_fn, init):
    return fold_fn(init, lax.all_gather(weight, "seq", axis=0, tiled=True), jnp.int32(0))


def project_in(normed, weight):
    flat_width = weight.shape[1] * weight.shape[2]

    def accumulate(running, weight_piece, first_row):
        row_count = weight_piece.shape[0]
        return jnp.dot(
            normed, weight_piece.reshape(row_count, flat_width), preferred_element_type=jnp.float32
        )

    running = fold_rows(weight, accumulate, jnp.zeros((normed.shape[0], flat_width), jnp.float32))
    return running.reshape(normed.shape[0], weight.shape[1], weight.shape[2])


def project_in_back(grads_low, weight):
    token_count = grads_low.shape[0]
    flat_grads = grads_low.reshape(token_count, -1)

    def place(running, weight_piece, first_row):
        row_count = weight_piece.shape[0]
        products = lax.dot_general(
            flat_grads,
            weight_piece.reshape(row_count, -1),
            (((1,), (1,)), ((), ())),
            preferred_element_type=jnp.float32,
        )
        return products

    return fold_rows(weight, place, jnp.zeros((token_count, D), jnp.float32))


def project_out(values, weight):
    return jnp.dot(
        values,
        lax.all_gather(weight, "seq", axis=1, tiled=True),
        preferred_element_type=jnp.float32,
    )


def project_out_back(grad_low, weight):

    def accumulate(running, weight_piece, first_col):
        return lax.dot_general(
            grad_low, weight_piece, (((1,), (1,)), ((), ())), preferred_element_type=jnp.float32
        )

    return accumulate(
        jnp.zeros((grad_low.shape[0], weight.shape[0]), jnp.float32),
        lax.all_gather(weight, "seq", axis=1, tiled=True),
        jnp.int32(0),
    )


def model_sum(values):
    return lax.psum(values.astype(jnp.bfloat16), "mp").astype(jnp.float32)


def gradient_total(values):
    return lax.psum(values.astype(jnp.bfloat16), "mp").astype(jnp.float32)


def make_terms(pairs):
    parts = []
    for left_side, right_side in pairs:
        parts.append(
            lax.dot_general(
                left_side, right_side, (((0,), (0,)), ((), ())), preferred_element_type=jnp.float32
            )
        )
    return jnp.concatenate(parts, axis=1)


def body(
    tokens,
    cotangent,
    starts,
    valid,
    w_rec,
    w_out,
    w_mlp,
    w_down,
    lru_gates,
    lru_bias,
    lam,
    conv_w,
    conv_b,
    gain_rec,
    gain_mlp,
    h_init,
    conv_state,
):
    token_count = tokens.shape[0]
    rec_half = w_rec.shape[2]
    mlp_half = w_mlp.shape[2]
    shard_rows = w_rec.shape[0]
    block_count = lru_gates.shape[1]
    block_size = lru_gates.shape[3]
    seq_index = lax.axis_index("seq")
    is_first = seq_index == 0
    edge_rows = CONV - 1
    tokens_wide = tokens.astype(jnp.float32)
    hat_rec, inverse_rec, rms_rec = rms_norm(tokens_wide)
    normed_rec = (hat_rec * gain_rec).astype(jnp.bfloat16)
    projected = project_in(normed_rec, w_rec)
    before = from_behind(projected[token_count - edge_rows :, 1], "seq", 1)
    gate_lin = projected[:, 0]
    rec_lin = projected[:, 1]
    before = jnp.where(is_first, conv_state, before)
    conv_in = jnp.concatenate([before, rec_lin], axis=0)
    conv_out = conv_b + sum(
        (conv_w[offset] * conv_in[offset : offset + token_count] for offset in range(CONV))
    )
    mixed_in = conv_out.astype(jnp.bfloat16)
    mixed_blocks = mixed_in.reshape(token_count, block_count, block_size)
    gate_logits = jnp.einsum(
        "tnk,gnkj->gtnj", mixed_blocks, lru_gates, preferred_element_type=jnp.float32
    )
    gate_logits = gate_logits.reshape(2, token_count, rec_half) + lru_bias[:, None, :]
    reset_gate = jax.nn.sigmoid(gate_logits[0])
    input_gate = jax.nn.sigmoid(gate_logits[1])
    rates = jax.nn.softplus(-lam)
    log_decay = -8.0 * rates * reset_gate
    decays = jnp.exp(log_decay)
    scale_in = jnp.sqrt(-jnp.expm1(2.0 * log_decay))
    mixed_wide = mixed_in.astype(jnp.float32)
    driven = scale_in * input_gate * mixed_wide
    keep_mask = (1 - starts).astype(jnp.float32)[:, None]
    decay_multipliers = decays * keep_mask
    cum_factor, cum_state = linear_recurrence_scan(decay_multipliers, driven)
    identity = (jnp.ones((rec_half,), jnp.float32), jnp.zeros((rec_half,), jnp.float32))
    prefix_factor, prefix_state = carried_in(
        (cum_factor[-1], cum_state[-1]), "seq", chain_combine, identity, False
    )
    carry_in = prefix_state + prefix_factor * h_init
    states = cum_state + cum_factor * carry_in[None, :]
    gate_act, gate_pull = jax.vjp(jax.nn.gelu, gate_lin)
    branch_in = (gate_act * states).astype(jnp.bfloat16)
    hidden = tokens_wide + model_sum(project_out(branch_in, w_out))
    hat_mlp, inverse_mlp, rms_mlp = rms_norm(hidden)
    normed_mlp = (hat_mlp * gain_mlp).astype(jnp.bfloat16)
    gate_up = project_in(normed_mlp, w_mlp)
    mlp_act, mlp_pull = jax.vjp(jax.nn.gelu, gate_up[:, 0])
    mlp_in = (mlp_act * gate_up[:, 1]).astype(jnp.bfloat16)
    mlp_terms = project_out(mlp_in, w_down)
    mlp_out = model_sum(mlp_terms)
    result = (hidden + mlp_out).astype(jnp.bfloat16)
    grad_out = cotangent.astype(jnp.float32) * valid.astype(jnp.float32)[:, None]
    grad_out_low = grad_out.astype(jnp.bfloat16)
    grad_mlp_in = project_out_back(grad_out_low, w_down)
    grad_gate = mlp_pull(grad_mlp_in * gate_up[:, 1])[0]
    grad_up = grad_mlp_in * mlp_act
    grad_gate_up = jnp.stack([grad_gate, grad_up], axis=1).astype(jnp.bfloat16)
    mlp_pairs = ((normed_mlp, grad_gate_up.reshape(token_count, -1)), (grad_out_low, mlp_in))
    mlp_back_terms = project_in_back(grad_gate_up, w_mlp)
    grad_normed_mlp = gradient_total(mlp_back_terms)
    grad_hidden_norm, grad_gain_mlp = rms_back(grad_normed_mlp, hat_mlp, inverse_mlp, gain_mlp)
    grad_hidden = grad_out + grad_hidden_norm
    grad_hidden_low = grad_hidden.astype(jnp.bfloat16)
    grad_branch = project_out_back(grad_hidden_low, w_out)
    grad_gate_lin = gate_pull(grad_branch * states)[0]
    grad_states = grad_branch * gate_act
    factor_next = jnp.concatenate(
        [decay_multipliers[1:], jnp.ones((1, rec_half), jnp.float32)], axis=0
    )
    back_factor, back_adjoint = linear_recurrence_scan(factor_next[::-1], grad_states[::-1])
    cum_back = back_factor[::-1]
    adjoint_local = back_adjoint[::-1]
    later_factor, later_adjoint = carried_in(
        (decay_multipliers[0] * cum_back[0], decay_multipliers[0] * adjoint_local[0]),
        "seq",
        chain_combine,
        identity,
        True,
    )
    adjoint = adjoint_local + cum_back * later_adjoint[None, :]
    grad_h_term = jnp.where(
        is_first, decay_multipliers[0] * adjoint[0], jnp.zeros((rec_half,), jnp.float32)
    )
    prev_states = jnp.concatenate([carry_in[None, :], states[:-1]], axis=0)
    grad_scale = adjoint * input_gate * mixed_wide
    grad_input_gate = adjoint * scale_in * mixed_wide
    grad_log = adjoint * prev_states * keep_mask * decays - grad_scale * decays * decays / scale_in
    grad_lam = jnp.sum(grad_log * 8.0 * reset_gate, axis=0) * jax.nn.sigmoid(-lam)
    grad_logits = jnp.stack(
        [
            grad_log * (-8.0 * rates) * reset_gate * (1.0 - reset_gate),
            grad_input_gate * input_gate * (1.0 - input_gate),
        ],
        axis=0,
    ).astype(jnp.bfloat16)
    grad_bias = jnp.sum(grad_logits.astype(jnp.float32), axis=1)
    grad_blocks = grad_logits.reshape(2, token_count, block_count, block_size)
    grad_gates = jnp.einsum(
        "tnk,gtnj->gnkj", mixed_blocks, grad_blocks, preferred_element_type=jnp.float32
    )
    grad_mixed = adjoint * scale_in * input_gate
    grad_mixed = grad_mixed + jnp.einsum(
        "gtnj,gnkj->tnk", grad_blocks, lru_gates, preferred_element_type=jnp.float32
    ).reshape(token_count, rec_half)
    conv_bias_gradient = jnp.sum(grad_mixed, axis=0)
    grad_conv_w = jnp.stack(
        [
            jnp.sum(grad_mixed * conv_in[offset : offset + token_count], axis=0)
            for offset in range(CONV)
        ],
        axis=0,
    )
    grad_conv_in = jnp.zeros((token_count + edge_rows, rec_half), jnp.float32)
    for offset in range(CONV):
        grad_conv_in = grad_conv_in + jnp.pad(
            conv_w[offset] * grad_mixed, ((offset, edge_rows - offset), (0, 0))
        )
    edge_back = from_behind(grad_conv_in[:edge_rows], "seq", -1)
    grad_rec_lin = grad_conv_in[edge_rows:] + jnp.pad(
        edge_back, ((token_count - edge_rows, 0), (0, 0))
    )
    state_term_gradient = jnp.where(
        is_first, grad_conv_in[:edge_rows], jnp.zeros((edge_rows, rec_half), jnp.float32)
    )
    grad_proj = jnp.stack([grad_gate_lin, grad_rec_lin], axis=1).astype(jnp.bfloat16)
    grad_normed_rec = gradient_total(project_in_back(grad_proj, w_rec))
    token_norm_gradient, grad_gain_rec = rms_back(grad_normed_rec, hat_rec, inverse_rec, gain_rec)
    grad_tokens = grad_hidden + token_norm_gradient
    rec_pairs = ((normed_rec, grad_proj.reshape(token_count, -1)), (grad_hidden_low, branch_in))
    all_grads = lax.psum_scatter(
        make_terms(rec_pairs + mlp_pairs), "seq", scatter_dimension=0, tiled=True
    )
    rec_grads = all_grads[:, : 3 * rec_half]
    mlp_grads = all_grads[:, 3 * rec_half :]
    grad_w_rec = rec_grads[:, : 2 * rec_half].reshape(shard_rows, 2, rec_half)
    grad_w_out = rec_grads[:, 2 * rec_half :].T
    grad_w_mlp = mlp_grads[:, : 2 * mlp_half].reshape(shard_rows, 2, mlp_half)
    grad_w_down = mlp_grads[:, 2 * mlp_half :].T
    summed = lax.psum(
        (
            grad_gates,
            grad_bias,
            grad_lam,
            grad_conv_w,
            conv_bias_gradient,
            grad_gain_rec,
            grad_gain_mlp,
            grad_h_term,
            state_term_gradient,
        ),
        "seq",
    )
    return (
        result,
        rms_rec,
        rms_mlp,
        grad_tokens,
        grad_w_rec,
        grad_w_out,
        grad_w_mlp,
        grad_w_down,
        summed[0],
        summed[1],
        summed[2],
        summed[3],
        summed[4],
        summed[5],
        summed[6],
        summed[7],
        summed[8],
    )


def solution(mesh):
    placed = (
        P("seq", None),
        P("seq", None),
        P("seq"),
        P("seq"),
        P("seq", None, "mp"),
        P("mp", "seq"),
        P("seq", None, "mp"),
        P("mp", "seq"),
        P(None, "mp", None, None),
        P(None, "mp"),
        P("mp"),
        P(None, "mp"),
        P("mp"),
        P(),
        P(),
        P("mp"),
        P(None, "mp"),
    )
    return jax.shard_map(
        body,
        mesh=mesh,
        in_specs=placed,
        out_specs=(
            P("seq", None),
            P("seq"),
            P("seq"),
            P("seq", None),
            P("seq", None, "mp"),
            P("mp", "seq"),
            P("seq", None, "mp"),
            P("mp", "seq"),
            P(None, "mp", None, None),
            P(None, "mp"),
            P("mp"),
            P(None, "mp"),
            P("mp"),
            P(),
            P(),
            P("mp"),
            P(None, "mp"),
        ),
        check_vma=False,
    )
```

profile of v0, /device:TPU:0, one launch (start us, length us, event | category | flops | bytes accessed | tf_op | source)
XLA Modules:
  0.0 2347.3 jit_solution(4587254864698257874)
XLA Ops:
  12.8 86.4 %all-gather.9.cloned.1.call-done = bf16[2048,2,1280]{2,0,1:T(8,128)(2,1)} async-done(((bf16[32,2,1280]{2,0,1:T(8,128)(2,1)}), bf16[2048,2,1280]{2,0,1:T(8,128)(2,1)}) %all-gather.9.cloned.1.call-update) | async-done | bytes 10485776 | tf_op jit(solution)/shard_map/all_gather | solution.py:61
  99.2 14.4 copy.69
  113.6 5.7 fusion.2
  139.2 4.2 slice.596
  143.5 4.2 slice.594
  147.7 4.3 slice.592
  153.4 4.2 slice.599
  157.6 4.3 slice.595
  184.3 4.3 slice.593
  210.5 4.8 pad.249
  217.6 5.0 pad.233
  226.4 4.9 pad.248
  232.1 177.4 %all-gather = f32[64,1,1280]{2,1,0:T(1,128)S(1)} all-gather(f32[1,1,1280]{2,1,0:T(1,128)S(1)} %add_bitcast_fusion.1), channel_id=1, replica_groups=mesh['seq'=64,'mp'=2] {'seq'}, dimensions={0}, use_global_device_ids=true | all-gather | bytes 332800 | tf_op jit(solution)/shard_map/all_gather | solution.py:21
  410.4 4.9 pad.232
  416.1 170.9 %all-gather.1 = f32[64,1,1280]{2,1,0:T(1,128)S(1)} all-gather(f32[1,1,1280]{2,1,0:T(1,128)S(1)} %add_bitcast_fusion), channel_id=1, replica_groups=mesh['seq'=64,'mp'=2] {'seq'}, dimensions={0}, use_global_device_ids=true | all-gather | bytes 332800 | tf_op jit(solution)/shard_map/all_gather | solution.py:21
  587.1 5.6 while.30
  592.7 4.6 multiply_convert_fusion.3
  597.3 5.2 convolution_convert_fusion.1
  608.4 4.2 slice.683
  615.8 4.2 slice.673
  620.0 5.9 slice.684
  626.0 6.0 slice.674
  637.4 122.3 %all-gather.13.cloned.1.call-done = bf16[2048,2,3072]{2,0,1:T(8,128)(2,1)} async-done(((bf16[32,2,3072]{2,0,1:T(8,128)(2,1)}), bf16[2048,2,3072]{2,0,1:T(8,128)(2,1)}) %all-gather.13.cloned.1.call-update) | async-done | bytes 25165840 | tf_op jit(solution)/shard_map/all_gather | solution.py:61
  759.7 32.8 %copy.76 = bf16[2048,2,3072]{0,2,1:T(8,128)(2,1)} copy(bf16[2048,2,3072]{2,0,1:T(8,128)(2,1)} %all-gather.13.cloned.1.call-done) | data formatting | bytes 50331648 | tf_op jit(solution)/shard_map/all_gather | solution.py:61
  792.5 13.9 fusion
  806.4 5.1 multiply_convert_fusion
  811.4 41.9 %all-gather.15.cloned.1.call-done = bf16[3072,2048]{0,1:T(8,128)(2,1)} async-done(((bf16[3072,32]{0,1:T(8,128)(2,1)}), bf16[3072,2048]{0,1:T(8,128)(2,1)}) %all-gather.15.cloned.1.call-update) | async-done | bytes 12582928 | tf_op jit(solution)/shard_map/all_gather | solution.py:97
  853.4 12.2 fusion.10
  869.3 4.7 copy.84
  874.0 24.4 %fusion.15 = bf16[256,2048]{1,0:T(8,128)(2,1)} fusion(bf16[2048,2,3072]{2,0,1:T(8,128)(2,1)} %all-gather.13.cloned.1.call-done, bf16[256,1,3072]{2,0,1:T(8,128)(2,1)} %copy-done.44, bf16[256,1,3072]{2,0,1:T(8,128)(2,1)} %copy-done.43), kind=kOutput, calls=%fused_computation.41 | convolution fusion | flops 6444548096 | bytes 29360128 | tf_op jit(solution)/shard_map/dot_general | solution.py:83
  898.5 9.5 convolution_convert_fusion
  907.9 15.4 all-reduce.81.cloned.1.call-done
  926.2 6.1 fusion.69
  934.1 4.2 slice.679
  938.3 4.2 slice.675
  942.6 4.2 slice.670
  946.8 5.9 slice.680
  952.7 5.9 slice.676
  1024.6 6.0 slice.671
  1103.8 5.0 pad.264
  1108.8 4.9 pad.280
  1113.7 4.9 pad.281
  1118.7 4.9 pad.265
  1128.6 10.8 rev.15
  1139.4 10.8 rev.14
  1150.2 178.3 %all-gather.3 = f32[64,1,1280]{2,1,0:T(1,128)S(1)} all-gather(f32[1,1,1280]{2,1,0:T(1,128)S(1)} %get-tuple-element.388), channel_id=1, replica_groups=mesh['seq'=64,'mp'=2] {'seq'}, dimensions={0}, use_global_device_ids=true | all-gather | bytes 332800 | tf_op jit(solution)/shard_map/all_gather | solution.py:21
  1329.2 5.5 rev.17
  1334.7 170.9 %all-gather.2 = f32[64,1,1280]{2,1,0:T(1,128)S(1)} all-gather(f32[1,1,1280]{2,1,0:T(1,128)S(1)} %get-tuple-element.389), channel_id=1, replica_groups=mesh['seq'=64,'mp'=2] {'seq'}, dimensions={0}, use_global_device_ids=true | all-gather | bytes 332800 | tf_op jit(solution)/shard_map/all_gather | solution.py:21
  1506.3 5.9 rev.16
  1512.2 55.5 %while.31 = (s32[]{:T(128)}, f32[1280]{0:T(1024)S(1)}, s32[]{:T(128)}, f32[64,1280]{1,0:T(8,128)}, f32[64,1280]{1,0:T(8,128)}, /*index=5*/s32[]{:T(128)}, s32[]{:T(128)}) while((s32[]{:T(128)}, f32[1280]{0:T(1024)S(1)}, s32[]{:T(128)}, f32[64,1280]{1,0:T(8,128)}, f32[64,1280]{1,0:T(8,128)}, /*index=5*/s32[]{:T(128)}, ...), condition=%wide.region_9.10_spmd.clone, body=%wide.region_8.9_spmd.clone.sunk | while | flops 5124 | bytes 41069 | solution.py:33
  1567.8 4.0 fusion.38
  1571.8 4.3 multiply_reduce_fusion.5
  1593.6 5.4 fusion.108
  1601.9 4.0 collective-permute-done.1
  1606.0 4.0 fusion.16
  1610.7 22.9 fusion.105
  1633.6 11.7 fusion.70
  1648.0 8.0 fusion.65
  1659.7 10.3 fusion.76
  1670.0 70.3 %pad_maximum_fusion = f32[2048,13056]{1,0:T(8,128)} fusion(f32[2048,3072]{1,0:T(8,128)} %fusion.70, f32[2048,6144]{1,0:T(8,128)} %fusion.105, f32[2048,1280]{1,0:T(8,128)} %fusion.65, f32[2048,2560]{1,0:T(8,128)} %fusion.76), kind=kLoop, calls=%fused_computation.7 | loop fusion | flops 80216064 | bytes 213909504 | tf_op jit(solution)/shard_map/concatenate | solution.py:132
  1748.1 5.2 fusion.21
  1753.3 23.8 %all-reduce.83.cloned.1.call-done = f32[2,5,256,256]{2,3,0,1:T(8,128)} async-done(((f32[2,5,256,256]{2,3,0,1:T(8,128)}), f32[2,5,256,256]{2,3,0,1:T(8,128)}) %all-reduce.83.cloned.1.call-update) | async-done | bytes 2621456 | tf_op jit(solution)/shard_map/psum | solution.py:296
  1780.3 417.2 %reduce-scatter.2.cloned.1.call-done = f32[32,13056]{1,0:T(8,128)} async-done(((f32[2048,13056]{1,0:T(8,128)}), f32[32,13056]{1,0:T(8,128)}) %reduce-scatter.2.cloned.1.call-update) | async-done | bytes 1671184 | tf_op jit(solution)/shard_map/reduce_scatter | solution.py:287
  2203.6 126.2 %all-reduce.85.cloned.1.call-done = (f32[2,1280]{1,0:T(2,128)}, f32[1280]{0:T(1024)}, f32[4,1280]{1,0:T(4,128)}, f32[1280]{0:T(1024)}, f32[2048]{0:T(1024)}, /*i...) async-done(((f32[2,1280]{1,0:T(2,128)}, f32[1280]{0:T(1024)}, f32[4,1280]{1,0:T(4,128)}, f32[1280]{0:T(1024)}, f32[2048]{0:T(1024)}, /*index=5*/f32[2048]{0:T(1024)}, ...) | async-done | bytes 77840 | tf_op jit(solution)/shard_map/psum | solution.py:296
  (800 shorter events, 359.1 us)
Async XLA Ops:
  7.2 118.9 %copy-start = (bf16[2,5,256,256]{3,2,1,0:T(8,128)(2,1)S(1)}, bf16[2,5,256,256]{3,2,1,0:T(8,128)(2,1)}, u32[]{:S(2)}) copy-start(bf16[2,5,256,256]{3,2,1,0:T(8,128)(2,1)} %param.29) | copy-start | bytes 3932164
  7.2 5.4 copy-start.73
  7.2 5.4 copy-start.83
  7.2 91.9 %all-gather.9.cloned.1.call-start = ((), (), s32[]{:S(2)}) async-start(), calls=%async_computation.1 | async-start | bytes 10649600 | tf_op jit(solution)/shard_map/all_gather | solution.py:61
  9.0 588.3 %all-gather.11.cloned.1.call-start = ((), (), s32[]{:S(2)}) async-start(), calls=%async_computation.2 | async-start | bytes 5324800 | tf_op jit(solution)/shard_map/all_gather | solution.py:97
  9.7 625.4 %all-reduce.79.cloned.1.call-start = ((), (), s32[]{:S(2)}) async-start(), calls=%async_computation.3 | async-start | bytes 2097152 | tf_op jit(solution)/shard_map/psum | solution.py:117
  10.5 124.4 %copy-start.100 = (f32[256]{0:T(256)}, f32[256]{0:T(256)S(1)}, u32[]{:S(2)}) copy-start(f32[256]{0:T(256)S(1)} %subtract_convert_fusion) | copy-start | bytes 3076
  12.6 101.0 %copy-start.76 = (f32[256]{0:T(256)}, f32[256]{0:T(256)S(1)}, u32[]{:S(2)}) copy-start(f32[256]{0:T(256)S(1)} %get-tuple-element.461) | copy-start | bytes 3076
  12.7 111.6 %copy-start.61 = (f32[1280]{0:T(1024)}, f32[1280]{0:T(1024)S(1)}, u32[]{:S(2)}) copy-start(f32[1280]{0:T(1024)S(1)} %get-tuple-element.326) | copy-start | bytes 15364
  12.7 111.6 %copy-start.63 = (f32[1280]{0:T(1024)}, f32[1280]{0:T(1024)S(1)}, u32[]{:S(2)}) copy-start(f32[1280]{0:T(1024)S(1)} %get-tuple-element.327) | copy-start | bytes 15364
  12.7 111.6 %copy-start.65 = (f32[1280]{0:T(1024)}, f32[1280]{0:T(1024)S(1)}, u32[]{:S(2)}) copy-start(f32[1280]{0:T(1024)S(1)} %get-tuple-element.328) | copy-start | bytes 15364
  12.7 111.6 %copy-start.67 = (f32[1280]{0:T(1024)}, f32[1280]{0:T(1024)S(1)}, u32[]{:S(2)}) copy-start(f32[1280]{0:T(1024)S(1)} %get-tuple-element.329) | copy-start | bytes 15364
  12.7 100.8 %copy-start.2 = (bf16[256,2048]{1,0:T(8,128)(2,1)S(1)}, bf16[256,2048]{1,0:T(8,128)(2,1)}, u32[]{:S(2)}) copy-start(bf16[256,2048]{1,0:T(8,128)(2,1)} %param.21) | copy-start | bytes 3145732
  12.7 100.8 %copy-start.59 = (f32[2048]{0:T(1024)S(1)}, f32[2048]{0:T(1024)}, u32[]{:S(2)}) copy-start(f32[2048]{0:T(1024)} %param.34) | copy-start | bytes 24580
  119.3 5.0 copy-start.84
  119.3 5.1 copy-start.102
  119.3 5.0 collective-permute-start
  125.0 10.0 copy-start.6
  201.2 5.5 copy-start.50
  226.4 183.1 %copy-start.41 = (f32[127,1280]{1,0:T(8,128)S(1)}, f32[127,1280]{1,0:T(8,128)}, u32[]{:S(2)}) copy-start(f32[127,1280]{1,0:T(8,128)} %get-tuple-element.394) | copy-start | bytes 1950724
  226.4 183.1 %copy-start.94 = (f32[1,1280]{1,0:T(1,128)S(1)}, f32[1,1280]{1,0:T(1,128)}, u32[]{:S(2)}) copy-start(f32[1,1280]{1,0:T(1,128)} %slice.768) | copy-start | bytes 15364
  410.4 182.2 %copy-start.103 = (f32[1280]{0:T(1024)S(1)}, f32[1280]{0:T(1024)}, u32[]{:S(2)}) copy-start(f32[1280]{0:T(1024)} %param.36) | copy-start | bytes 15364
  597.3 5.3 copy-start.32
  602.5 157.2 %all-gather.13.cloned.1.call-start = ((), (), s32[]{:S(2)}) async-start(), calls=%async_computation.4 | async-start | bytes 25559040 | tf_op jit(solution)/shard_map/all_gather | solution.py:61
  604.3 249.0 %all-gather.15.cloned.1.call-start = ((), (), s32[]{:S(2)}) async-start(), calls=%async_computation.5 | async-start | bytes 12779520 | tf_op jit(solution)/shard_map/all_gather | solution.py:97
  604.9 318.4 %all-reduce.81.cloned.1.call-start = ((), (), s32[]{:S(2)}) async-start(), calls=%async_computation.6 | async-start | bytes 2097152 | tf_op jit(solution)/shard_map/psum | solution.py:121
  605.0 321.2 %copy-start.69 = (f32[256]{0:T(256)}, f32[256]{0:T(256)S(1)}, u32[]{:S(2)}) copy-start(f32[256]{0:T(256)S(1)} %convert_element_type.106) | copy-start | bytes 3076
  637.4 288.8 %copy-start.57 = (f32[256]{0:T(256)}, f32[256]{0:T(256)S(1)}, u32[]{:S(2)}) copy-start(f32[256]{0:T(256)S(1)} %get-tuple-element.459) | copy-start | bytes 3076
  637.4 155.1 %copy-start.5 = (bf16[256,2048]{1,0:T(8,128)(2,1)S(1)}, bf16[256,2048]{1,0:T(8,128)(2,1)}, u32[]{:S(2)}) copy-start(bf16[256,2048]{1,0:T(8,128)(2,1)} %all-reduce.79.cloned.1.call-done) | copy-start | bytes 3145732
  637.4 155.1 %copy-start.52 = (f32[2048]{0:T(1024)S(1)}, f32[2048]{0:T(1024)}, u32[]{:S(2)}) copy-start(f32[2048]{0:T(1024)} %param.35) | copy-start | bytes 24580
  898.4 847.0 %all-reduce.87.cloned.1.call-start = ((), (), s32[]{:S(2)}) async-start(), calls=%async_computation.10 | async-start | bytes 4194304 | tf_op jit(solution)/shard_map/psum | solution.py:117
  926.2 6.1 copy-start.97
  1023.9 6.6 copy-start.85
  1023.9 6.6 copy-start.86
  1023.9 6.7 copy-start.71
  1024.6 6.0 copy-start.72
  1045.0 8.9 copy-start.89
  1045.0 10.3 copy-start.88
  1059.8 7.6 copy-start.93
  1063.8 6.9 copy-start.91
  1506.3 65.5 %copy-start.78 = (f32[1,1280]{1,0:T(1,128)S(1)}, f32[1,1280]{1,0:T(1,128)}, u32[]{:S(2)}) copy-start(f32[1,1280]{1,0:T(1,128)} %broadcast_in_dim.4) | copy-start | bytes 15364
  1567.8 4.0 copy-start.4
  1567.8 4.0 copy-start.7
  1567.8 4.0 copy-start.14
  1593.5 5.4 copy-start.62
  1593.5 5.4 copy-start.64
  1593.5 5.4 copy-start.66
  1593.5 5.4 copy-start.68
  1593.6 12.4 slice-start
  1598.9 7.1 slice-start.1
  1599.3 6.7 slice-start.2
  1599.9 5.9 collective-permute-start.1
  1601.9 4.1 copy-start.33
  1610.0 167.1 %all-reduce.83.cloned.1.call-start = ((), (), s32[]{:S(2)}) async-start(), calls=%async_computation.8 | async-start | bytes 5242880 | tf_op jit(solution)/shard_map/psum | solution.py:296
  1610.7 22.9 copy-start.9
  1610.7 22.9 copy-start.70
  1633.6 11.7 copy-start.17
  1633.6 11.7 copy-start.37
  1633.6 11.7 copy-start.38
  1647.4 550.0 %reduce-scatter.2.cloned.1.call-start = ((), (), s32[]{:S(2)}) async-start(), calls=%async_computation.7 | async-start | bytes 108625920 | tf_op jit(solution)/shard_map/reduce_scatter | solution.py:287
  1648.0 8.0 copy-start.34
  1648.0 8.0 copy-start.40
  1740.4 589.4 %all-reduce.85.cloned.1.call-start = ((), (), s32[]{:S(2)}) async-start(), calls=%async_computation.9 | async-start | bytes 184320 | tf_op jit(solution)/shard_map/psum | solution.py:296
  2200.9 139.3 %copy-start.1 = (bf16[2,5,256,256]{3,2,1,0:T(8,128)(2,1)S(1)}, bf16[2,5,256,256]{3,2,1,0:T(8,128)(2,1)}, u32[]{:S(2)}) copy-start(bf16[2,5,256,256]{3,2,1,0:T(8,128)(2,1)} %param.29) | copy-start | bytes 3932164
  (58 other events, 131.9 us)
Sparse Core Ops, SparseCore 0:
  11.5 87.6 all-gather.8
  102.0 70.0 all-gather.10
  602.7 20.4 all-reduce.78
  626.7 132.9 all-gather.12
  762.7 90.6 all-gather.14
  898.5 24.7 all-reduce.80
  1610.2 22.0 all-reduce.86
  1647.6 129.4 all-reduce.82
  1783.1 414.3 reduce-scatter.1
  2205.4 124.3 all-reduce.84
where the time goes:
time: 2370 us; the launch traced here: 2350 us
  waiting for transfers between devices  840 us (35%)
  blocking collectives  697 us (29%)
  local copies, waits for them, and re-layouts  442 us (19%)
  other arithmetic  201 us (8%)
  matrix products  141 us (6%)
    all_gather x4, blocking collectives, carried_in(): pieces = jax.tree.map(lambda part: lax.all_gather(part, axis), value)  697 us
    reduce_scatter x1, waiting for transfers between devices, body(): lax.psum_scatter(make_terms(rec_pairs + mlp_pairs), 'seq', scatter_dimens...  417 us
    all_gather x2, waiting for transfers between devices, fold_rows(): lax.all_gather(weight, 'seq', axis=0, tiled=True)  209 us
    slice x109, local copies, waits for them, and re-layouts, linear_recurrence_scan(): lax.associative_scan(merge_pairs, (decay_multipliers, scan_increments), a...  154 us
    psum x2, waiting for transfers between devices, body(): lax.psum((grad_gates, grad_bias, grad_lam, grad_conv_w, conv_bias_gradien...  150 us
    pad x56, local copies, waits for them, and re-layouts, linear_recurrence_scan(): lax.associative_scan(merge_pairs, (decay_multipliers, scan_increments), a...  88.5 us
    concatenate x1, other arithmetic, make_terms(): return jnp.concatenate(parts, axis=1)  70.3 us
    dynamic_slice x126, local copies, waits for them, and re-layouts, lap(): longer = join(running, jax.tree.map(lambda part: part[position], pieces))  55.4 us
  transfers between devices with their start and end apart: 12, of which 9 were waited for; matrix products, arithmetic and copies ran while one was open for 17% of the time, Pallas kernels for 0%

commit v1 on v0

v1 whole, which is shorter than its diff:
```python
import functools
import jax
import jax.numpy as jnp
from jax import lax
from jax.experimental import pallas as pl
from jax.experimental.pallas import tpu as pltpu
from jax.sharding import Mesh, PartitionSpec as P

CONV = 4
EDGE = CONV - 1
EPSILON = 1e-06
MESH = pl.DeviceIdType.MESH
ANY = pl.BlockSpec(memory_space=pl.ANY)
VM = pl.BlockSpec(memory_space=pltpu.VMEM)
MIB = 1024 * 1024
AXES = ("z", "y", "x")
SEQ = ("z", "y", "x")
ORDERS = (("x", "y", "z"), ("y", "z", "x"), ("z", "x", "y"))
F32, BF16 = jnp.float32, jnp.bfloat16
DMA = pltpu.SemaphoreType.DMA


def greet(peers):
    sem = pltpu.get_barrier_semaphore()
    for peer in peers:
        pl.semaphore_signal(sem, inc=1, device_id=peer, device_id_type=MESH)
    pl.semaphore_wait(sem, len(peers))


def push(src, dst, send, recv, peer):
    return pltpu.make_async_remote_copy(
        src_ref=src, dst_ref=dst, send_sem=send, recv_sem=recv, device_id=peer, device_id_type=MESH
    )


def ring(axis):
    me = lax.axis_index(axis)
    return me, lax.rem(me + 1, 4), lax.rem(me + 2, 4), lax.rem(me + 3, 4)


def all_neighbours():
    peers = []
    for axis in AXES:
        _, up, _, down = ring(axis)
        peers += [{axis: up}, {axis: down}]
    return peers


def params(cid, mib):
    return pltpu.CompilerParams(
        collective_id=cid, has_side_effects=True, vmem_limit_bytes=mib * MIB
    )


def part_of(done, axis, index, rows, cols):
    spot = []
    for name in AXES:
        if name in done:
            spot.append(pl.ds(0, 4))
        elif name == axis:
            spot.append(index)
        else:
            spot.append(lax.axis_index(name))
    return tuple(spot) + (rows, cols)


def torus_gather_kernel(count, chunks, *refs):
    ins, outs = refs[:count], refs[count : 2 * count]
    send_sem, recv_sem, own_sem = refs[2 * count :]
    rows = ins[0].shape[0]
    half = rows // 2
    every, top, low = pl.ds(0, rows), pl.ds(0, half), pl.ds(half, half)
    greet(all_neighbours())
    entries = []
    for chunk in range(chunks):
        for a in range(count):
            width = ins[a].shape[1] // chunks
            entries.append((a, pl.ds(chunk * width, width), ORDERS[a % 3]))
    mine = []
    for a in range(count):
        spot = part_of((), "x", lax.axis_index("x"), every, pl.ds(0, ins[a].shape[1]))
        copy = pltpu.make_async_copy(ins[a], outs[a].at[spot], own_sem.at[a])
        copy.start()
        mine.append(copy)
    ended = []
    for phase in range(3):
        first = []
        for e, (a, cols, order) in enumerate(entries):
            axis, done = order[phase], order[:phase]
            me, up, _, down = ring(axis)
            spot = outs[a].at[part_of(done, axis, me, every, cols)]
            source = ins[a].at[every, cols] if phase == 0 else spot
            if phase > 0:
                for copy in ended[e]:
                    copy.wait()
            pair = []
            for way, peer in enumerate((up, down)):
                copy = push(
                    source,
                    spot,
                    send_sem.at[e, phase, 0, way],
                    recv_sem.at[e, phase, 0, way],
                    {axis: peer},
                )
                copy.start()
                pair.append(copy)
            first.append(pair)
        second = []
        for e, (a, cols, order) in enumerate(entries):
            axis, done = order[phase], order[:phase]
            me, up, _, down = ring(axis)
            pair = []
            for way, (peer, origin, piece) in enumerate(((up, down, top), (down, up, low))):
                first[e][way].wait_recv()
                spot = outs[a].at[part_of(done, axis, origin, piece, cols)]
                copy = push(
                    spot,
                    spot,
                    send_sem.at[e, phase, 1, way],
                    recv_sem.at[e, phase, 1, way],
                    {axis: peer},
                )
                copy.start()
                pair.append(copy)
            second.append(pair)
        for e in range(len(entries)):
            for way in range(2):
                first[e][way].wait_send()
        ended = second
        if phase == 0:
            for copy in mine:
                copy.wait()
    for pair in ended:
        for copy in pair:
            copy.wait()


def torus_gather(parts, cid, chunks=1):
    count = len(parts)
    outs = pl.pallas_call(
        functools.partial(torus_gather_kernel, count, chunks),
        out_shape=[jax.ShapeDtypeStruct((4, 4, 4) + p.shape, p.dtype) for p in parts],
        in_specs=[ANY] * count,
        out_specs=[ANY] * count,
        scratch_shapes=[
            DMA((count * chunks, 3, 2, 2)),
            DMA((count * chunks, 3, 2, 2)),
            DMA((count,)),
        ],
        compiler_params=params(cid, 16),
    )(*parts)
    return [o.reshape(64 * o.shape[3], o.shape[4]) for o in outs]


def pick(names, axis, index, others):
    spot, rest = [], iter(others)
    for name in names:
        spot.append(index if name == axis else next(rest))
    return tuple(spot)


def torus_scatter_kernel(count, *refs):
    ins, outs = refs[:count], refs[count : 2 * count]
    bufs = refs[2 * count : 2 * count + 8 * count]
    send_sem, recv_sem = refs[10 * count :]
    greet(all_neighbours())
    rows = ins[0].shape[3]
    half = rows // 2
    top, low = pl.ds(0, half), pl.ds(half, half)
    halves = (top, low)
    left = [AXES] * count
    source = list(ins)
    sent = []
    for phase in range(3):
        full = (pl.ds(0, 4),) * (2 - phase)
        tiles = 4 ** (2 - phase)
        ones = [bufs[8 * a + 3 * phase] for a in range(count)]
        twos = [bufs[8 * a + 3 * phase + 1] for a in range(count)]
        accs = [bufs[8 * a + 3 * phase + 2] if phase < 2 else outs[a] for a in range(count)]

        def spread(i):
            return (i // 4, lax.rem(i, 4)) if phase == 0 else ((i,) if phase == 1 else ())

        first, second, axes = [], [], []
        for a in range(count):
            axis = ORDERS[a % 3][phase]
            axes.append(axis)
            me, up, far, down = ring(axis)
            pair, direct = [], []
            for way, peer in enumerate((up, down)):
                mine, theirs = halves[way], halves[1 - way]
                k = (a, phase, way)
                copy = push(
                    source[a].at[pick(left[a], axis, far, full) + (mine,)],
                    ones[a].at[way],
                    send_sem.at[k + (0,)],
                    recv_sem.at[k + (0,)],
                    {axis: peer},
                )
                copy.start()
                pair.append(copy)
                copy = push(
                    source[a].at[pick(left[a], axis, peer, full) + (theirs,)],
                    twos[a].at[(way,) + full + (theirs,)],
                    send_sem.at[k + (1,)],
                    recv_sem.at[k + (1,)],
                    {axis: peer},
                )
                copy.start()
                direct.append(copy)
            first.append(pair)
            second.append(direct)
        for a in range(count):
            axis = axes[a]
            me, up, far, down = ring(axis)
            for way, peer in enumerate((up, down)):
                first[a][way].wait_recv()

                def add(i, carry, a=a, way=way, peer=peer, axis=axis):
                    there = (way,) + spread(i)
                    own = source[a][pick(left[a], axis, peer, spread(i)) + (halves[way],)]
                    total = ones[a][there].astype(F32) + own.astype(F32)
                    ones[a][there] = total.astype(BF16)
                    return carry

                lax.fori_loop(0, tiles, add, 0)
                k = (a, phase, way)
                copy = push(
                    ones[a].at[way],
                    twos[a].at[(way,) + full + (halves[way],)],
                    send_sem.at[k + (2,)],
                    recv_sem.at[k + (2,)],
                    {axis: peer},
                )
                copy.start()
                second[a].append(copy)
        for a in range(count):
            axis = axes[a]
            me, up, far, down = ring(axis)
            for copy in second[a]:
                copy.wait_recv()

            def total(i, carry, a=a, me=me, axis=axis):
                own = source[a][pick(left[a], axis, me, spread(i))].astype(F32)
                whole = own + twos[a][(0,) + spread(i)].astype(F32)
                whole = whole + twos[a][(1,) + spread(i)].astype(F32)
                accs[a][spread(i) + (slice(None), slice(None))] = whole.astype(accs[a].dtype)
                return carry

            lax.fori_loop(0, tiles, total, 0)
            sent += first[a] + second[a]
        source = accs
        left = [tuple(n for n in left[a] if n != axes[a]) for a in range(count)]
    for copy in sent:
        copy.wait_send()


def torus_scatter(parts, cid):
    count = len(parts)
    rows = parts[0].shape[0] // 64
    scratch = []
    for part in parts:
        width = part.shape[1]
        for phase in range(3):
            cube = (4,) * (2 - phase)
            scratch.append(pltpu.VMEM((2,) + cube + (rows // 2, width), BF16))
            scratch.append(pltpu.VMEM((2,) + cube + (rows, width), BF16))
            if phase < 2:
                scratch.append(pltpu.VMEM(cube + (rows, width), BF16))
    return pl.pallas_call(
        functools.partial(torus_scatter_kernel, count),
        out_shape=[jax.ShapeDtypeStruct((rows, p.shape[1]), F32) for p in parts],
        in_specs=[VM] * count,
        out_specs=[VM] * count,
        scratch_shapes=scratch + [DMA((count, 3, 2, 3)), DMA((count, 3, 2, 3))],
        compiler_params=params(cid, 56),
    )(*[p.reshape(4, 4, 4, rows, p.shape[1]) for p in parts])


def group_gather_kernel(in_ref, out_ref, send_sem, recv_sem, sib_send, sib_recv, own_sem):
    half = in_ref.shape[0] // 2
    me, up, far, down = ring("x")
    core = lax.axis_index("mp")
    other = {"mp": 1 - core}
    greet([{"x": up}, {"x": down}, other])
    top, low = pl.ds(0, half), pl.ds(half, half)
    spot = out_ref.at[me, core]
    mine = pltpu.make_async_copy(in_ref, spot, own_sem)
    mine.start()
    first = []
    for way, peer in enumerate((up, down)):
        copy = push(in_ref, spot, send_sem.at[0, way], recv_sem.at[0, way], {"x": peer})
        copy.start()
        first.append(copy)
    across = [push(in_ref, spot, sib_send.at[0], sib_recv.at[0], other)]
    across[0].start()
    second = []
    for way, (peer, origin, piece) in enumerate(((up, down, top), (down, up, low))):
        first[way].wait_recv()
        spot = out_ref.at[origin, core, piece]
        copy = push(spot, spot, send_sem.at[1, way], recv_sem.at[1, way], {"x": peer})
        copy.start()
        second.append(copy)
        whole = out_ref.at[origin, core]
        copy = push(whole, whole, sib_send.at[1 + way], sib_recv.at[1 + way], other)
        copy.start()
        across.append(copy)
    for way, piece in enumerate((top, low)):
        second[way].wait_recv()
        spot = out_ref.at[far, core, piece]
        copy = push(spot, spot, sib_send.at[3 + way], sib_recv.at[3 + way], other)
        copy.start()
        across.append(copy)
    for copy in first + second:
        copy.wait_send()
    for copy in across:
        copy.wait()
    mine.wait()


def group_gather(block, cid):
    rows, width = block.shape
    return pl.pallas_call(
        group_gather_kernel,
        out_shape=jax.ShapeDtypeStruct((4, 2, rows, width), block.dtype),
        in_specs=[VM],
        out_specs=VM,
        scratch_shapes=[DMA((2, 2)), DMA((2, 2)), DMA((5,)), DMA((5,)), DMA],
        compiler_params=params(cid, 32),
    )(block).reshape(8 * rows, width)


def group_scatter_kernel(in_ref, out_ref, got, one, two, send_sem, recv_sem, sib_send, sib_recv):
    rows = in_ref.shape[2]
    half = rows // 2
    me, up, far, down = ring("x")
    core = lax.axis_index("mp")
    other = {"mp": 1 - core}
    greet([{"x": up}, {"x": down}, other])
    across = []
    for k, chip in enumerate((far, up, down, me)):
        copy = push(in_ref.at[chip, 1 - core], got.at[chip], sib_send.at[k], sib_recv.at[k], other)
        copy.start()
        across.append(copy)

    def add(dst, src):
        dst[...] = (dst[...].astype(F32) + src[...].astype(F32)).astype(dst.dtype)

    across[0].wait_recv()
    add(got.at[far], in_ref.at[far, core])
    first = []
    for way, peer in enumerate((up, down)):
        copy = push(
            got.at[far, pl.ds(way * half, half)],
            one.at[way],
            send_sem.at[0, way],
            recv_sem.at[0, way],
            {"x": peer},
        )
        copy.start()
        first.append(copy)
    second = []
    for way, peer in enumerate((up, down)):
        across[1 + way].wait_recv()
        add(got.at[peer], in_ref.at[peer, core])
        first[way].wait_recv()
        add(got.at[peer, pl.ds(way * half, half)], one.at[way])
        copy = push(got.at[peer], two.at[way], send_sem.at[1, way], recv_sem.at[1, way], {"x": peer})
        copy.start()
        second.append(copy)
    across[3].wait_recv()
    out_ref[...] = got[me].astype(F32) + in_ref[me, core].astype(F32)
    for way in range(2):
        second[way].wait_recv()
        out_ref[...] += two[way].astype(F32)
    for copy in across + first + second:
        copy.wait_send()


def group_scatter(partial, cid):
    total, width = partial.shape
    rows = total // 8
    return pl.pallas_call(
        group_scatter_kernel,
        out_shape=jax.ShapeDtypeStruct((rows, width), F32),
        in_specs=[VM],
        out_specs=VM,
        scratch_shapes=[
            pltpu.VMEM((4, rows, width), partial.dtype),
            pltpu.VMEM((2, rows // 2, width), partial.dtype),
            pltpu.VMEM((2, rows, width), partial.dtype),
            DMA((2, 2)),
            DMA((2, 2)),
            DMA((4,)),
            DMA((4,)),
        ],
        compiler_params=params(cid, 40),
    )(partial.reshape(4, 2, rows, width))


def swap_kernel(count, *refs):
    ins, outs = refs[:count], refs[count : 2 * count]
    send_sem, recv_sem = refs[2 * count :]
    other = {"mp": 1 - lax.axis_index("mp")}
    greet([other])
    copies = [push(ins[k], outs[k], send_sem.at[k], recv_sem.at[k], other) for k in range(count)]
    for copy in copies:
        copy.start()
    for copy in copies:
        copy.wait()


def swap(blocks, cid):
    count = len(blocks)
    return pl.pallas_call(
        functools.partial(swap_kernel, count),
        out_shape=[jax.ShapeDtypeStruct(b.shape, b.dtype) for b in blocks],
        in_specs=[VM] * count,
        out_specs=[VM] * count,
        scratch_shapes=[DMA((count,)), DMA((count,))],
        compiler_params=params(cid, 32),
    )(*blocks)


def exchange_kernel(in_ref, out_ref, send_sem, recv_sem, own_sem):
    me = lax.axis_index("x")
    peers = ring("x")[1:]
    greet([{"x": peer} for peer in peers])
    mine = pltpu.make_async_copy(in_ref.at[me], out_ref.at[me], own_sem)
    mine.start()
    copies = []
    for k, peer in enumerate(peers):
        copy = push(in_ref.at[peer], out_ref.at[me], send_sem.at[k], recv_sem.at[k], {"x": peer})
        copy.start()
        copies.append(copy)
    for copy in copies:
        copy.wait()
    mine.wait()


def exchange(block, cid):
    return pl.pallas_call(
        exchange_kernel,
        out_shape=jax.ShapeDtypeStruct(block.shape, block.dtype),
        in_specs=[VM],
        out_specs=VM,
        scratch_shapes=[DMA((3,)), DMA((3,)), DMA],
        compiler_params=params(cid, 16),
    )(block)


def prefix_kernel(backward, in_ref, out_ref, slots, send_sem, recv_sem):
    axes = ("x", "y", "z")
    greet([{axis: ring(axis)[step]} for axis in axes for step in (1, 2, 3)])
    cur = (in_ref[0:1], in_ref[1:2])
    head = None
    for k, axis in enumerate(axes):
        me = lax.axis_index(axis)
        slots[k, me, 0:1] = cur[0]
        slots[k, me, 1:2] = cur[1]
        copies = []
        for step in (1, 2, 3):
            spot = slots.at[k, me]
            copy = push(
                spot,
                spot,
                send_sem.at[k, step - 1],
                recv_sem.at[k, step - 1],
                {axis: ring(axis)[step]},
            )
            copy.start()
            copies.append(copy)
        for copy in copies:
            copy.wait()
        run = (jnp.ones_like(cur[0]), jnp.zeros_like(cur[1]))
        mine = run
        for j in (3, 2, 1, 0) if backward else (0, 1, 2, 3):
            take = me == j
            mine = (jnp.where(take, run[0], mine[0]), jnp.where(take, run[1], mine[1]))
            fac, val = slots[k, j, 0:1], slots[k, j, 1:2]
            run = (run[0] * fac, val + fac * run[1])
        cur = run
        head = mine if head is None else (mine[0] * head[0], head[1] + head[0] * mine[1])
    out_ref[0:1] = head[0]
    out_ref[1:2] = head[1]


def prefix(pair, cid, backward):
    return pl.pallas_call(
        functools.partial(prefix_kernel, backward),
        out_shape=jax.ShapeDtypeStruct(pair.shape, pair.dtype),
        in_specs=[VM],
        out_specs=VM,
        scratch_shapes=[pltpu.VMEM((3, 4) + pair.shape, pair.dtype), DMA((3, 3)), DMA((3, 3))],
        compiler_params=params(cid, 16),
    )(pair)


def small_sum_kernel(in_ref, out_ref, slots, send_sem, recv_sem):
    axes = ("x", "y", "z")
    greet([{axis: ring(axis)[step]} for axis in axes for step in (1, 2, 3)])
    cur = in_ref[...]
    for k, axis in enumerate(axes):
        me = lax.axis_index(axis)
        slots[k, me] = cur
        copies = []
        for step in (1, 2, 3):
            spot = slots.at[k, me]
            copy = push(
                spot,
                spot,
                send_sem.at[k, step - 1],
                recv_sem.at[k, step - 1],
                {axis: ring(axis)[step]},
            )
            copy.start()
            copies.append(copy)
        for copy in copies:
            copy.wait()
        cur = (slots[k, 0] + slots[k, 1]) + (slots[k, 2] + slots[k, 3])
    out_ref[...] = cur


def small_sum(values, cid):
    return pl.pallas_call(
        small_sum_kernel,
        out_shape=jax.ShapeDtypeStruct(values.shape, values.dtype),
        in_specs=[VM],
        out_specs=VM,
        scratch_shapes=[pltpu.VMEM((3, 4) + values.shape, values.dtype), DMA((3, 3)), DMA((3, 3))],
        compiler_params=params(cid, 16),
    )(values)


def scan_kernel(f_ref, d_ref, cf_ref, cd_ref):
    rows, width = f_ref.shape

    def group(i, carry):
        base = pl.multiple_of(i * 8, 8)
        f, d = f_ref[pl.ds(base, 8)], d_ref[pl.ds(base, 8)]
        cf, cd = carry
        cfs, cds = [], []
        for r in range(8):
            cf = cf * f[r : r + 1]
            cd = cd * f[r : r + 1] + d[r : r + 1]
            cfs.append(cf)
            cds.append(cd)
        cf_ref[pl.ds(base, 8)] = jnp.concatenate(cfs, axis=0)
        cd_ref[pl.ds(base, 8)] = jnp.concatenate(cds, axis=0)
        return cf, cd

    zero = jnp.zeros((1, width), F32)
    lax.fori_loop(0, rows // 8, group, (zero + 1.0, zero))


def scan_back_kernel(f_ref, d_ref, cf_ref, cd_ref):
    rows, width = f_ref.shape

    def group(i, carry):
        base = pl.multiple_of(rows - 8 - i * 8, 8)
        f, d = f_ref[pl.ds(base, 8)], d_ref[pl.ds(base, 8)]
        follow, cf, cd = carry
        cfs, cds = [None] * 8, [None] * 8
        for r in (7, 6, 5, 4, 3, 2, 1, 0):
            cf = cf * follow
            cd = cd * follow + d[r : r + 1]
            cfs[r], cds[r] = cf, cd
            follow = f[r : r + 1]
        cf_ref[pl.ds(base, 8)] = jnp.concatenate(cfs, axis=0)
        cd_ref[pl.ds(base, 8)] = jnp.concatenate(cds, axis=0)
        return follow, cf, cd

    zero = jnp.zeros((1, width), F32)
    lax.fori_loop(0, rows // 8, group, (zero + 1.0, zero + 1.0, zero))


def local_scan(factors, values, backward):
    rows, width = factors.shape
    block = 256
    spec = pl.BlockSpec((rows, block), lambda i: (0, i))
    return pl.pallas_call(
        scan_back_kernel if backward else scan_kernel,
        out_shape=[jax.ShapeDtypeStruct((rows, width), F32)] * 2,
        grid=(width // block,),
        in_specs=[spec, spec],
        out_specs=[spec, spec],
    )(factors, values)


def rms_norm(values):
    mean_sq = jnp.mean(values * values, axis=-1, keepdims=True)
    inverse = lax.rsqrt(mean_sq + EPSILON)
    return values * inverse, inverse, jnp.sqrt(mean_sq[:, 0] + EPSILON)


def rms_back(grad_normed, normed, inverse, scales):
    grad_hat = grad_normed * scales
    inner_mean = jnp.mean(grad_hat * normed, axis=-1, keepdims=True)
    return inverse * (grad_hat - normed * inner_mean), jnp.sum(grad_normed * normed, axis=0)


def dot(left, right):
    return jnp.dot(left, right, preferred_element_type=F32)


def dot_t(left, right):
    return lax.dot_general(left, right, (((1,), (1,)), ((), ())), preferred_element_type=F32)


def outer(left, right):
    return lax.dot_general(left, right, (((0,), (0,)), ((), ())), preferred_element_type=F32)


def whole(half, theirs, core):
    first = jnp.where(core == 0, half, theirs)
    second = jnp.where(core == 0, theirs, half)
    return jnp.concatenate([first, second], axis=0)


def body(
    tokens,
    cotangent,
    starts,
    valid,
    w_rec,
    w_out,
    w_mlp,
    w_down,
    lru_gates,
    lru_bias,
    lam,
    conv_w,
    conv_b,
    gain_rec,
    gain_mlp,
    h_init,
    conv_state,
):
    count, width = tokens.shape
    shard, _, rec = w_rec.shape
    hidden_units = w_mlp.shape[2] // 4
    blocks, size = lru_gates.shape[1], lru_gates.shape[3]
    half = count // 2
    core = lax.axis_index("mp")
    here = lax.axis_index(SEQ)
    is_first = here == 0

    def my_half(array):
        return lax.dynamic_slice_in_dim(array, core * half, half, axis=0)

    def their_half(array):
        return lax.dynamic_slice_in_dim(array, (1 - core) * half, half, axis=0)

    down_t = w_down.T
    quarters = jnp.stack([w_mlp[:, 0], w_mlp[:, 1], down_t], axis=1)
    quarters = quarters.reshape(shard, 3, 4, hidden_units).transpose(2, 0, 1, 3)
    quarters = exchange(quarters.reshape(4, shard, 3 * hidden_units), 0)
    mlp_weights = lax.all_gather(
        quarters.reshape(4 * shard, 3 * hidden_units), ("z", "y"), axis=0, tiled=True
    )
    grad_out = my_half(cotangent).astype(F32) * my_half(valid).astype(F32)[:, None]
    grad_out_all = lax.all_gather(grad_out.astype(BF16), ("x", "mp"), axis=0, tiled=True)
    tail = lax.ppermute(tokens[count - 16 :], SEQ, [(i, (i + 1) % 64) for i in range(64)])

    w_gate, w_lin, w_back = torus_gather([w_rec[:, 0], w_rec[:, 1], w_out.T], 1, 2)

    tokens_wide = tokens.astype(F32)
    hat_rec, inverse_rec, rms_rec = rms_norm(tokens_wide)
    normed_rec = (hat_rec * gain_rec).astype(BF16)
    tail_normed = (rms_norm(tail.astype(F32))[0] * gain_rec).astype(BF16)
    gate_lin = dot(normed_rec, w_gate)
    rec_ext = dot(jnp.concatenate([tail_normed, normed_rec], axis=0), w_lin)
    rec_lin = rec_ext[16:]
    before = jnp.where(is_first, conv_state, rec_ext[16 - EDGE : 16])
    conv_in = jnp.concatenate([before, rec_lin], axis=0)
    conv_out = conv_b + sum(
        (conv_w[offset] * conv_in[offset : offset + count] for offset in range(CONV))
    )
    mixed_in = conv_out.astype(BF16)
    mixed_blocks = mixed_in.reshape(count, blocks, size)
    gate_logits = jnp.einsum("tnk,gnkj->gtnj", mixed_blocks, lru_gates, preferred_element_type=F32)
    gate_logits = gate_logits.reshape(2, count, rec) + lru_bias[:, None, :]
    reset_gate = jax.nn.sigmoid(gate_logits[0])
    input_gate = jax.nn.sigmoid(gate_logits[1])
    rates = jax.nn.softplus(-lam)
    log_decay = -8.0 * rates * reset_gate
    decays = jnp.exp(log_decay)
    scale_in = jnp.sqrt(-jnp.expm1(2.0 * log_decay))
    mixed_wide = mixed_in.astype(F32)
    driven = scale_in * input_gate * mixed_wide
    keep_mask = (1 - starts).astype(F32)[:, None]
    factors = decays * keep_mask
    cum_factor, cum_state = local_scan(factors, driven, False)
    pair = prefix(jnp.concatenate([cum_factor[-1:], cum_state[-1:]], axis=0), 2, False)
    carry_in = pair[1] + pair[0] * h_init
    states = cum_state + cum_factor * carry_in[None, :]
    gate_act, gate_pull = jax.vjp(jax.nn.gelu, gate_lin)
    branch_in = (gate_act * states).astype(BF16)

    out_part = dot_t(branch_in, w_back)
    (out_theirs,) = swap([their_half(out_part).astype(BF16)], 3)
    hidden = my_half(tokens_wide) + (my_half(out_part) + out_theirs.astype(F32))
    hat_mlp, inverse_mlp, rms_half = rms_norm(hidden)
    normed_mlp = (hat_mlp * gain_mlp).astype(BF16)
    normed_all = group_gather(normed_mlp, 4)
    gate_up = dot(normed_all, mlp_weights[:, : 2 * hidden_units])
    up_lin = gate_up[:, hidden_units:]
    mlp_act, mlp_pull = jax.vjp(jax.nn.gelu, gate_up[:, :hidden_units])
    mlp_in = (mlp_act * up_lin).astype(BF16)
    w_down_t = mlp_weights[:, 2 * hidden_units :]
    mlp_out = group_scatter(dot_t(mlp_in, w_down_t).astype(BF16), 5)
    result_half = (hidden + mlp_out).astype(BF16)

    grad_mlp_in = dot(grad_out_all, w_down_t)
    grad_gate = mlp_pull(grad_mlp_in * up_lin)[0]
    grad_up = grad_mlp_in * mlp_act
    grad_gate_up = jnp.concatenate([grad_gate, grad_up], axis=1).astype(BF16)
    normed_part = dot_t(grad_gate_up, mlp_weights[:, : 2 * hidden_units])
    grad_normed_mlp = group_scatter(normed_part.astype(BF16), 6)
    mlp_terms = jnp.concatenate(
        [outer(normed_all, grad_gate_up), outer(grad_out_all, mlp_in)], axis=1
    ).astype(BF16)
    mlp_sums = lax.psum_scatter(mlp_terms, ("z", "y"), scatter_dimension=0, tiled=True)
    grad_hidden_norm, gain_mlp_term = rms_back(grad_normed_mlp, hat_mlp, inverse_mlp, gain_mlp)
    grad_hidden = grad_out + grad_hidden_norm
    result_theirs, rms_theirs, low_theirs = swap(
        [
            result_half,
            jnp.broadcast_to(rms_half[None, :], (8, half)),
            grad_hidden.astype(BF16),
        ],
        7,
    )
    result = whole(result_half, result_theirs, core)
    rms_mlp = whole(rms_half, rms_theirs[0], core)
    grad_hidden_low = whole(grad_hidden.astype(BF16), low_theirs, core)

    grad_branch = dot(grad_hidden_low, w_back)
    grad_gate_lin = gate_pull(grad_branch * states)[0]
    grad_states = grad_branch * gate_act
    cum_back, adjoint_local = local_scan(factors, grad_states, True)
    pair = jnp.stack([factors[0] * cum_back[0], factors[0] * adjoint_local[0]])
    later = prefix(pair, 8, True)[1]
    adjoint = adjoint_local + cum_back * later[None, :]
    grad_h_term = jnp.where(is_first, factors[0] * adjoint[0], 0.0)
    prev_states = jnp.concatenate([carry_in[None, :], states[:-1]], axis=0)
    grad_scale = adjoint * input_gate * mixed_wide
    grad_input_gate = adjoint * scale_in * mixed_wide
    grad_log = adjoint * prev_states * keep_mask * decays - grad_scale * decays * decays / scale_in
    grad_lam = jnp.sum(grad_log * 8.0 * reset_gate, axis=0) * jax.nn.sigmoid(-lam)
    grad_logits = jnp.stack(
        [
            grad_log * (-8.0 * rates) * reset_gate * (1.0 - reset_gate),
            grad_input_gate * input_gate * (1.0 - input_gate),
        ],
        axis=0,
    ).astype(BF16)
    grad_bias = jnp.sum(grad_logits.astype(F32), axis=1)
    grad_blocks = grad_logits.reshape(2, count, blocks, size)
    grad_gates = jnp.einsum("tnk,gtnj->gnkj", mixed_blocks, grad_blocks, preferred_element_type=F32)
    grad_mixed = adjoint * scale_in * input_gate
    grad_mixed = grad_mixed + jnp.einsum(
        "gtnj,gnkj->tnk", grad_blocks, lru_gates, preferred_element_type=F32
    ).reshape(count, rec)
    conv_bias_gradient = jnp.sum(grad_mixed, axis=0)
    grad_conv_w = jnp.stack(
        [jnp.sum(grad_mixed * conv_in[k : k + count], axis=0) for k in range(CONV)], axis=0
    )
    grad_conv_in = jnp.zeros((count + EDGE, rec), F32)
    for offset in range(CONV):
        grad_conv_in = grad_conv_in + jnp.pad(
            conv_w[offset] * grad_mixed, ((offset, EDGE - offset), (0, 0))
        )
    edge_back = lax.ppermute(grad_conv_in[:EDGE], SEQ, [(i + 1, i) for i in range(63)])
    grad_rec_lin = grad_conv_in[EDGE:] + jnp.pad(edge_back, ((count - EDGE, 0), (0, 0)))
    conv_state_term = jnp.where(is_first, grad_conv_in[:EDGE], 0.0)
    grad_gate_low, grad_rec_low = grad_gate_lin.astype(BF16), grad_rec_lin.astype(BF16)
    normed_part = dot_t(grad_gate_low, w_gate) + dot_t(grad_rec_low, w_lin)
    (part_theirs,) = swap([their_half(normed_part).astype(BF16)], 9)
    grad_normed_rec = my_half(normed_part) + part_theirs.astype(F32)
    token_norm_gradient, gain_rec_term = rms_back(
        grad_normed_rec, my_half(hat_rec), my_half(inverse_rec), gain_rec
    )
    tokens_half = grad_hidden + token_norm_gradient
    (tokens_theirs,) = swap([tokens_half], 10)
    grad_tokens = whole(tokens_half, tokens_theirs, core)

    gate_terms = grad_gates.astype(BF16).reshape(64 * shard, -1)
    gate_terms = jnp.pad(gate_terms, ((0, 0), (0, 3 * 128 - gate_terms.shape[1])))
    sums = torus_scatter(
        [
            outer(normed_rec, grad_gate_low).astype(BF16),
            outer(normed_rec, grad_rec_low).astype(BF16),
            outer(grad_hidden_low, branch_in).astype(BF16),
            gate_terms[:, :128],
            gate_terms[:, 128:256],
            gate_terms[:, 256:],
        ],
        11,
    )
    grad_w_rec = jnp.stack([sums[0], sums[1]], axis=1)
    grad_w_out = sums[2].T
    gate_sums = jnp.concatenate(torus_gather(sums[3:], 12), axis=1)[:, : grad_gates.size // (64 * shard)]
    grad_gates = gate_sums.reshape(grad_gates.shape)

    mlp_sums = exchange(mlp_sums.astype(F32).reshape(4, shard, 3 * hidden_units), 13)
    mlp_sums = mlp_sums.reshape(4, shard, 3, hidden_units).transpose(1, 2, 0, 3)
    mlp_sums = mlp_sums.reshape(shard, 3, 4 * hidden_units)
    grad_w_mlp = mlp_sums[:, :2]
    grad_w_down = mlp_sums[:, 2].T

    pieces = (
        grad_bias,
        grad_lam,
        grad_conv_w,
        conv_bias_gradient,
        grad_h_term,
        conv_state_term,
        gain_rec_term,
        gain_mlp_term,
    )
    flat = jnp.concatenate([p.reshape(-1, 128) for p in pieces], axis=0)
    total = small_sum(flat, 14)
    summed, at = [], 0
    for piece in pieces:
        rows = piece.size // 128
        summed.append(total[at : at + rows].reshape(piece.shape))
        at += rows
    gains = total[at - 2 * width // 128 :]
    (gains_theirs,) = swap([gains], 15)
    gains = (gains + gains_theirs).reshape(2, width)
    return (
        result,
        rms_rec,
        rms_mlp,
        grad_tokens,
        grad_w_rec,
        grad_w_out,
        grad_w_mlp,
        grad_w_down,
        grad_gates,
        summed[0],
        summed[1],
        summed[2],
        summed[3],
        gains[0],
        gains[1],
        summed[4],
        summed[5],
    )


def solution(mesh):
    cube = Mesh(mesh.devices.reshape(4, 4, 4, 2), ("z", "y", "x", "mp"))
    placed = (
        P(SEQ, None),
        P(SEQ, None),
        P(SEQ),
        P(SEQ),
        P(SEQ, None, "mp"),
        P("mp", SEQ),
        P(SEQ, None, "mp"),
        P("mp", SEQ),
        P(None, "mp", None, None),
        P(None, "mp"),
        P("mp"),
        P(None, "mp"),
        P("mp"),
        P(),
        P(),
        P("mp"),
        P(None, "mp"),
    )
    return jax.shard_map(
        body,
        mesh=cube,
        in_specs=placed,
        out_specs=(
            P(SEQ, None),
            P(SEQ),
            P(SEQ),
            P(SEQ, None),
            P(SEQ, None, "mp"),
            P("mp", SEQ),
            P(SEQ, None, "mp"),
            P("mp", SEQ),
            P(None, "mp", None, None),
            P(None, "mp"),
            P("mp"),
            P(None, "mp"),
            P("mp"),
            P(),
            P(),
            P("mp"),
            P(None, "mp"),
        ),
        check_vma=False,
    )
```

time: 2370 us -> 652 us (0.28)
  waiting for transfers between devices: 840 us -> 0.06 us
  blocking collectives: 697 us -> 0 us
  Pallas kernels: 0 us -> 399 us
  local copies, waits for them, and re-layouts: 442 us -> 85.5 us
  other arithmetic: 201 us -> 56.5 us
  matrix products: 141 us -> 89.6 us
    all_gather x4 -> x0, blocking collectives: 697 us -> none  [carried_in(): pieces = jax.tree.map(lambda part: lax.all_gather(part, axis), value)]
    reduce_scatter x1 -> x0, waiting for transfers between devices: 417 us -> none  [body(): lax.psum_scatter(make_terms(rec_pairs + mlp_pairs), 'seq', scatter_dimens...]
    pallas_call x0 -> x18, Pallas kernels: none -> 399 us  [the longest x2 140 us: torus_gather(): pl.pallas_call(functools.partial(torus_gather_kernel, count, chunks), out...]
    all_gather x4 -> x2, waiting for transfers between devices: 251 us -> 0.01 us  [the longest x1 0.01 us: body(): lax.all_gather(quarters.reshape(4 * shard, 3 * hidden_units), ('z', 'y'),...]
    psum x5 -> x0, waiting for transfers between devices: 165 us -> none  [the longest x2 150 us: body(): lax.psum((grad_gates, grad_bias, grad_lam, grad_conv_w, conv_bias_gradien...]
    slice x115 -> x14, local copies, waits for them, and re-layouts: 156 us -> 3.3 us  [the longest x1 1.23 us: body(): gate_terms[:, 256:]]
    pad x56 -> x0, local copies, waits for them, and re-layouts: 88.5 us -> none  [linear_recurrence_scan(): lax.associative_scan(merge_pairs, (decay_multipliers, scan_increments), a...]
    concatenate x27 -> x6, other arithmetic: 85.2 us -> 16.6 us  [the longest x1 11.5 us: body(): jnp.concatenate([outer(normed_all, grad_gate_up), outer(grad_out_all, mlp...]
  transfers between devices with their start and end apart: 12 -> 5, of which waited for: 9 -> 0; matrix products, arithmetic and copies ran while one was open for 17% -> 23% of each run, Pallas kernels for 0% -> 57%
where the time goes in v1:
time: 652 us; the launch traced here: 647 us
  Pallas kernels  399 us (61%)
  matrix products  89.6 us (14%)
  local copies, waits for them, and re-layouts  85.5 us (13%)
  other arithmetic  56.5 us (9%)
  between operations  15.3 us (2%)
    pallas_call x2, Pallas kernels, torus_gather(): pl.pallas_call(functools.partial(torus_gather_kernel, count, chunks), out...  140 us
    pallas_call x1, Pallas kernels, torus_scatter(): pl.pallas_call(functools.partial(torus_scatter_kernel, count), out_shape=...  84.4 us
    pallas_call x2, Pallas kernels, group_scatter(): pl.pallas_call(group_scatter_kernel, out_shape=jax.ShapeDtypeStruct((rows...  50.7 us
    unnamed x167, local copies, waits for them, and re-layouts  37.4 us
    dot_general x5, matrix products, dot(): return jnp.dot(left, right, preferred_element_type=F32)  34.3 us
    pallas_call x2, Pallas kernels, exchange(): pl.pallas_call(exchange_kernel, out_shape=jax.ShapeDtypeStruct(block.shap...  29.2 us
    pallas_call x2, Pallas kernels, prefix(): pl.pallas_call(functools.partial(prefix_kernel, backward), out_shape=jax....  26.8 us
    dot_general x5, matrix products, outer(): lax.dot_general(left, right, (((0,), (0,)), ((), ())), preferred_element_...  24.7 us
  transfers between devices with their start and end apart: 5, of which 0 were waited for; matrix products, arithmetic and copies ran while one was open for 23% of the time, Pallas kernels for 57%

profile of v1, /device:TPU:0, one launch (start us, length us, event | category | flops | bytes accessed | tf_op | source)
XLA Modules:
  0.0 647.4 jit_solution(15622104686533879425)
XLA Ops:
  10.0 1.7 maximum_bitcast_fusion
  11.7 1.8 reshape.253.in_ref
  13.5 12.1 %shard_map.301 = bf16[4,32,2304]{2,1,0:T(8,128)(2,1)} custom-call(bf16[4,32,2304]{2,1,0:T(8,128)(2,1)S(1)} %reshape.253.in_ref), custom_call_target="tpu_custom_call" | custom-call | tf_op jit(solution)/shard_map/pallas_call | solution.py:442
  25.9 2.0 fusion.51
  31.1 2.9 broadcast_multiply_fusion
  33.9 113.0 %shard_map.296 = (bf16[4,4,4,32,1280]{4,3,2,1,0:T(8,128)(2,1)S(1)}, bf16[4,4,4,32,1280]{4,3,2,1,0:T(8,128)(2,1)S(1)}, bf16[4,4,4,32,1280]{4,3,2,1,0:T(8,128)(2,1)S(1)}) custom-call(bf16[32,1280]{1,0:T(8,128)(2,1)S(1)} %get-tuple-element.195.refs_0_, bf16[32,1280]{1,0:T(8,128)(2,1)S(1)} %get-tuple-element.194.refs_1_, bf16[32,1280]{1,0:T(8,128)(2,1)S(1)} %bitcast.148), custom_call_target="tpu_custom_call" | custom-call | tf_op jit(solution)/shard_map/pallas_call | solution.py:140
  147.0 2.3 copy-done.2
  149.2 2.3 copy-done.10
  157.7 1.7 convolution_bitcast_fusion
  159.4 1.8 copy.105
  161.2 3.4 copy.106
  164.6 1.9 broadcast_add_fusion
  166.5 2.9 convert_multiply_fusion.2
  169.5 6.9 %shard_map.297 = (f32[256,1280]{1,0:T(8,128)}, f32[256,1280]{1,0:T(8,128)}) custom-call(f32[256,1280]{1,0:T(8,128)} %get-tuple-element.159.f_ref, f32[256,1280]{1,0:T(8,128)} %get-tuple-element.158.d_ref), custom_call_target="tpu_custom_call" | custom-call | tf_op jit(solution)/shard_map/pallas_call | solution.py:581
  177.9 13.5 %shard_map.298 = f32[2,1280]{1,0:T(2,128)S(1)} custom-call(f32[2,1280]{1,0:T(2,128)S(1)} %pad_maximum_fusion.17.in_ref), custom_call_target="tpu_custom_call" | custom-call | tf_op jit(solution)/shard_map/pallas_call | solution.py:489
  191.5 6.5 %multiply_convert_fusion.4 = (bf16[256,1280]{1,0:T(8,128)(2,1)S(1)}, f32[256,1280]{1,0:T(8,128)}, f32[256,1280]{1,0:T(8,128)}) fusion(f32[256,1280]{1,0:T(8,128)} %get-tuple-element.38, f32[256,1280]{1,0:T(8,128)} %get-tuple-element.39, f32[1280]{0:T(1024)S(1)} %multiply_add_fusion.5, bf16[256,2048]{1,0:T(8,128)(2,1)S(1)} %get-tuple-element.174, ...), kind=kOutput, calls=%fused_computation.87 | convolution fusion | flops 1346109440 | bytes 12194816 | tf_op jit(solution)/shard_map/dot_general | solution.py:603
  199.7 1.9 shard_map.299
  202.5 22.9 %shard_map.300 = bf16[4,2,128,2048]{3,2,1,0:T(8,128)(2,1)S(1)} custom-call(bf16[128,2048]{1,0:T(8,128)(2,1)S(1)} %multiply_convert_fusion.5.in_ref), custom_call_target="tpu_custom_call" | custom-call | tf_op jit(solution)/shard_map/pallas_call | solution.py:323
  225.5 2.1 copy-done.4
  227.6 12.3 %fusion.2 = f32[1024,1536]{1,0:T(8,128)} fusion(bf16[1024,2048]{1,0:T(8,128)(2,1)} %bitcast.143, bf16[2048,2304]{1,0:T(8,128)(2,1)} %all-gather.3.cloned.1.call-done), kind=kOutput, calls=%fused_computation.7 | convolution fusion | flops 6442450944 | bytes 16777216 | tf_op jit(solution)/shard_map/dot_general | solution.py:603
  239.9 10.4 %fusion.13 = (bf16[1024,768]{1,0:T(8,128)(2,1)S(1)}, bf16[1024,768]{1,0:T(8,128)(2,1)S(1)}, bf16[1024,768]{1,0:T(8,128)(2,1)S(1)}) fusion(f32[1024,1536]{1,0:T(8,128)} %fusion.2, bf16[1024,2048]{1,0:T(8,128)(2,1)} %all-gather.5.cloned.1.call-done, bf16[2048,2304]{1,0:T(8,128)(2,1)} %all-gather.3.cloned.1.call-done), kind=kOutput, calls=%fused_computation.20 | convolution fusion | flops 3241672704 | bytes 18350080 | tf_op jit(solution)/shard_map/dot_general | solution.py:603
  250.4 7.8 %convolution_convert_fusion = bf16[2048,1536]{0,1:T(8,128)(2,1)S(1)} fusion(bf16[1024,2048]{1,0:T(8,128)(2,1)S(1)} %bitcast.144, bf16[1024,768]{1,0:T(8,128)(2,1)S(1)} %get-tuple-element.154, bf16[1024,768]{1,0:T(8,128)(2,1)S(1)} %get-tuple-element.153), kind=kOutput, calls=%fused_computation.1 | convolution fusion | flops 6451888128 | bytes 13631488 | tf_op jit(solution)/shard_map/dot_general | solution.py:611
  258.2 3.9 convolution_convert_fusion.5
  262.1 11.5 %pad_maximum_fusion = bf16[2048,2304]{0,1:T(8,128)(2,1)} fusion(bf16[2048,768]{0,1:T(8,128)(2,1)S(1)} %convolution_convert_fusion.5, bf16[2048,1536]{0,1:T(8,128)(2,1)S(1)} %convolution_convert_fusion), kind=kLoop, calls=%fused_computation | loop fusion | flops 18874368 | bytes 18874368 | tf_op jit(solution)/shard_map/concatenate | solution.py:720
  273.6 12.8 %copy.135 = bf16[2048,2304]{1,0:T(8,128)(2,1)} copy(bf16[2048,2304]{0,1:T(8,128)(2,1)} %pad_maximum_fusion) | data formatting | bytes 18874368
  287.6 5.8 convolution_convert_fusion.4
  293.5 25.8 %shard_map.302 = f32[128,2048]{1,0:T(8,128)S(1)} custom-call(bf16[4,2,128,2048]{3,2,1,0:T(8,128)(2,1)S(1)} %bitcast.142), custom_call_target="tpu_custom_call" | custom-call | tf_op jit(solution)/shard_map/pallas_call | solution.py:383
  319.3 8.8 %fusion.4 = bf16[1024,2048]{1,0:T(8,128)(2,1)S(1)} fusion(bf16[2048,2304]{1,0:T(8,128)(2,1)} %all-gather.3.cloned.1.call-done, bf16[1024,768]{1,0:T(8,128)(2,1)S(1)} %copy-done.74, bf16[1024,768]{1,0:T(8,128)(2,1)S(1)} %copy-done.72), kind=kOutput, calls=%fused_computation.11 | convolution fusion | flops 6450839552 | bytes 13631488 | tf_op jit(solution)/shard_map/dot_general | solution.py:607
  328.1 25.0 %shard_map.303 = f32[128,2048]{1,0:T(8,128)S(1)} custom-call(bf16[4,2,128,2048]{3,2,1,0:T(8,128)(2,1)S(1)} %bitcast.141), custom_call_target="tpu_custom_call" | custom-call | tf_op jit(solution)/shard_map/pallas_call | solution.py:383
  354.3 2.7 fusion.76
  357.0 2.7 shard_map.304
  361.5 3.4 fusion.53
  364.9 7.1 %shard_map.305 = (f32[256,1280]{1,0:T(8,128)}, f32[256,1280]{1,0:T(8,128)}) custom-call(f32[256,1280]{1,0:T(8,128)} %get-tuple-element.159.f_ref, f32[256,1280]{1,0:T(8,128)} %get-tuple-element.160.d_ref), custom_call_target="tpu_custom_call" | custom-call | tf_op jit(solution)/shard_map/pallas_call | solution.py:581
  372.8 13.3 %shard_map.306 = f32[2,1280]{1,0:T(2,128)S(1)} custom-call(f32[2,1280]{1,0:T(2,128)S(1)} %pad_maximum_fusion.18.in_ref), custom_call_target="tpu_custom_call" | custom-call | tf_op jit(solution)/shard_map/pallas_call | solution.py:489
  386.2 5.2 multiply_reduce_fusion.5
  391.5 2.7 multiply_convert_fusion.3
  394.2 2.2 copy.111
  396.4 2.2 copy.113
  398.5 2.2 copy.112
  400.7 2.2 copy.114
  402.9 3.0 fusion.43
  405.9 2.8 copy.116
  408.7 5.0 fusion.74
  417.9 1.7 fusion.17
  419.6 2.8 copy.119
  422.5 4.1 reshape.261
  430.6 2.9 pad_add_fusion
  433.6 4.0 convolution_convert_fusion.1
  437.5 3.8 convolution_convert_fusion.3
  441.4 2.9 fusion.79
  446.4 5.1 convolution_add_fusion
  451.6 1.9 shard_map.307
  454.7 20.1 %shard_map.312 = f32[152,128]{1,0:T(8,128)S(1)} custom-call(f32[152,128]{1,0:T(8,128)S(1)} %concatenate.52.in_ref), custom_call_target="tpu_custom_call" | custom-call | tf_op jit(solution)/shard_map/pallas_call | solution.py:525
  477.9 5.3 convolution_convert_fusion.2
  483.2 84.4 %shard_map.309 = (f32[32,1280]{1,0:T(8,128)}, f32[32,1280]{1,0:T(8,128)}, f32[32,1280]{1,0:T(8,128)}, f32[32,128]{1,0:T(8,128)}, f32[32,128]{1,0:T(8,128)}, /*index=5*/f32[32,128]{1,0:T(8,128)}) custom-call(bf16[4,4,4,32,1280]{4,3,2,1,0:T(8,128)(2,1)} %bitcast.156, bf16[4,4,4,32,1280]{4,3,2,1,0:T(8,128)(2,1)} %bitcast.157, ...), custom_call_target="tpu_custom_call" | custom-call | tf_op jit(solution)/shard_map/pallas_call | solution.py:270
  569.8 27.1 %shard_map.311 = (f32[4,4,4,32,128]{4,3,2,1,0:T(8,128)S(1)}, f32[4,4,4,32,128]{4,3,2,1,0:T(8,128)S(1)}, f32[4,4,4,32,128]{4,3,2,1,0:T(8,128)S(1)}) custom-call(f32[32,128]{1,0:T(8,128)S(1)} %copy-done.7, f32[32,128]{1,0:T(8,128)S(1)} %copy-done.8, f32[32,128]{1,0:T(8,128)S(1)} %copy-done.9), custom_call_target="tpu_custom_call" | custom-call | tf_op jit(solution)/shard_map/pallas_call | solution.py:140
  596.9 2.0 pad_maximum_fusion.1
  598.9 4.9 reshape.272
  605.0 1.9 multiply_add_fusion.3.refs_0_
  606.9 2.7 shard_map.308
  614.1 17.1 %shard_map.310 = f32[4,32,2304]{2,1,0:T(8,128)S(1)} custom-call(f32[4,32,2304]{2,1,0:T(8,128)S(1)} %bitcast.140), custom_call_target="tpu_custom_call" | custom-call | tf_op jit(solution)/shard_map/pallas_call | solution.py:442
  632.2 1.7 reshape.267
  634.0 1.8 copy.121
  635.8 1.9 reshape.268
  (258 shorter events, 47.7 us)
Async XLA Ops:
  7.2 150.5 %copy-start = (bf16[2,5,256,256]{3,2,1,0:T(8,128)(2,1)S(1)}, bf16[2,5,256,256]{3,2,1,0:T(8,128)(2,1)}, u32[]{:S(2)}) copy-start(bf16[2,5,256,256]{3,2,1,0:T(8,128)(2,1)} %param.25) | copy-start | bytes 3932164
  7.2 220.4 %all-gather.3.cloned.1.call-start = ((), (), s32[]{:S(2)}) async-start(), calls=%async_computation.1 | async-start | bytes 10027008 | tf_op jit(solution)/shard_map/all_gather | solution.py:658
  11.7 14.0 %copy-start.27 = (bf16[256,2048]{1,0:T(8,128)(2,1)S(1)}, bf16[256,2048]{1,0:T(8,128)(2,1)}, u32[]{:S(2)}) copy-start(bf16[256,2048]{1,0:T(8,128)(2,1)} %param.17) | copy-start | bytes 3145732
  11.7 14.1 %copy-start.69 = (s32[256]{0:T(256)S(1)}, s32[256]{0:T(256)}, u32[]{:S(2)}) copy-start(s32[256]{0:T(256)} %param.20) | copy-start | bytes 3076
  25.6 214.3 %all-gather.5.cloned.1.call-start = ((), (), s32[]{:S(2)}) async-start(), calls=%async_computation.2 | async-start | bytes 4718592 | tf_op jit(solution)/shard_map/all_gather | solution.py:662
  25.7 125.9 %collective-permute-start = (bf16[16,2048]{1,0:T(8,128)(2,1)S(1)}, bf16[16,2048]{1,0:T(8,128)(2,1)S(1)}, u32[]{:S(2)}, u32[]{:S(2)}) collective-permute-start(bf16[16,2048]{1,0:T(8,128)(2,1)S(1)} %slice.159), channel_id=1, source_target_pairs={{0,2},{2,4},{4,6},{6,8},{8,10},{10,12},{12,14},{14,16},{16,18},{18... | collective-permute-start | bytes 196616 | tf_op jit(solution)/shard_map/ppermute | solution.py:663
  25.9 2.7 copy-start.64
  27.9 584.6 %reduce-scatter.4.cloned.1.call-start = ((), (), s32[]{:S(2)}) async-start(), calls=%async_computation.3 | async-start | bytes 10027008
  28.5 2.4 copy-start.53
  28.5 2.4 copy-start.66
  28.6 2.5 copy-start.51
  30.9 3.0 copy-start.62
  31.0 135.5 %copy-start.58 = (f32[256]{0:T(256)}, f32[256]{0:T(256)S(1)}, u32[]{:S(2)}) copy-start(f32[256]{0:T(256)S(1)} %subtract_convert_fusion) | copy-start | bytes 3076
  31.0 2.9 copy-start.6
  31.0 120.5 %copy-start.55 = (f32[4,1280]{1,0:T(4,128)S(1)}, f32[4,1280]{1,0:T(4,128)}, u32[]{:S(2)}) copy-start(f32[4,1280]{1,0:T(4,128)} %param.28) | copy-start | bytes 61444
  147.0 2.3 copy-start.2
  149.2 2.3 copy-start.10
  151.5 2.3 copy-start.1
  153.8 2.1 copy-start.60
  156.6 9.9 %copy-start.14 = (bf16[256,1280]{1,0:T(8,128)(2,1)}, bf16[256,1280]{1,0:T(8,128)(2,1)S(1)}, u32[]{:S(2)}) copy-start(bf16[256,1280]{1,0:T(8,128)(2,1)S(1)} %add_convert_fusion) | copy-start | bytes 1966084
  161.2 3.4 copy-start.57
  166.5 3.0 copy-start.11
  169.5 22.0 %copy-start.61 = (f32[1280]{0:T(1024)S(1)}, f32[1280]{0:T(1024)}, u32[]{:S(2)}) copy-start(f32[1280]{0:T(1024)} %param.32) | copy-start | bytes 15364
  169.5 28.6 %slice-start.2 = ((s8[5242880]{0:T(1024)(128)(4,1)}), s8[1048576]{0:T(1024)(128)(4,1)S(1)}, s32[]{:S(2)}) async-start(s8[5242880]{0:T(1024)(128)(4,1)} %bitcast.149), calls=%async_computation.6 | async-start | bytes 2097152
  191.5 6.6 %slice-start.3 = ((s8[5242880]{0:T(1024)(128)(4,1)}), s8[4194304]{0:T(1024)(128)(4,1)S(1)}, s32[]{:S(2)}) async-start(s8[5242880]{0:T(1024)(128)(4,1)} %bitcast.149), calls=%async_computation.7 | async-start | bytes 8388608
  199.6 2.0 copy-start.33
  202.0 151.1 %copy-start.13 = (f32[128,2048]{1,0:T(8,128)}, f32[128,2048]{1,0:T(8,128)S(1)}, u32[]{:S(2)}) copy-start(f32[128,2048]{1,0:T(8,128)S(1)} %get-tuple-element.150) | copy-start | bytes 3145732
  225.5 2.1 copy-start.4
  239.9 10.5 %copy-start.5 = (bf16[4,2,128,2048]{3,2,1,0:T(8,128)(2,1)S(1)}, bf16[4,2,128,2048]{3,2,1,0:T(8,128)(2,1)}, u32[]{:S(2)}) copy-start(bf16[4,2,128,2048]{3,2,1,0:T(8,128)(2,1)} %copy-done.4) | copy-start | bytes 12582916
  250.3 7.9 %copy-start.71 = (bf16[1024,768]{1,0:T(8,128)(2,1)}, bf16[1024,768]{1,0:T(8,128)(2,1)S(1)}, u32[]{:S(2)}) copy-start(bf16[1024,768]{1,0:T(8,128)(2,1)S(1)} %get-tuple-element.153) | copy-start | bytes 4718596
  250.3 7.9 %copy-start.73 = (bf16[1024,768]{1,0:T(8,128)(2,1)}, bf16[1024,768]{1,0:T(8,128)(2,1)S(1)}, u32[]{:S(2)}) copy-start(bf16[1024,768]{1,0:T(8,128)(2,1)S(1)} %get-tuple-element.154) | copy-start | bytes 4718596
  250.3 7.9 %copy-start.70 = (bf16[1024,768]{1,0:T(8,128)(2,1)}, bf16[1024,768]{1,0:T(8,128)(2,1)S(1)}, u32[]{:S(2)}) copy-start(bf16[1024,768]{1,0:T(8,128)(2,1)S(1)} %get-tuple-element.155) | copy-start | bytes 4718596
  250.3 7.8 %copy-start.68 = (bf16[1024,2048]{1,0:T(8,128)(2,1)S(1)}, bf16[1024,2048]{1,0:T(8,128)(2,1)}, u32[]{:S(2)}) copy-start(bf16[1024,2048]{1,0:T(8,128)(2,1)} %all-gather.5.cloned.1.call-done) | copy-start | bytes 12582916
  293.5 25.8 %copy-start.72 = (bf16[1024,768]{1,0:T(8,128)(2,1)S(1)}, bf16[1024,768]{1,0:T(8,128)(2,1)}, u32[]{:S(2)}) copy-start(bf16[1024,768]{1,0:T(8,128)(2,1)} %copy-done.71) | copy-start | bytes 4718596
  293.5 25.8 %copy-start.74 = (bf16[1024,768]{1,0:T(8,128)(2,1)S(1)}, bf16[1024,768]{1,0:T(8,128)(2,1)}, u32[]{:S(2)}) copy-start(bf16[1024,768]{1,0:T(8,128)(2,1)} %copy-done.73) | copy-start | bytes 4718596
  328.1 31.8 %slice-start.4 = ((s8[5242880]{0:T(1024)(128)(4,1)}), s8[4194304]{0:T(1024)(128)(4,1)S(1)}, s32[]{:S(2)}) async-start(s8[5242880]{0:T(1024)(128)(4,1)} %bitcast.152), calls=%async_computation.8 | async-start | bytes 8388608
  354.3 5.6 slice-start.5
  357.0 2.9 copy-start.42
  359.9 5.0 copy-start.38
  359.9 5.0 copy-start.40
  364.9 21.3 %copy-start.59 = (f32[256]{0:T(256)S(1)}, f32[256]{0:T(256)}, u32[]{:S(2)}) copy-start(f32[256]{0:T(256)} %copy-done.58) | copy-start | bytes 3076
  386.2 5.3 copy-start.12
  386.2 5.3 copy-start.15
  391.4 2.8 copy-start.16
  414.2 2.4 copy-start.24
  414.2 3.7 copy-start.37
  414.2 3.7 copy-start.45
  414.2 3.7 copy-start.46
  416.6 29.7 %collective-permute-start.1 = (f32[3,1280]{1,0:T(4,128)}, f32[3,1280]{1,0:T(4,128)S(1)}, u32[]{:S(2)}, u32[]{:S(2)}) collective-permute-start(f32[3,1280]{1,0:T(4,128)} %get-tuple-element.142), channel_id=1, source_target_pairs={{2,0},{4,2},{6,4},{8,6},{10,8},{12,10},{14,12},{16,14},{18,16},{20... | collective-permute-start | bytes 46088 | tf_op jit(solution)/shard_map/ppermute | solution.py:774
  422.5 5.5 copy-start.54
  428.1 2.1 copy-start.23
  428.2 2.4 copy-start.19
  430.6 3.0 copy-start.36
  430.6 3.0 copy-start.39
  430.6 3.0 copy-start.41
  430.6 10.8 %slice-start = ((s8[5242880]{0:T(1024)(128)(4,1)}), s8[4194304]{0:T(1024)(128)(4,1)S(1)}, s32[]{:S(2)}) async-start(s8[5242880]{0:T(1024)(128)(4,1)} %bitcast.137), calls=%async_computation.4 | async-start | bytes 8388608
  433.5 4.0 copy-start.44
  433.5 7.8 %slice-start.1 = ((s8[5242880]{0:T(1024)(128)(4,1)}), s8[1048576]{0:T(1024)(128)(4,1)S(1)}, s32[]{:S(2)}) async-start(s8[5242880]{0:T(1024)(128)(4,1)} %bitcast.137), calls=%async_computation.5 | async-start | bytes 2097152
  441.4 2.9 copy-start.25
  451.5 2.7 copy-start.26
  451.5 2.4 copy-start.28
  598.9 4.9 copy-start.48
  598.9 4.9 copy-start.49
  637.8 2.3 copy-start.50
  (22 other events, 28.0 us)
Sparse Core Ops, SparseCore 0:
  25.7 119.9 all-gather.2
  147.4 30.5 all-gather.4
  286.5 86.0 reduce-scatter.3

commit v2 on v0

v2 whole, which is shorter than its diff:
```python
import functools
import jax
import jax.numpy as jnp
from jax import lax
from jax.experimental import pallas as pl
from jax.experimental.pallas import tpu as pltpu
from jax.sharding import Mesh, PartitionSpec as P

CONV = 4
EDGE = CONV - 1
BLOCK = 256
EPSILON = 1e-06
MESH = pl.DeviceIdType.MESH
ANY = pl.BlockSpec(memory_space=pl.ANY)
HBM = pl.BlockSpec(memory_space=pltpu.HBM)
VM = pl.BlockSpec(memory_space=pltpu.VMEM)
MIB = 1024 * 1024
AXES = ("z", "y", "x")
SEQ = ("z", "y", "x")
ORDERS = (("x", "y", "z"), ("y", "z", "x"), ("z", "x", "y"))
F32, BF16 = jnp.float32, jnp.bfloat16
GELU_C, GELU_A = 0.7978845608028654, 0.044715
DMA = pltpu.SemaphoreType.DMA


def dot(left, right):
    return jnp.dot(left, right, preferred_element_type=F32)


def dot_t(left, right):
    return lax.dot_general(left, right, (((1,), (1,)), ((), ())), preferred_element_type=F32)


def outer(left, right):
    return lax.dot_general(left, right, (((0,), (0,)), ((), ())), preferred_element_type=F32)


def greet(peers):
    sem = pltpu.get_barrier_semaphore()
    for peer in peers:
        pl.semaphore_signal(sem, inc=1, device_id=peer, device_id_type=MESH)
    pl.semaphore_wait(sem, len(peers))


def push(src, dst, send, recv, peer):
    return pltpu.make_async_remote_copy(
        src_ref=src, dst_ref=dst, send_sem=send, recv_sem=recv, device_id=peer, device_id_type=MESH
    )


def ring(axis):
    me = lax.axis_index(axis)
    return me, lax.rem(me + 1, 4), lax.rem(me + 2, 4), lax.rem(me + 3, 4)


def all_neighbours():
    peers = []
    for axis in AXES:
        _, up, _, down = ring(axis)
        peers += [{axis: up}, {axis: down}]
    return peers


def params(cid, mib):
    return pltpu.CompilerParams(
        collective_id=cid, has_side_effects=True, vmem_limit_bytes=mib * MIB
    )


def part_of(done, axis, index, rows, cols):
    spot = []
    for name in AXES:
        if name in done:
            spot.append(pl.ds(0, 4))
        elif name == axis:
            spot.append(index)
        else:
            spot.append(lax.axis_index(name))
    return tuple(spot) + (rows, cols)


def pick(names, axis, index, others):
    spot, rest = [], iter(others)
    for name in names:
        spot.append(index if name == axis else next(rest))
    return tuple(spot)


class Scatter:
    def __init__(self, entry, src, cols, order, cuts, bufs, out, send, recv):
        self.entry, self.src, self.order = entry, src, order
        self.start, self.width = cols
        self.cuts, self.bufs, self.out = cuts, list(bufs), out
        self.send, self.recv = send, recv
        self.left, self.sent = AXES, []
        self.direct = 0 if cuts is None else 1

    def view(self, at, rows, cols):
        start = self.start if self.phase == 0 else 0
        if rows is None:
            rows = pl.ds(0, self.src.shape[-2])
        first, width = (0, self.width) if cols is None else cols
        return at + (rows, pl.ds(start + first, width))

    def spread(self, i):
        return ((i // 4, lax.rem(i, 4)), (i,), ())[self.phase]

    def target(self, at, rows, cols):
        rows = pl.ds(0, self.src.shape[-2]) if rows is None else rows
        cols = pl.ds(0, self.width) if cols is None else pl.ds(*cols)
        return at + (rows, cols)

    def copy(self, src, dst, way, kind, peer):
        at = (self.entry, self.phase, way, kind)
        copy = push(src, dst, self.send.at[at], self.recv.at[at], {self.axis: peer})
        copy.start()
        self.sent.append(copy)
        return copy

    def begin(self, phase):
        self.phase, self.axis = phase, self.order[phase]
        self.full = (pl.ds(0, 4),) * (2 - phase)
        self.first, self.second = [], []
        if phase >= self.direct:
            self.threes = self.bufs.pop(0)
            self.acc = self.bufs.pop(0) if phase < 2 else self.out
            for step, peer in enumerate(ring(self.axis)[1:]):
                src = self.src.at[self.view(pick(self.left, self.axis, peer, self.full), None, None)]
                self.second.append(self.copy(src, self.threes.at[step], step, 0, peer))
            return
        self.ones, self.twos, self.acc = self.bufs.pop(0), self.bufs.pop(0), self.bufs.pop(0)
        _, up, far, down = ring(self.axis)
        for way, peer in enumerate((up, down)):
            src = self.src.at[self.view(pick(self.left, self.axis, far, self.full), *self.cuts[way])]
            self.first.append(self.copy(src, self.ones.at[way], way, 0, peer))
        for way, peer in enumerate((up, down)):
            cut = self.cuts[1 - way]
            src = self.src.at[self.view(pick(self.left, self.axis, peer, self.full), *cut)]
            dst = self.twos.at[self.target((way,) + self.full, *cut)]
            self.second.append(self.copy(src, dst, way, 1, peer))

    def middle(self):
        _, up, _, down = ring(self.axis)
        for way, peer in enumerate((up, down)):
            cut = self.cuts[way]
            self.first[way].wait_recv()

            def add(i, carry, way=way, peer=peer, cut=cut):
                there = (way,) + self.spread(i)
                own = self.src[self.view(pick(self.left, self.axis, peer, self.spread(i)), *cut)]
                total = self.ones[there].astype(F32) + own.astype(F32)
                self.ones[there] = total.astype(BF16)
                return carry

            lax.fori_loop(0, 4 ** (2 - self.phase), add, 0)
            dst = self.twos.at[self.target((way,) + self.full, *cut)]
            self.second.append(self.copy(self.ones.at[way], dst, way, 2, peer))

    def finish(self):
        me = lax.axis_index(self.axis)
        for copy in self.second:
            copy.wait_recv()
        if self.phase >= self.direct:
            parts = [(self.threes, 0), (self.threes, 1), (self.threes, 2)]
        else:
            parts = [(self.twos, 0), (self.twos, 1)]

        def total(i, carry):
            there = self.spread(i)
            whole = self.src[self.view(pick(self.left, self.axis, me, there), None, None)].astype(F32)
            for buf, slot in parts:
                whole = whole + buf[(slot,) + there].astype(F32)
            self.acc[there + (slice(None), slice(None))] = whole.astype(self.acc.dtype)
            return carry

        lax.fori_loop(0, 4 ** (2 - self.phase), total, 0)
        self.src = self.acc
        self.left = tuple(name for name in self.left if name != self.axis)

    def drain(self):
        for copy in self.sent:
            copy.wait_send()


def scatter_buffers(rows, width, cut):
    bufs = []
    for phase in range(3):
        cube = (4,) * (2 - phase)
        if phase == 0 and cut is not None:
            bufs.append(pltpu.VMEM((2,) + cube + cut, BF16))
            bufs.append(pltpu.VMEM((2,) + cube + (rows, width), BF16))
        else:
            bufs.append(pltpu.VMEM((3,) + cube + (rows, width), BF16))
        if phase < 2:
            bufs.append(pltpu.VMEM(cube + (rows, width), BF16))
    return bufs


class Gather:
    def __init__(self, entry, out, order, cols, send, recv, done=(), ring_rounds=()):
        self.entry, self.out, self.order, self.cols = entry, out, order, pl.ds(*cols)
        self.send, self.recv, self.sent = send, recv, []
        self.done, self.ring_rounds = done, ring_rounds

    def spot(self, origin, rows=None):
        rows = pl.ds(0, self.out.shape[3]) if rows is None else rows
        return self.out.at[part_of(self.done, self.axis, origin, rows, self.cols)]

    def copy(self, src, dst, step, way, peer):
        at = (self.entry, self.phase, step, way)
        copy = push(src, dst, self.send.at[at], self.recv.at[at], {self.axis: peer})
        copy.start()
        self.sent.append(copy)
        return copy

    def begin(self, phase, src=None):
        self.phase, self.axis = phase, self.order[phase]
        me, up, far, down = ring(self.axis)
        here = self.spot(me)
        src = here if src is None else src.at[:, self.cols]
        peers = (up, down) if phase in self.ring_rounds else (up, far, down)
        self.copies = [self.copy(src, here, 0, way, peer) for way, peer in enumerate(peers)]

    def middle(self):
        _, up, _, down = ring(self.axis)
        half = self.out.shape[3] // 2
        first, self.copies = self.copies, []
        for way, (peer, origin) in enumerate(((up, down), (down, up))):
            first[way].wait_recv()
            spot = self.spot(origin, pl.ds(way * half, half))
            self.copies.append(self.copy(spot, spot, 1, way, peer))

    def hold(self):
        for copy in self.copies:
            copy.wait_recv()

    def finish(self):
        self.hold()
        self.done = self.done + (self.axis,)

    def drain(self):
        for copy in self.sent:
            copy.wait_send()


class Rounds:
    def __init__(self, slots, send, recv, entry=0, order=("x", "y", "z")):
        self.slots, self.send, self.recv, self.sent = slots, send, recv, []
        self.entry, self.order = entry, order

    def begin(self, phase, rows):
        self.phase, axis = phase, self.order[phase]
        me = lax.axis_index(axis)
        for at, value in rows:
            self.slots[phase, me, at] = value
        self.copies = []
        for step, peer in enumerate(ring(axis)[1:]):
            spot = self.slots.at[phase, me]
            at = (self.entry, phase, step)
            copy = push(spot, spot, self.send.at[at], self.recv.at[at], {axis: peer})
            copy.start()
            self.copies.append(copy)

    def finish(self):
        for copy in self.copies:
            copy.wait_recv()
        self.sent += self.copies

    def drain(self):
        for copy in self.sent:
            copy.wait_send()


class Prefix(Rounds):
    def start(self, pair, backward):
        self.backward, self.cur, self.head = backward, pair, None
        self.share(0)

    def share(self, phase):
        self.begin(phase, [(slice(0, 1), self.cur[0]), (slice(1, 2), self.cur[1])])

    def step(self):
        self.finish()
        me = lax.axis_index(self.order[self.phase])
        run = (jnp.ones_like(self.cur[0]), jnp.zeros_like(self.cur[1]))
        mine = run
        for j in (3, 2, 1, 0) if self.backward else (0, 1, 2, 3):
            take = me == j
            mine = (jnp.where(take, run[0], mine[0]), jnp.where(take, run[1], mine[1]))
            fac, val = self.slots[self.phase, j, 0:1], self.slots[self.phase, j, 1:2]
            run = (run[0] * fac, val + fac * run[1])
        self.cur = run
        if self.head is None:
            self.head = mine
        else:
            self.head = (mine[0] * self.head[0], self.head[1] + self.head[0] * mine[1])
        if self.phase < 2:
            self.share(self.phase + 1)
        return self.head


class Total(Rounds):
    def start(self, value):
        self.begin(0, [(slice(None), value)])

    def step(self):
        self.finish()
        at = self.slots
        k = self.phase
        value = (at[k, 0] + at[k, 1]) + (at[k, 2] + at[k, 3])
        if k + 1 < len(self.order):
            self.begin(k + 1, [(slice(None), value)])
        return value


def axis_peers():
    return [{axis: ring(axis)[step]} for axis in AXES for step in (1, 2, 3)]


def along_seq(distance):
    place = lax.axis_index("z") * 16 + lax.axis_index("y") * 4 + lax.axis_index("x")
    place = lax.rem(place + distance + 64, 64)
    return {"z": place // 16, "y": lax.rem(place // 4, 4), "x": lax.rem(place, 4)}


CHUNKS = ((0, 384), (384, 512), (896, 384))
ROW_CUTS = ((pl.ds(0, 16), None), (pl.ds(16, 16), None))
HALVES = ((0, 128), (128, 128))


def gelu_parts(x):
    inner = GELU_C * (x + GELU_A * x * x * x)
    t = jnp.tanh(inner)
    slope = GELU_C * (1.0 + 3.0 * GELU_A * x * x)
    return 0.5 * x * (1.0 + t), 0.5 * (1.0 + t) + 0.5 * x * (1.0 - t * t) * slope


def mlp_kernel(
    nm_ref, go_ref, hidden_ref, inv_ref, gain_ref, go_hbm, w_hbm,
    result_ref, grad_hidden_ref, low_ref, term_ref, dw_ref,
    go, w, gathered, npart, opart, mlp_in, ggu, got, one, two, ogot, oone, otwo, low_half, result_half,
    load_sem, wsend, wrecv, gsend, grecv, gsib_send, gsib_recv,
    send_sem, recv_sem, sib_send, sib_recv, osend_sem, orecv_sem, osib_send, osib_recv, core_sem,
):
    rows, width = nm_ref.shape
    half = rows // 2
    units = mlp_in.shape[1]
    me, up, far, down = ring("x")
    core = lax.axis_index("mp")
    other = {"mp": 1 - core}
    loads = [
        pltpu.make_async_copy(go_hbm, go, load_sem.at[0]),
        pltpu.make_async_copy(nm_ref, gathered.at[me, core], load_sem.at[1]),
    ]
    wide = w.shape[4] // 2
    full, every = pl.ds(0, 4), pl.ds(0, w.shape[3])
    last = (("z", 0), ("y", wide))

    def weight_set(axis, index, at, cols):
        return ((index, full) if axis == "z" else (full, index)) + (full, at, pl.ds(cols, wide))

    for e, (axis, cols) in enumerate(last):
        here, ahead, _, behind = ring(axis)
        for k, index in enumerate((here, ahead, behind)):
            spot = weight_set(axis, index, every, cols)
            loads.append(pltpu.make_async_copy(w_hbm.at[spot], w.at[spot], load_sem.at[2 + 3 * e + k]))
    for load in loads:
        load.start()
    peers = [{"x": up}, {"x": down}, other]
    for axis in ("y", "z"):
        peers += [{axis: ring(axis)[1]}, {axis: ring(axis)[3]}]
    greet(peers)
    top, low = pl.ds(0, half), pl.ds(half, half)
    spot = gathered.at[me, core]
    first = []
    for way, peer in enumerate((up, down)):
        copy = push(nm_ref, spot, gsend.at[0, way], grecv.at[0, way], {"x": peer})
        copy.start()
        first.append(copy)
    across = [push(nm_ref, spot, gsib_send.at[0], gsib_recv.at[0], other)]
    across[0].start()
    rest = []
    for e, (axis, cols) in enumerate(last):
        _, ahead, _, behind = ring(axis)
        deep = w.shape[3] // 2
        for way, (peer, origin) in enumerate(((ahead, behind), (behind, ahead))):
            spot = weight_set(axis, origin, pl.ds(way * deep, deep), cols)
            copy = push(w_hbm.at[spot], w.at[spot], wsend.at[e, way], wrecv.at[e, way], {axis: peer})
            copy.start()
            rest.append(copy)
    second = []
    for way, (peer, origin, piece) in enumerate(((up, down, top), (down, up, low))):
        first[way].wait_recv()
        spot = gathered.at[origin, core, piece]
        copy = push(spot, spot, gsend.at[1, way], grecv.at[1, way], {"x": peer})
        copy.start()
        second.append(copy)
        spot = gathered.at[origin, core]
        copy = push(spot, spot, gsib_send.at[1 + way], gsib_recv.at[1 + way], other)
        copy.start()
        across.append(copy)
    for copy in rest:
        copy.wait_recv()
    for load in loads:
        load.wait()
    for way, piece in enumerate((top, low)):
        second[way].wait_recv()
        spot = gathered.at[far, core, piece]
        copy = push(spot, spot, gsib_send.at[3 + way], gsib_recv.at[3 + way], other)
        copy.start()
        across.append(copy)
    for copy in across:
        copy.wait_recv()

    def tile(j, start=0):
        return pl.ds(pl.multiple_of(start + j * 256, 256), 256)

    def columns(at):
        return w[:, :, :, :, at].reshape(width, 256)

    def shard_tile(i, at):
        return w[i // 2, pl.ds(2 * lax.rem(i, 2), 2), :, :, at].reshape(256, -1)

    def hidden_tile(j, carry):
        tokens_in = gathered[...].reshape(8 * rows, width)
        gate = dot(tokens_in, columns(tile(j)))
        up_lin = dot(tokens_in, columns(tile(j, units)))
        grad = dot(go[...], columns(tile(j, 2 * units)))
        act, slope = gelu_parts(gate)
        mlp_in[:, tile(j)] = (act * up_lin).astype(BF16)
        ggu[:, tile(j)] = (slope * (grad * up_lin)).astype(BF16)
        ggu[:, tile(j, units)] = (grad * act).astype(BF16)
        return carry

    lax.fori_loop(0, units // 256, hidden_tile, 0)

    def back_tile(j, carry):
        back = dot_t(ggu[...], shard_tile(j, pl.ds(0, 2 * units)))
        npart[:, :, :, tile(j)] = back.astype(BF16).reshape(4, 2, rows, 256)
        return carry

    def out_tile(j, carry):
        part = dot_t(mlp_in[...], shard_tile(j, pl.ds(2 * units, units)))
        opart[:, :, :, tile(j)] = part.astype(BF16).reshape(4, 2, rows, 256)
        return carry

    def send_across(part, got, sib_send, sib_recv):
        copies = {}
        for k, (name, chip) in enumerate((("far", far), ("up", up), ("down", down), ("me", me))):
            copy = push(part.at[chip, 1 - core], got.at[chip], sib_send.at[k], sib_recv.at[k], other)
            copy.start()
            copies[name] = copy
        return copies

    def weight_grads(lower, upper):
        def step(i, carry):
            left = gathered[:, :, :, tile(i)].reshape(8 * rows, 256)
            dw_ref[tile(i), pl.ds(0, 2 * units)] = outer(left, ggu[...]).astype(BF16)
            dw_ref[tile(i), pl.ds(2 * units, units)] = outer(go[:, tile(i)], mlp_in[...]).astype(BF16)
            return carry

        lax.fori_loop(lower, upper, step, 0)

    def add(dst, src):
        dst[...] = (dst[...].astype(F32) + src[...].astype(F32)).astype(dst.dtype)

    def far_step(sums, part, got, one, send_sem, recv_sem):
        sums["far"].wait_recv()
        add(got.at[far], part.at[far, core])
        copies = []
        for way, peer in enumerate((up, down)):
            piece = got.at[far, pl.ds(way * half, half)]
            copy = push(piece, one.at[way], send_sem.at[0, way], recv_sem.at[0, way], {"x": peer})
            copy.start()
            copies.append(copy)
        return copies

    def near_step(sums, part, got, one, two, send_sem, recv_sem, before):
        copies = []
        for way, (peer, name) in enumerate(((up, "up"), (down, "down"))):
            sums[name].wait_recv()
            add(got.at[peer], part.at[peer, core])
            before[way].wait_recv()
            add(got.at[peer, pl.ds(way * half, half)], one.at[way])
            copy = push(
                got.at[peer], two.at[way], send_sem.at[1, way], recv_sem.at[1, way], {"x": peer}
            )
            copy.start()
            copies.append(copy)
        return copies

    def last_step(sums, part, got, two, before):
        sums["me"].wait_recv()
        total = got[me].astype(F32) + part[me, core].astype(F32)
        for way in range(2):
            before[way].wait_recv()
            total = total + two[way].astype(F32)
        return total

    lax.fori_loop(0, width // 256, back_tile, 0)
    sums = send_across(npart, got, sib_send, sib_recv)
    lax.fori_loop(0, width // 256, out_tile, 0)
    third = far_step(sums, npart, got, one, send_sem, recv_sem)
    osums = send_across(opart, ogot, osib_send, osib_recv)
    weight_grads(0, 3)
    fourth = near_step(sums, npart, got, one, two, send_sem, recv_sem, third)
    fifth = far_step(osums, opart, ogot, oone, osend_sem, orecv_sem)
    weight_grads(3, 7)
    grad_normed = last_step(sums, npart, got, two, fourth)
    sixth = near_step(osums, opart, ogot, oone, otwo, osend_sem, orecv_sem, fifth)
    hat = hidden_ref[...] * inv_ref[...]
    grad_hat = grad_normed * gain_ref[...]
    inner = jnp.mean(grad_hat * hat, axis=-1, keepdims=True)
    grad_hidden = go_ref[...].astype(F32) + inv_ref[...] * (grad_hat - hat * inner)
    grad_hidden_ref[...] = grad_hidden
    term_ref[...] = jnp.sum(grad_normed * hat, axis=0, keepdims=True)
    low_half[...] = grad_hidden.astype(BF16)
    low_ref[core] = low_half[...]
    swaps = [push(low_half, low_ref.at[core], core_sem.at[0], core_sem.at[1], other)]
    swaps[0].start()
    weight_grads(7, 8)
    mlp_out = last_step(osums, opart, ogot, otwo, sixth)
    result_half[...] = (hidden_ref[...] + mlp_out).astype(BF16)
    result_ref[core] = result_half[...]
    swaps.append(push(result_half, result_ref.at[core], core_sem.at[2], core_sem.at[3], other))
    swaps[1].start()
    for copy in swaps:
        copy.wait()
    for copy in first + second + third + fourth + fifth + sixth + across + rest:
        copy.wait_send()
    for copies in (sums, osums):
        for copy in copies.values():
            copy.wait_send()


def mlp(normed, grad_out, hidden, inverse, gain, grad_out_all, weights, cid):
    rows, width = normed.shape
    units = weights.shape[4] // 3

    def block(dtype, *shape):
        return pltpu.VMEM(shape, dtype)

    return pl.pallas_call(
        mlp_kernel,
        out_shape=[
            jax.ShapeDtypeStruct((2, rows, width), BF16),
            jax.ShapeDtypeStruct((rows, width), F32),
            jax.ShapeDtypeStruct((2, rows, width), BF16),
            jax.ShapeDtypeStruct((1, width), F32),
            jax.ShapeDtypeStruct((width, 3 * units), BF16),
        ],
        in_specs=[VM] * 5 + [ANY] * 2,
        out_specs=[VM] * 5,
        scratch_shapes=[
            block(BF16, 8 * rows, width),
            block(BF16, *weights.shape),
            block(BF16, 4, 2, rows, width),
            block(BF16, 4, 2, rows, width),
            block(BF16, 4, 2, rows, width),
            block(BF16, 8 * rows, units),
            block(BF16, 8 * rows, 2 * units),
        ]
        + [block(BF16, 4, rows, width), block(BF16, 2, rows // 2, width), block(BF16, 2, rows, width)] * 2
        + [block(BF16, rows, width)] * 2
        + [DMA((8,)), DMA((2, 2)), DMA((2, 2)), DMA((2, 2)), DMA((2, 2)), DMA((5,)), DMA((5,))]
        + [DMA((2, 2)), DMA((2, 2)), DMA((4,)), DMA((4,))] * 2
        + [DMA((4,))],
        compiler_params=params(cid, 60),
    )(normed, grad_out, hidden, inverse, gain, grad_out_all, weights)


def lanes(n):
    return pl.ds(pl.multiple_of(n * BLOCK, BLOCK), BLOCK)


def minus_expm1(x):
    series = jnp.ones_like(x)
    for k in (9, 8, 7, 6, 5, 4, 3, 2):
        series = 1.0 + x * (1.0 / k) * series
    return jnp.where(x > -0.4, -x * series, 1.0 - jnp.exp(x))


CONV_W, CONV_B, RATES, BIAS, CONV_STATE, H_INIT, SLOPE = 0, 4, 5, 6, 8, 11, 12


def rec_forward_kernel(*refs):
    (
        tokens_ref, tail_ref, gain_ref, gain_mlp_ref, v_ref, keep_ref, lin_in, gate_in, back_in, quarters_ref, g_hbm,
        lin_out, gate_out, back_out, mlp_out, ext_out, act_out, mixed_out, reset_out, input_out, f_out, states_out,
        branch_out, normed_out, inv_ref, rms_ref, hidden_ref, nm_ref, inv_mlp_ref, rms_mlp_ref,
        wl, wg, wb, ext, gate_lin, mixed_v, reset_v, input_v, f_v, states, branch_v, normed, tail_in, driven, cf_v,
        part, part_low, part_in, g_v, rms_v, slots,
        tail_sem, load_sem, save_sem, own_sem, move_send, move_recv, send, recv, small_send, small_recv, core_sem,
    ) = refs
    count, width = tokens_ref.shape
    rec = f_v.shape[1]
    blocks = rec // BLOCK
    half = count // 2
    core = lax.axis_index("mp")
    other = {"mp": 1 - core}
    here = tuple(lax.axis_index(name) for name in AXES)
    load = pltpu.make_async_copy(g_hbm, g_v, load_sem)
    load.start()
    owns = [
        pltpu.make_async_copy(lin_in, wl.at[here], own_sem.at[0]),
        pltpu.make_async_copy(gate_in, wg.at[here], own_sem.at[1]),
        pltpu.make_async_copy(back_in, wb.at[here], own_sem.at[2]),
        pltpu.make_async_copy(quarters_ref.at[here[2]], mlp_out.at[here], own_sem.at[3]),
    ]
    for own in owns:
        own.start()
    greet(axis_peers() + [other, along_seq(1), along_seq(-1)])
    tail_copy = push(tail_ref, tail_in, tail_sem.at[0], tail_sem.at[1], along_seq(1))
    tail_copy.start()
    lin = [Gather(e, wl, ORDERS[e], CHUNKS[e], send, recv, ring_rounds=(2,)) for e in range(3)]
    rest = [
        Gather(3 * k + e, out, ORDERS[(e + k) % 3], CHUNKS[e], send, recv, ring_rounds=(1, 2))
        for k, out in ((1, wg), (2, wb))
        for e in range(3)
    ]
    wide = mlp_out.shape[4] // 2
    mlp_flows = [
        Gather(9 + e, mlp_out, order, (e * wide, wide), send, recv, done=("x",), ring_rounds=(1,))
        for e, order in enumerate((("y", "z"), ("z", "y")))
    ]

    def each(group, name, *args):
        for flow in group:
            getattr(flow, name)(*args)

    each(lin, "begin", 0, lin_in)
    moves = []
    for step, peer in enumerate(ring("x")[1:]):
        copy = push(
            quarters_ref.at[peer], mlp_out.at[here], move_send.at[step], move_recv.at[step], {"x": peer}
        )
        copy.start()
        moves.append(copy)
    each(rest[:3], "begin", 0, gate_in)
    each(rest[3:], "begin", 0, back_in)

    def norm(values):
        mean_sq = jnp.mean(values * values, axis=-1, keepdims=True)
        inverse = lax.rsqrt(mean_sq + EPSILON)
        return values * inverse, inverse, jnp.sqrt(mean_sq + EPSILON)

    def norm_step(i, carry):
        at = pl.ds(pl.multiple_of(i * 64, 64), 64)
        hat, inverse, rms = norm(tokens_ref[at].astype(F32))
        inv_ref[at] = inverse
        rms_ref[at] = rms
        normed[pl.ds(pl.multiple_of(16 + i * 64, 16), 64)] = (hat * gain_ref[...]).astype(BF16)
        return carry

    lax.fori_loop(0, count // 64, norm_step, 0)
    for own in owns:
        own.wait()
    each(lin, "finish")
    each(lin, "begin", 1)
    each(rest, "finish")
    tail_copy.wait_recv()
    normed[0:16] = (norm(tail_in[...].astype(F32))[0] * gain_ref[...]).astype(BF16)
    saves = []

    def save(src, dst):
        copy = pltpu.make_async_copy(src, dst, save_sem.at[len(saves)])
        copy.start()
        saves.append(copy)

    save(normed.at[pl.ds(16, count)], normed_out)
    each(lin, "finish")
    each(lin, "begin", 2)
    each(rest, "begin", 1)
    each(lin, "middle")
    each(rest, "middle")
    for copy in moves:
        copy.wait_recv()
    each(mlp_flows, "begin", 0)
    each(rest, "finish")
    each(rest, "begin", 2)
    load.wait()
    each(lin, "finish")
    save(wl, lin_out)
    is_first = (here[0] + here[1] + here[2]) == 0

    def rec_step(n, carry):
        at = lanes(n)
        ext[:, at] = dot(normed[...], wl[:, :, :, :, at].reshape(width, BLOCK))

        @pl.when(is_first)
        def _():
            ext[16 - EDGE : 16, at] = v_ref[CONV_STATE : CONV_STATE + EDGE, at]

        total = v_ref[CONV_B : CONV_B + 1, at] + jnp.zeros((count, BLOCK), F32)
        for k in range(CONV):
            total = total + v_ref[CONV_W + k : CONV_W + k + 1, at] * ext[pl.ds(16 - EDGE + k, count), at]
        mixed = total.astype(BF16)
        mixed_v[:, at] = mixed
        reset = jax.nn.sigmoid(dot(mixed, g_v[0, n]) + v_ref[BIAS : BIAS + 1, at])
        gated = jax.nn.sigmoid(dot(mixed, g_v[1, n]) + v_ref[BIAS + 1 : BIAS + 2, at])
        reset_v[:, at] = reset
        input_v[:, at] = gated
        log_decay = -8.0 * v_ref[RATES : RATES + 1, at] * reset
        f_v[:, at] = jnp.exp(log_decay) * keep_ref[...]
        driven[:, at] = jnp.sqrt(minus_expm1(2.0 * log_decay)) * gated * mixed.astype(F32)
        return carry

    lax.fori_loop(0, blocks, rec_step, 0)
    for src, dst in ((ext, ext_out), (mixed_v, mixed_out), (reset_v, reset_out), (input_v, input_out), (f_v, f_out)):
        save(src, dst)

    def group(i, carry):
        base = pl.multiple_of(i * 8, 8)
        f, d = f_v[pl.ds(base, 8)], driven[pl.ds(base, 8)]
        cf, cd = carry
        cfs, cds = [], []
        for r in range(8):
            cf = cf * f[r : r + 1]
            cd = cd * f[r : r + 1] + d[r : r + 1]
            cfs.append(cf)
            cds.append(cd)
        cf_v[pl.ds(base, 8)] = jnp.concatenate(cfs, axis=0)
        states[pl.ds(pl.multiple_of(base + 8, 8), 8)] = jnp.concatenate(cds, axis=0)
        return cf, cd

    zero = jnp.zeros((1, rec), F32)
    ends = lax.fori_loop(0, count // 8, group, (zero + 1.0, zero))
    prefix = Prefix(slots, small_send, small_recv)
    prefix.start(ends, False)
    prefix.step()
    prefix.step()
    each(rest, "middle")
    each(mlp_flows, "finish")
    each(mlp_flows, "begin", 1)
    head = prefix.step()
    carry_in = head[1] + head[0] * v_ref[H_INIT : H_INIT + 1]
    each(rest, "finish")
    save(wg, gate_out)
    save(wb, back_out)

    def gate_step(n, carry):
        gate_lin[:, lanes(n)] = dot(normed[16:], wg[:, :, :, :, lanes(n)].reshape(width, BLOCK))
        return carry

    lax.fori_loop(0, blocks, gate_step, 0)
    save(gate_lin, act_out)
    states[0:8] = jnp.broadcast_to(carry_in, (8, rec))

    def branch_step(n, carry):
        at = lanes(n)
        value = states[8:, at] + cf_v[:, at] * states[0:1, at]
        states[8:, at] = value
        branch_v[:, at] = (gelu_parts(gate_lin[:, at])[0] * value).astype(BF16)
        return carry

    lax.fori_loop(0, blocks, branch_step, 0)
    save(states, states_out)
    save(branch_v, branch_out)

    def out_step(i, carry):
        at = pl.ds(pl.multiple_of(i * 256, 256), 256)
        rows = wb[i // 2, pl.ds(2 * lax.rem(i, 2), 2)].reshape(256, rec)
        value = dot_t(branch_v[...], rows)
        part[0, :, at] = value[:half]
        part[1, :, at] = value[half:]
        return carry

    lax.fori_loop(0, width // 256, out_step, 0)
    part_low[...] = part[1 - core].astype(BF16)
    part_copy = push(part_low, part_in, core_sem.at[0], core_sem.at[1], other)
    part_copy.start()
    part_copy.wait_recv()
    mine = pl.ds(pl.multiple_of(core * half, half), half)
    hidden = tokens_ref[mine].astype(F32) + (part[core] + part_in[...].astype(F32))
    hidden_ref[...] = hidden
    hat, inverse, rms = norm(hidden)
    inv_mlp_ref[...] = inverse
    rms_v[...] = jnp.broadcast_to(rms, (half, 128))
    rms_mlp_ref[core] = rms_v[...]
    rms_copy = push(rms_v, rms_mlp_ref.at[core], core_sem.at[2], core_sem.at[3], other)
    rms_copy.start()
    nm_ref[...] = (hat * gain_mlp_ref[...]).astype(BF16)
    each(mlp_flows, "hold")
    rms_copy.wait()
    for copy in moves:
        copy.wait_send()
    for copy in saves:
        copy.wait()
    each(lin, "drain")
    each(rest, "drain")
    each(mlp_flows, "drain")
    prefix.drain()
    part_copy.wait_send()
    tail_copy.wait_send()


def rec_forward(tokens, tail, gain_rec, gain_mlp, vectors, keep, lin, gate, back, quarters, gates, cid):
    count, width = tokens.shape
    rows, rec = lin.shape
    half = count // 2

    def cube(last):
        return (4, 4, 4, rows, last)

    def sds(shape, dtype):
        return jax.ShapeDtypeStruct(shape, dtype)

    saved = [
        (cube(rec), BF16),
        (cube(rec), BF16),
        (cube(rec), BF16),
        (cube(quarters.shape[2]), BF16),
        ((count + 16, rec), F32),
        ((count, rec), F32),
        ((count, rec), BF16),
        ((count, rec), F32),
        ((count, rec), F32),
        ((count, rec), F32),
        ((count + 8, rec), F32),
        ((count, rec), BF16),
        ((count, width), BF16),
    ]
    small = [
        ((count, 1), F32),
        ((count, 1), F32),
        ((half, width), F32),
        ((half, width), BF16),
        ((half, 1), F32),
        ((2, half, 128), F32),
    ]
    scratch = saved[:3] + saved[4:12] + [((count + 16, width), BF16), (tail.shape, BF16)]
    scratch += [((count, rec), F32), ((count, rec), F32), ((2, half, width), F32)]
    scratch += [((half, width), BF16), ((half, width), BF16), (gates.shape, BF16), ((half, 128), F32), ((3, 4, 2, rec), F32)]
    return pl.pallas_call(
        rec_forward_kernel,
        out_shape=[sds(*one) for one in saved + small],
        in_specs=[VM] * 9 + [ANY] * 2,
        out_specs=[HBM] * len(saved) + [VM] * len(small),
        scratch_shapes=[pltpu.VMEM(*one) for one in scratch]
        + [
            DMA((2,)),
            DMA,
            DMA((12,)),
            DMA((4,)),
            DMA((3,)),
            DMA((3,)),
            DMA((11, 3, 2, 3)),
            DMA((11, 3, 2, 3)),
            DMA((1, 3, 3)),
            DMA((1, 3, 3)),
            DMA((4,)),
        ],
        compiler_params=params(cid, 60),
    )(tokens, tail, gain_rec[None], gain_mlp[None], vectors, keep, lin, gate, back, quarters, gates)


G_BIAS, G_LAM, G_CONV_W, G_CONV_B, G_H, G_STATE = 0, 2, 3, 7, 8, 9
GATE_ROWS = 48


def shard_rows(ref, i, value):
    value = value.reshape(2, 4, 32, value.shape[1])
    ref[i // 2, pl.ds(2 * lax.rem(i, 2), 2)] = value


def rec_back_kernel(*refs):
    (
        gh_ref, branch_ref, normed_ref, gate_ref, states_ref, f_ref, v_ref,
        wb_hbm, ext_hbm, mixed_hbm, reset_hbm, input_hbm, g_hbm,
        gate_low_ref, low_ref, small_ref, out0, out1, out2, out3, out4, out5, out6, out7,
        wb, ext, mixed_v, reset_v, input_v, g_v, cb, al, gs, gm, dw_out, dw_gate, tail, edge, edge_in, gg_ref,
    ) = refs[:40]
    bufs, refs = refs[40 : 40 + 46], refs[40 + 46 :]
    slots, load_sem, send, recv, small_send, small_recv, edge_sem = refs
    count = gate_ref.shape[0]
    rec = gate_ref.shape[1]
    blocks = rec // BLOCK
    pairs = ((wb_hbm, wb), (ext_hbm, ext), (mixed_hbm, mixed_v), (reset_hbm, reset_v), (input_hbm, input_v), (g_hbm, g_v))
    loads = [pltpu.make_async_copy(src, dst, load_sem.at[k]) for k, (src, dst) in enumerate(pairs)]
    for load in loads:
        load.start()
    ahead, behind = along_seq(1), along_seq(-1)
    greet(axis_peers() + [ahead, behind])
    place = lax.axis_index("z") * 16 + lax.axis_index("y") * 4 + lax.axis_index("x")
    is_first = jnp.where(place == 0, 1.0, 0.0)
    has_next = jnp.where(place == 63, 0.0, 1.0)
    outs = (out0, out1, out2, out3, out4, out5, out6, out7)
    flows = [
        Scatter(
            e, dw_out if e < 3 else dw_gate, CHUNKS[e % 3], ORDERS[e % 3], ROW_CUTS,
            bufs[6 * e : 6 * e + 6], outs[e], send, recv,
        )
        for e in range(6)
    ]
    gates = [
        Scatter(6 + e, gg_ref, HALVES[e], ORDERS[e], None, bufs[36 + 5 * e : 41 + 5 * e], outs[6 + e], send, recv)
        for e in range(2)
    ]
    flows += gates
    early, late = flows[:3], flows[3:6]

    def each(group, name, *args):
        for flow in group:
            getattr(flow, name)(*args)

    def weight_grad(ref, left, right):
        def step(i, carry):
            cols = pl.ds(pl.multiple_of(i * 256, 256), 256)
            shard_rows(ref, i, outer(left[:, cols], right[...]).astype(BF16))
            return carry

        lax.fori_loop(0, left.shape[1] // 256, step, 0)

    weight_grad(dw_out, gh_ref, branch_ref)
    each(early, "begin", 0)
    loads[0].wait()

    def branch_step(n, carry):
        grad = dot(gh_ref[...], wb[:, lanes(n)])
        act, slope = gelu_parts(gate_ref[:, lanes(n)])
        gate_low_ref[:, lanes(n)] = (slope * (grad * states_ref[8:, lanes(n)])).astype(BF16)
        gs[:, lanes(n)] = grad * act
        return carry

    lax.fori_loop(0, blocks, branch_step, 0)

    def group(i, carry):
        base = pl.multiple_of(count - 8 - i * 8, 8)
        f, d = f_ref[pl.ds(base, 8)], gs[pl.ds(base, 8)]
        follow, cf, cd = carry
        cfs, cds = [None] * 8, [None] * 8
        for r in (7, 6, 5, 4, 3, 2, 1, 0):
            cf = cf * follow
            cd = cd * follow + d[r : r + 1]
            cfs[r], cds[r] = cf, cd
            follow = f[r : r + 1]
        cb[pl.ds(base, 8)] = jnp.concatenate(cfs, axis=0)
        al[pl.ds(base, 8)] = jnp.concatenate(cds, axis=0)
        return follow, cf, cd

    zero = jnp.zeros((1, rec), F32)
    follow, cf, cd = lax.fori_loop(0, count // 8, group, (zero + 1.0, zero + 1.0, zero))
    prefix = Prefix(slots, small_send, small_recv)
    prefix.start((follow * cf, follow * cd), True)
    weight_grad(dw_gate, normed_ref, gate_low_ref)
    each(late, "begin", 0)
    prefix.step()
    each(early, "middle")
    prefix.step()
    for load in loads[1:]:
        load.wait()
    later = prefix.step()[1]
    al[...] = al[...] + cb[...] * later

    def grads_step(n, carry):
        at = lanes(n)
        adjoint = al[:, at]
        factors, reset, gated = f_ref[:, at], reset_v[:, at], input_v[:, at]
        mixed_low = mixed_v[:, at]
        mixed = mixed_low.astype(F32)
        rates = v_ref[RATES : RATES + 1, at]
        log_decay = -8.0 * rates * reset
        decays = jnp.exp(log_decay)
        scale_in = jnp.sqrt(minus_expm1(2.0 * log_decay))
        grad_log = adjoint * states_ref[pl.ds(7, count), at] * factors
        grad_log = grad_log - adjoint * gated * mixed * decays * decays / scale_in
        small_ref[G_LAM : G_LAM + 1, at] = (
            8.0 * jnp.sum(grad_log * reset, axis=0, keepdims=True) * v_ref[SLOPE : SLOPE + 1, at]
        )
        small_ref[G_H : G_H + 1, at] = is_first * factors[0:1] * adjoint[0:1]
        grad_reset = (grad_log * (-8.0 * rates) * reset * (1.0 - reset)).astype(BF16)
        grad_input = (adjoint * scale_in * mixed * gated * (1.0 - gated)).astype(BF16)
        for g, grad in enumerate((grad_reset, grad_input)):
            small_ref[G_BIAS + g : G_BIAS + g + 1, at] = jnp.sum(
                grad.astype(F32), axis=0, keepdims=True
            )
            b = g * blocks + n
            rows = pl.ds(pl.multiple_of(16 * lax.rem(b, 3), 16), 16)
            gg_ref[:, :, b // 3, rows, :] = outer(mixed_low, grad).astype(BF16).reshape(4, 4, 16, BLOCK)
        grad_mixed = adjoint * scale_in * gated
        grad_mixed = grad_mixed + dot_t(grad_reset, g_v[0, n]) + dot_t(grad_input, g_v[1, n])
        gm[0:8] = jnp.zeros((8, BLOCK), F32)
        gm[8 : 8 + count] = grad_mixed
        gm[8 + count :] = jnp.zeros((8, BLOCK), F32)
        small_ref[G_CONV_B : G_CONV_B + 1, at] = jnp.sum(grad_mixed, axis=0, keepdims=True)
        total = jnp.zeros((count, BLOCK), F32)
        front = jnp.zeros((8, BLOCK), F32)
        for k in range(CONV):
            small_ref[G_CONV_W + k : G_CONV_W + k + 1, at] = jnp.sum(
                grad_mixed * ext[pl.ds(16 - EDGE + k, count), at], axis=0, keepdims=True
            )
            weight = v_ref[CONV_W + k : CONV_W + k + 1, at]
            total = total + weight * gm[pl.ds(8 + EDGE - k, count)]
            front = front + weight * gm[pl.ds(8 - k, 8)]
        low_ref[:, at] = total.astype(BF16)
        tail[:, at] = total[count - 16 :]
        edge[:, at] = front
        small_ref[G_STATE : G_STATE + EDGE, at] = is_first * front[:EDGE]
        small_ref[G_STATE + EDGE :, at] = jnp.zeros((16 - G_STATE - EDGE, BLOCK), F32)
        return carry

    for x, j in ((3, 1), (3, 2)):
        gg_ref[:, :, x, 16 * j : 16 * j + 16, :] = jnp.zeros((4, 4, 16, BLOCK), BF16)
    lax.fori_loop(0, 2, grads_step, 0)
    each(early, "finish")
    each(early, "begin", 1)
    each(late, "middle")
    lax.fori_loop(2, 4, grads_step, 0)
    each(early, "finish")
    each(early, "begin", 2)
    lax.fori_loop(4, blocks, grads_step, 0)
    edge_copy = push(edge, edge_in, edge_sem.at[0], edge_sem.at[1], behind)
    edge_copy.start()
    each(gates, "begin", 0)
    each(late, "finish")
    each(late, "begin", 1)
    each(early, "finish")
    edge_copy.wait_recv()
    last = jnp.concatenate([tail[0:13], tail[13:16] + has_next * edge_in[0:EDGE]], axis=0)
    low_ref[count - 16 :] = last.astype(BF16)
    each(gates, "finish")
    each(gates, "begin", 1)
    each(late, "finish")
    each(late, "begin", 2)
    each(gates, "finish")
    each(gates, "begin", 2)
    each(late, "finish")
    each(gates, "finish")
    each(flows, "drain")
    prefix.drain()
    edge_copy.wait_send()


def rec_back(gh, branch, normed, gate_lin, states_ext, factors, vectors, w_back, ext, mixed, reset, gated, gates, cid):
    count, rec = gate_lin.shape
    blocks = rec // BLOCK
    rows = normed.shape[1] // 64

    def like(array):
        return pltpu.VMEM(array.shape, array.dtype)

    wide = pltpu.VMEM((count, rec), F32)
    cube = pltpu.VMEM((4, 4, 4, rows, rec), BF16)
    bufs = []
    for e in range(6):
        width = CHUNKS[e % 3][1]
        bufs += scatter_buffers(rows, width, (rows // 2, width))
    for _ in range(2):
        bufs += scatter_buffers(GATE_ROWS, BLOCK // 2, None)
    out = pl.pallas_call(
        rec_back_kernel,
        out_shape=[
            jax.ShapeDtypeStruct((count, rec), BF16),
            jax.ShapeDtypeStruct((count, rec), BF16),
            jax.ShapeDtypeStruct((16, rec), F32),
        ]
        + [jax.ShapeDtypeStruct((rows, CHUNKS[e % 3][1]), F32) for e in range(6)]
        + [jax.ShapeDtypeStruct((GATE_ROWS, BLOCK // 2), F32)] * 2,
        in_specs=[VM] * 7 + [ANY] * 6,
        out_specs=[VM] * 11,
        scratch_shapes=[
            like(w_back), like(ext), like(mixed), like(reset), like(gated), like(gates),
            wide, wide, wide, pltpu.VMEM((count + 16, BLOCK), F32), cube, cube,
            pltpu.VMEM((16, rec), F32), pltpu.VMEM((8, rec), F32), pltpu.VMEM((8, rec), F32),
            pltpu.VMEM((4, 4, 4, GATE_ROWS, BLOCK), BF16),
        ]
        + bufs
        + [
            pltpu.VMEM((3, 4, 2, rec), F32),
            DMA((6,)),
            DMA((8, 3, 3, 3)),
            DMA((8, 3, 3, 3)),
            DMA((1, 3, 3)),
            DMA((1, 3, 3)),
            DMA((2,)),
        ],
        compiler_params=params(cid, 62),
    )(gh, branch, normed, gate_lin, states_ext, factors, vectors, w_back, ext, mixed, reset, gated, gates)
    gates = jnp.concatenate(out[9:11], axis=1)
    return out[:3], jnp.concatenate(out[3:6], axis=1), jnp.concatenate(out[6:9], axis=1), gates


def rec_end_kernel(*refs):
    (
        gate_low_ref, low_ref, normed_ref, gg_ref, small_ref, gain_term_ref, gh_ref, tokens_in, inverse_ref, gain_ref,
        quarters_ref, wg_hbm, wl_hbm,
        tokens_ref, total_ref, gains_ref, all_gates_ref, grad_mlp_ref, grad_down_ref, out0, out1, out2,
        wg, wl, dw_lin, part, part_low, part_in, gates_ref, back, ring_gains, gains0, small0, small1, small2,
    ) = refs[:35]
    bufs, refs = refs[35 : 35 + 18], refs[35 + 18 :]
    load_sem, send, recv, gsend, grecv, small_send, small_recv, ring_send, ring_recv, core_sem, token_sem, move_send, move_recv = refs
    half, width = gh_ref.shape
    loads = [
        pltpu.make_async_copy(wg_hbm, wg, load_sem.at[0]),
        pltpu.make_async_copy(wl_hbm, wl, load_sem.at[1]),
    ]
    for load in loads:
        load.start()
    core = lax.axis_index("mp")
    other = {"mp": 1 - core}
    x_here = lax.axis_index("x")
    greet(axis_peers() + [other] + [{"x": peer, "mp": 1 - core} for peer in ring("x")[1:]])
    small = [
        Total(slots, small_send, small_recv, e, ORDERS[e])
        for e, slots in enumerate((small0, small1, small2))
    ]
    for flow, (start, wide) in zip(small, CHUNKS):
        flow.start(small_ref[:, start : start + wide])
    moves = []
    for step, peer in enumerate(ring("x")[1:]):
        copy = push(quarters_ref.at[peer], back.at[x_here], move_send.at[step], move_recv.at[step], {"x": peer})
        copy.start()
        moves.append(copy)
    back[x_here] = quarters_ref[x_here]
    outs = (out0, out1, out2)
    lin = [
        Scatter(e, dw_lin, CHUNKS[e], ORDERS[e], ROW_CUTS, bufs[6 * e : 6 * e + 6], outs[e], send, recv)
        for e in range(3)
    ]
    spread = [Gather(e, gates_ref, ORDERS[e], HALVES[e], gsend, grecv) for e in range(2)]

    def each_gate(name, *args):
        for flow in spread:
            getattr(flow, name)(*args)

    def each(name, *args):
        for flow in lin:
            getattr(flow, name)(*args)

    gates_ref[lax.axis_index("z"), lax.axis_index("y"), lax.axis_index("x")] = gg_ref[...].astype(BF16)

    def weight_grad(i, carry):
        cols = pl.ds(pl.multiple_of(i * 256, 256), 256)
        shard_rows(dw_lin, i, outer(normed_ref[:, cols], low_ref[...]).astype(BF16))
        return carry

    lax.fori_loop(0, width // 512, weight_grad, 0)
    for flow in small:
        flow.step()
    lax.fori_loop(width // 512, width // 256, weight_grad, 0)
    for flow in small:
        flow.step()
    each_gate("begin", 0)
    each("begin", 0)
    for load in loads:
        load.wait()

    def part_tile(i, carry):
        at = pl.ds(pl.multiple_of(i * 256, 256), 256)
        value = dot_t(gate_low_ref[...], wg[at, :]) + dot_t(low_ref[...], wl[at, :])
        part[0, :, at] = value[:half]
        part[1, :, at] = value[half:]
        return carry

    lax.fori_loop(0, width // 256, part_tile, 0)
    part_low[...] = part[1 - core].astype(BF16)
    part_copy = push(part_low, part_in, core_sem.at[0], core_sem.at[1], other)
    part_copy.start()
    for flow, (start, wide) in zip(small, CHUNKS):
        total_ref[:, start : start + wide] = flow.step()
    each_gate("finish")
    each_gate("begin", 1)
    part_copy.wait_recv()
    grad_normed = part[core] + part_in[...].astype(F32)
    hat = tokens_in[...].astype(F32) * inverse_ref[...]
    gain_term = jnp.sum(grad_normed * hat, axis=0, keepdims=True)
    quarter = width // 4
    for k in range(4):
        cols = slice(k * quarter, (k + 1) * quarter)
        ring_gains[x_here, core, k : k + 1] = gain_term[:, cols]
        ring_gains[x_here, core, 4 + k : 5 + k] = gain_term_ref[:, cols]
    shares = []
    spot = ring_gains.at[x_here, core]
    group = [{"x": x, "mp": c} for x in ring("x") for c in (core, 1 - core)][1:]
    for k, peer in enumerate(group):
        copy = push(spot, spot, ring_send.at[k], ring_recv.at[k], peer)
        copy.start()
        shares.append(copy)
    grad_hat = grad_normed * gain_ref[...]
    inner = jnp.mean(grad_hat * hat, axis=-1, keepdims=True)
    part[core] = gh_ref[...] + inverse_ref[...] * (grad_hat - hat * inner)
    token_copy = push(part.at[core], tokens_ref.at[core], token_sem.at[0], token_sem.at[1], other)
    token_copy.start()
    tokens_ref[core] = part[core]
    each("middle")
    for copy in shares:
        copy.wait_recv()
    gains = Total(gains0, small_send, small_recv, 3, ("y", "z"))
    sums = [ring_gains[x, 0] + ring_gains[x, 1] for x in range(4)]
    gains.start((sums[0] + sums[1]) + (sums[2] + sums[3]))
    each_gate("finish")
    each_gate("begin", 2)
    for copy in moves:
        copy.wait_recv()
    quarter = grad_down_ref.shape[1] // 4
    for q in range(4):
        value = back[q].astype(F32)
        for k in range(2):
            grad_mlp_ref[:, pl.ds((4 * k + q) * quarter, quarter)] = value[:, k * quarter : (k + 1) * quarter]
        grad_down_ref[:, pl.ds(q * quarter, quarter)] = value[:, 2 * quarter :]
    gains.step()
    each("finish")
    each("begin", 1)
    gains_ref[...] = gains.step()
    each_gate("finish")

    def unpack(b, carry):
        at = pl.ds(pl.multiple_of(16 * lax.rem(b, 3), 16), 16)
        all_gates_ref[b] = gates_ref[:, :, b // 3, at, :].reshape(BLOCK, BLOCK).astype(F32)
        return carry

    lax.fori_loop(0, all_gates_ref.shape[0], unpack, 0)
    each("finish")
    each("begin", 2)
    token_copy.wait_recv()
    each("finish")
    each("drain")
    each_gate("drain")
    gains.drain()
    for flow in small:
        flow.drain()
    for copy in shares + moves + [part_copy, token_copy]:
        copy.wait_send()


def rec_end(gate_low, low, normed, gg, small, gain_term, grad_hidden, tokens, inverse, gain, quarters, w_gate, w_lin, cid):
    count, rec = low.shape
    half, width = grad_hidden.shape
    rows = width // 64
    units = quarters.shape[2] // 3
    gate_blocks = 2 * rec // BLOCK
    bufs = []
    for e in range(3):
        bufs += scatter_buffers(rows, CHUNKS[e][1], (rows // 2, CHUNKS[e][1]))

    def sds(*shape):
        return jax.ShapeDtypeStruct(shape, F32)

    out = pl.pallas_call(
        rec_end_kernel,
        out_shape=[
            sds(2, half, width),
            sds(16, rec),
            sds(8, width // 4),
            sds(gate_blocks, BLOCK, BLOCK),
            sds(rows, 8 * units),
            sds(rows, 4 * units),
        ]
        + [sds(rows, CHUNKS[e][1]) for e in range(3)],
        in_specs=[VM] * 11 + [ANY] * 2,
        out_specs=[VM] * 9,
        scratch_shapes=[
            pltpu.VMEM(w_gate.shape, BF16),
            pltpu.VMEM(w_lin.shape, BF16),
            pltpu.VMEM((4, 4, 4, rows, rec), BF16),
            pltpu.VMEM((2, half, width), F32),
            pltpu.VMEM((half, width), BF16),
            pltpu.VMEM((half, width), BF16),
            pltpu.VMEM((4, 4, 4) + gg.shape, BF16),
            pltpu.VMEM(quarters.shape, quarters.dtype),
            pltpu.VMEM((4, 2, 8, width // 4), F32),
            pltpu.VMEM((2, 4, 8, width // 4), F32),
        ]
        + [pltpu.VMEM((3, 4, 16, wide), F32) for _, wide in CHUNKS]
        + bufs
        + [
            DMA((2,)),
            DMA((3, 3, 3, 3)),
            DMA((3, 3, 3, 3)),
            DMA((2, 3, 1, 3)),
            DMA((2, 3, 1, 3)),
            DMA((4, 3, 3)),
            DMA((4, 3, 3)),
            DMA((7,)),
            DMA((7,)),
            DMA((2,)),
            DMA((2,)),
            DMA((3,)),
            DMA((3,)),
        ],
        compiler_params=params(cid, 60),
    )(gate_low, low, normed, gg, small, gain_term, grad_hidden, tokens, inverse, gain, quarters, w_gate, w_lin)
    return (out[0].reshape(2 * half, width),) + tuple(out[1:6]) + (jnp.concatenate(out[6:9], axis=1),)


def body(
    tokens,
    cotangent,
    starts,
    valid,
    w_rec,
    w_out,
    w_mlp,
    w_down,
    lru_gates,
    lru_bias,
    lam,
    conv_w,
    conv_b,
    gain_rec,
    gain_mlp,
    h_init,
    conv_state,
):
    count, width = tokens.shape
    shard, _, rec = w_rec.shape
    hidden_units = w_mlp.shape[2] // 4
    half = count // 2
    core = lax.axis_index("mp")

    def my_half(array):
        return lax.dynamic_slice_in_dim(array, core * half, half, axis=0)

    quarters = jnp.stack([w_mlp[:, 0], w_mlp[:, 1], w_down.T], axis=1)
    quarters = quarters.reshape(shard, 3, 4, hidden_units).transpose(2, 0, 1, 3)
    quarters = quarters.reshape(4, shard, 3 * hidden_units)
    grad_out = my_half(cotangent) * my_half(valid).astype(BF16)[:, None]
    grad_out_all = lax.all_gather(grad_out, ("x", "mp"), axis=0, tiled=True)
    vectors = jnp.concatenate(
        [
            conv_w,
            conv_b[None],
            jax.nn.softplus(-lam)[None],
            lru_bias,
            conv_state,
            h_init[None],
            jax.nn.sigmoid(-lam)[None],
            jnp.zeros((3, rec), F32),
        ],
        axis=0,
    )
    (
        w_lin, w_gate, w_back, mlp_weights, ext, gate_lin, mixed, reset, gated, factors, states_ext, branch_in,
        normed_rec, inverse_rec, rms_rec, hidden, normed_mlp, inverse_mlp, rms_half,
    ) = rec_forward(
        tokens,
        tokens[count - 16 :],
        gain_rec,
        gain_mlp,
        vectors,
        (1 - starts).astype(F32)[:, None],
        w_rec[:, 1],
        w_rec[:, 0],
        w_out.T,
        quarters,
        lru_gates,
        0,
    )
    w_lin, w_gate, w_back = (w.reshape(width, rec) for w in (w_lin, w_gate, w_back))
    result, grad_hidden, grad_hidden_low, gain_mlp_term, mlp_terms = mlp(
        normed_mlp, grad_out, hidden, inverse_mlp, gain_mlp[None], grad_out_all, mlp_weights, 1
    )
    mlp_sums = lax.psum_scatter(mlp_terms, ("z", "y"), scatter_dimension=0, tiled=True)
    result = result.reshape(count, width)
    grad_hidden_low = grad_hidden_low.reshape(count, width)
    (grad_gate_low, grad_rec_low, small), out_sums, gate_sums, gate_terms = rec_back(
        grad_hidden_low,
        branch_in,
        normed_rec,
        gate_lin,
        states_ext,
        factors,
        vectors,
        w_back,
        ext,
        mixed,
        reset,
        gated,
        lru_gates,
        2,
    )
    grad_tokens, small, gains, gate_blocks, grad_w_mlp, grad_down, lin_sums = rec_end(
        grad_gate_low,
        grad_rec_low,
        normed_rec,
        gate_terms,
        small,
        gain_mlp_term,
        grad_hidden,
        my_half(tokens),
        my_half(inverse_rec),
        gain_rec[None],
        mlp_sums.reshape(4, shard, 3 * hidden_units),
        w_gate,
        w_lin,
        3,
    )
    grad_w_rec = jnp.stack([gate_sums, lin_sums], axis=1)
    grad_w_out = out_sums.T
    grad_gates = gate_blocks.reshape(lru_gates.shape)
    grad_w_mlp = grad_w_mlp.reshape(shard, 2, 4 * hidden_units)
    grad_w_down = grad_down.T
    rms_mlp = rms_half[:, :, 0].reshape(count)
    gains = gains.reshape(2, width)
    return (
        result,
        rms_rec[:, 0],
        rms_mlp,
        grad_tokens,
        grad_w_rec,
        grad_w_out,
        grad_w_mlp,
        grad_w_down,
        grad_gates,
        small[G_BIAS : G_BIAS + 2],
        small[G_LAM],
        small[G_CONV_W : G_CONV_W + CONV],
        small[G_CONV_B],
        gains[0],
        gains[1],
        small[G_H],
        small[G_STATE : G_STATE + EDGE],
    )


def solution(mesh):
    cube = Mesh(mesh.devices.reshape(4, 4, 4, 2), ("z", "y", "x", "mp"))
    placed = (
        P(SEQ, None),
        P(SEQ, None),
        P(SEQ),
        P(SEQ),
        P(SEQ, None, "mp"),
        P("mp", SEQ),
        P(SEQ, None, "mp"),
        P("mp", SEQ),
        P(None, "mp", None, None),
        P(None, "mp"),
        P("mp"),
        P(None, "mp"),
        P("mp"),
        P(),
        P(),
        P("mp"),
        P(None, "mp"),
    )
    return jax.shard_map(
        body,
        mesh=cube,
        in_specs=placed,
        out_specs=(
            P(SEQ, None),
            P(SEQ),
            P(SEQ),
            P(SEQ, None),
            P(SEQ, None, "mp"),
            P("mp", SEQ),
            P(SEQ, None, "mp"),
            P("mp", SEQ),
            P(None, "mp", None, None),
            P(None, "mp"),
            P("mp"),
            P(None, "mp"),
            P("mp"),
            P(),
            P(),
            P("mp"),
            P(None, "mp"),
        ),
        check_vma=False,
    )
```

time: 2370 us -> 463 us (0.20)
  waiting for transfers between devices: 840 us -> 0.08 us
  blocking collectives: 697 us -> 0 us
  local copies, waits for them, and re-layouts: 442 us -> 27.8 us
  Pallas kernels: 0 us -> 410 us
  other arithmetic: 201 us -> 9.71 us
  matrix products: 141 us -> 0 us
    all_gather x4 -> x0, blocking collectives: 697 us -> none  [carried_in(): pieces = jax.tree.map(lambda part: lax.all_gather(part, axis), value)]
    reduce_scatter x1, waiting for transfers between devices: 417 us -> 0.02 us  [body(): lax.psum_scatter(mlp_terms, ('z', 'y'), scatter_dimension=0, tiled=True)]
    pallas_call x0 -> x4, Pallas kernels: none -> 410 us  [the longest x1 138 us: rec_forward(): pl.pallas_call(rec_forward_kernel, out_shape=[sds(*one) for one in saved...]
    all_gather x4 -> x1, waiting for transfers between devices: 251 us -> 0.02 us  [body(): grad_out_all = lax.all_gather(grad_out, ('x', 'mp'), axis=0, tiled=True)]
    psum x5 -> x0, waiting for transfers between devices: 165 us -> none  [the longest x2 150 us: body(): lax.psum((grad_gates, grad_bias, grad_lam, grad_conv_w, conv_bias_gradien...]
    slice x115 -> x7, local copies, waits for them, and re-layouts: 156 us -> 8.09 us  [the longest x1 1.56 us: body(): small[G_H]]
    dot_general x15 -> x0, matrix products: 141 us -> none  [the longest x4 52.9 us: make_terms(): lax.dot_general(left_side, right_side, (((0,), (0,)), ((), ())), preferre...]
    pad x56 -> x0, local copies, waits for them, and re-layouts: 88.5 us -> none  [linear_recurrence_scan(): lax.associative_scan(merge_pairs, (decay_multipliers, scan_increments), a...]
  transfers between devices with their start and end apart: 12 -> 2, of which waited for: 9 -> 0; matrix products, arithmetic and copies ran while one was open for 17% -> 4% of each run, Pallas kernels for 0% -> 55%
where the time goes in v2:
time: 463 us; the launch traced here: 462 us
  Pallas kernels  410 us (89%)
  local copies, waits for them, and re-layouts  27.8 us (6%)
  between operations  14.3 us (3%)
  other arithmetic  9.71 us (2%)
    pallas_call x1, Pallas kernels, rec_forward(): pl.pallas_call(rec_forward_kernel, out_shape=[sds(*one) for one in saved...  138 us
    pallas_call x1, Pallas kernels, rec_back(): pl.pallas_call(rec_back_kernel, out_shape=[jax.ShapeDtypeStruct((count, r...  117 us
    pallas_call x1, Pallas kernels, mlp(): pl.pallas_call(mlp_kernel, out_shape=[jax.ShapeDtypeStruct((2, rows, widt...  95.1 us
    pallas_call x1, Pallas kernels, rec_end(): pl.pallas_call(rec_end_kernel, out_shape=[sds(2, half, width), sds(16, re...  59.6 us
  transfers between devices with their start and end apart: 2, of which 0 were waited for; matrix products, arithmetic and copies ran while one was open for 4% of the time, Pallas kernels for 55%

profile of v2, /device:TPU:0, one launch (start us, length us, event | category | flops | bytes accessed | tf_op | source)
XLA Modules:
  0.0 461.9 jit_solution(15016289998996256249)
XLA Ops:
  7.2 0.0 copy-start.5
  7.2 0.0 all-gather.2.cloned.1.call-start
  7.2 0.8 dynamic-slice_convert_fusion
  8.0 2.0 dynamic-slice_multiply_fusion.go_ref
  10.0 0.0 all-gather.2.cloned.1.call-update
  10.1 0.0 reduce-scatter.2.cloned.1.call-start
  10.1 0.7 add_divide_fusion
  10.9 0.7 broadcast_in_dim.29
  11.6 0.7 broadcast_in_dim.31
  12.3 1.1 stack.19
  13.3 0.0 copy-start.14
  13.3 0.3 copy.42
  13.7 0.0 copy-start.10
  13.7 0.0 copy-start.11
  13.7 0.0 copy-start.13
  13.7 0.0 copy-done.5
  13.7 0.0 copy-start.4
  13.7 0.3 copy.53
  14.0 0.8 maximum_bitcast_fusion
  14.8 1.4 reshape.74.refs_9_
  16.2 0.0 copy-done.14
  16.2 0.8 copy.43.refs_5_
  17.0 1.5 slice.41.refs_1_
  18.5 0.0 copy-done.10
  18.5 0.0 copy-done.11
  18.5 0.0 copy-done.13
  18.5 1.3 concatenate.16.refs_4_.refs_6_
  19.8 0.0 copy-done.4
  19.8 0.2 fusion
  20.1 0.7 copy_bitcast_fusion.1
  20.8 138.5 %shard_map.296 = (bf16[4,4,4,32,1280]{4,3,2,1,0:T(8,128)(2,1)}, bf16[4,4,4,32,1280]{4,3,2,1,0:T(8,128)(2,1)}, bf16[4,4,4,32,1280]{4,3,2,1,0:T(8,128)(2,1)}, bf16...) custom-call(bf16[256,2048]{1,0:T(8,128)(2,1)} %refs_0_.1, ...), custom_call_target="tpu_custom_call" | custom-call | tf_op jit(solution)/shard_map/pallas_call | solution.py:834
  159.2 0.0 all-gather.2.cloned.1.call-done.go_hbm
  159.3 95.1 %shard_map.297 = (bf16[2,128,2048]{2,1,0:T(8,128)(2,1)}, f32[128,2048]{1,0:T(8,128)}, bf16[2,128,2048]{2,1,0:T(8,128)(2,1)}, f32[1,2048]{1,0:T(1,128)}, bf16[2048,2304]{1,0:T(8,128)(2,1)}) custom-call(bf16[128,2048]{1,0:T(8,128)(2,1)} %get-tuple-element.61.nm_ref, bf16[128,2048]{1,0:T(8,128)(2,1)} %dynamic-slice_multiply_fusion.go_ref, ...), custom_call_target="tpu_custom_call" | custom-call | tf_op jit(solution)/shard_map/pallas_call | solution.py:543
  254.4 0.0 copy-start.8
  254.4 0.0 copy-start.9
  254.4 0.0 copy-start.7
  254.4 0.0 copy-start.1
  254.4 0.0 reduce-scatter.2.cloned.1.call-update
  254.5 0.8 copy-done.8
  255.3 0.7 reduce
  256.0 0.0 copy-done.9
  256.0 0.6 constant_dynamic-slice_fusion.refs_8_
  256.6 0.7 slice_reduce_fusion
  257.3 0.8 constant_dynamic-slice_fusion.1.refs_7_
  258.1 116.8 %shard_map.298 = (bf16[256,1280]{1,0:T(8,128)(2,1)}, bf16[256,1280]{1,0:T(8,128)(2,1)}, f32[16,1280]{1,0:T(8,128)}, f32[32,384]{1,0:T(8,128)}, f32[32,512]{1,0:T...) custom-call(bf16[256,2048]{1,0:T(8,128)(2,1)} %bitcast.43, ...), custom_call_target="tpu_custom_call" | custom-call | tf_op jit(solution)/shard_map/pallas_call | solution.py:1050
  374.9 1.4 pad_maximum_fusion.1.refs_3_
  376.3 1.5 maximum_bitcast_fusion.3
  377.9 0.9 maximum_bitcast_fusion.1
  378.7 0.0 reduce-scatter.2.cloned.1.call-done
  378.8 59.6 %shard_map.299 = (f32[2,128,2048]{2,1,0:T(8,128)}, f32[16,1280]{1,0:T(8,128)}, f32[8,512]{1,0:T(8,128)}, f32[10,256,256]{2,1,0:T(8,128)}, f32[32,6144]{1,0:T(8,1...) custom-call(bf16[256,1280]{1,0:T(8,128)(2,1)} %get-tuple-element.79.refs_0_, ...), custom_call_target="tpu_custom_call" | custom-call | tf_op jit(solution)/shard_map/pallas_call | solution.py:1239
  438.3 1.6 slice_reduce_fusion.1
  439.9 1.4 slice.47
  441.3 1.4 slice.52
  442.7 1.4 slice.45
  444.1 0.9 maximum_bitcast_fusion.2
  445.0 1.0 copy.44
  446.0 2.7 reshape.82
  448.6 0.6 copy.48
  449.2 0.6 copy.49
  449.9 1.0 copy.58
  450.8 1.3 copy.59
  452.2 0.7 copy.60
  452.9 0.7 copy-done
  453.6 1.5 copy.61
  (17 shorter events, 0.1 us)
Async XLA Ops:
  7.2 6.5 %copy-start.5 = (bf16[32,2,3072]{2,1,0:T(2,128)(2,1)S(1)}, bf16[32,2,3072]{2,1,0:T(2,128)(2,1)}, u32[]{:S(2)}) copy-start(bf16[32,2,3072]{2,1,0:T(2,128)(2,1)} %param.23) | copy-start | bytes 1179652
  7.2 152.1 %all-gather.2.cloned.1.call-start = ((), (), s32[]{:S(2)}) async-start(), calls=%async_computation.1 | async-start | bytes 4718592 | tf_op jit(solution)/shard_map/all_gather | solution.py:1318
  10.1 368.7 %reduce-scatter.2.cloned.1.call-start = ((), (), s32[]{:S(2)}) async-start(), calls=%async_computation.2 | async-start | bytes 10027008 | tf_op jit(solution)/shard_map/reduce_scatter | solution.py:1353
  13.3 2.9 copy-start.14
  13.7 4.9 %copy-start.10 = (f32[4,1280]{1,0:T(4,128)S(1)}, f32[4,1280]{1,0:T(4,128)}, u32[]{:S(2)}) copy-start(f32[4,1280]{1,0:T(4,128)} %param.28) | copy-start | bytes 61444
  13.7 4.9 %copy-start.11 = (f32[3,1280]{1,0:T(4,128)S(1)}, f32[3,1280]{1,0:T(4,128)}, u32[]{:S(2)}) copy-start(f32[3,1280]{1,0:T(4,128)} %param.33) | copy-start | bytes 46084
  13.7 4.8 %copy-start.13 = (f32[2,1280]{1,0:T(2,128)S(1)}, f32[2,1280]{1,0:T(2,128)}, u32[]{:S(2)}) copy-start(f32[2,1280]{1,0:T(2,128)} %param.26) | copy-start | bytes 30724
  13.7 6.1 %copy-start.4 = (bf16[32,2,1280]{2,1,0:T(2,128)(2,1)S(1)}, bf16[32,2,1280]{2,1,0:T(2,128)(2,1)}, u32[]{:S(2)}) copy-start(bf16[32,2,1280]{2,1,0:T(2,128)(2,1)} %param.21) | copy-start | bytes 491524
  254.4 0.9 copy-start.8
  254.4 1.6 copy-start.9
  254.4 2.2 copy-start.7
  254.4 2.9 copy-start.1
  438.3 10.3 %copy-start.12 = (f32[8,512]{1,0:T(8,128)S(1)}, f32[8,512]{1,0:T(8,128)}, u32[]{:S(2)}) copy-start(f32[8,512]{1,0:T(8,128)} %get-tuple-element.104) | copy-start | bytes 49156
  438.3 11.5 %copy-start.3 = (bf16[2,128,2048]{2,1,0:T(8,128)(2,1)S(1)}, bf16[2,128,2048]{2,1,0:T(8,128)(2,1)}, u32[]{:S(2)}) copy-start(bf16[2,128,2048]{2,1,0:T(8,128)(2,1)} %get-tuple-element.65) | copy-start | bytes 3145732
  445.0 5.9 %copy-start.2 = (f32[2,128,2048]{2,1,0:T(8,128)S(1)}, f32[2,128,2048]{2,1,0:T(8,128)}, u32[]{:S(2)}) copy-start(f32[2,128,2048]{2,1,0:T(8,128)} %get-tuple-element.90) | copy-start | bytes 6291460
  450.8 1.3 copy-start.6
  450.8 2.8 copy-start
Sparse Core Ops, SparseCore 0:
  10.3 47.9 all-gather.1
  254.6 115.6 reduce-scatter.1

commit v3 on v2

v3 whole, which is shorter than its diff:
```python
import functools
import jax
import jax.numpy as jnp
from jax import lax
from jax.experimental import pallas as pl
from jax.experimental.pallas import tpu as pltpu
from jax.sharding import Mesh, PartitionSpec as P

CONV = 4
EDGE = CONV - 1
BLOCK = 256
EPSILON = 1e-06
MESH = pl.DeviceIdType.MESH
ANY = pl.BlockSpec(memory_space=pl.ANY)
HBM = pl.BlockSpec(memory_space=pltpu.HBM)
VM = pl.BlockSpec(memory_space=pltpu.VMEM)
MIB = 1024 * 1024
AXES = ("z", "y", "x")
SEQ = ("z", "y", "x")
ORDERS = (("x", "y", "z"), ("y", "z", "x"), ("z", "x", "y"))
F32, BF16 = jnp.float32, jnp.bfloat16
GELU_C, GELU_A = 0.7978845608028654, 0.044715
DMA = pltpu.SemaphoreType.DMA


def dot(left, right):
    return jnp.dot(left, right, preferred_element_type=F32)


def dot_t(left, right):
    return lax.dot_general(left, right, (((1,), (1,)), ((), ())), preferred_element_type=F32)


def outer(left, right):
    return lax.dot_general(left, right, (((0,), (0,)), ((), ())), preferred_element_type=F32)


def greet(peers):
    sem = pltpu.get_barrier_semaphore()
    for peer in peers:
        pl.semaphore_signal(sem, inc=1, device_id=peer, device_id_type=MESH)
    pl.semaphore_wait(sem, len(peers))


def push(src, dst, send, recv, peer):
    return pltpu.make_async_remote_copy(
        src_ref=src, dst_ref=dst, send_sem=send, recv_sem=recv, device_id=peer, device_id_type=MESH
    )


def ring(axis):
    me = lax.axis_index(axis)
    return me, lax.rem(me + 1, 4), lax.rem(me + 2, 4), lax.rem(me + 3, 4)


def all_neighbours():
    peers = []
    for axis in AXES:
        _, up, _, down = ring(axis)
        peers += [{axis: up}, {axis: down}]
    return peers


def params(cid, mib):
    return pltpu.CompilerParams(
        collective_id=cid, has_side_effects=True, vmem_limit_bytes=mib * MIB
    )


def part_of(done, axis, index, rows, cols):
    spot = []
    for name in AXES:
        if name in done:
            spot.append(pl.ds(0, 4))
        elif name == axis:
            spot.append(index)
        else:
            spot.append(lax.axis_index(name))
    return tuple(spot) + (rows, cols)


def pick(names, axis, index, others):
    spot, rest = [], iter(others)
    for name in names:
        spot.append(index if name == axis else next(rest))
    return tuple(spot)


class Scatter:
    def __init__(self, entry, src, cols, order, halves, bufs, out, own_sem, send, recv, band=None):
        self.band, self.band_rows = band, src.shape[-2] if band is None else band[1]
        self.entry, self.src, self.order = entry, src, order
        self.start, self.width = cols
        self.halves, self.bufs, self.out = halves, list(bufs), out
        self.own_sem, self.send, self.recv = own_sem, send, recv
        self.left, self.sent = AXES, []

    def view(self, at, rows=None):
        if rows is None:
            first = self.band[0] if self.band is not None and self.phase == 0 else 0
            rows = pl.ds(first, self.band_rows)
        return at + (rows, pl.ds(self.start if self.phase == 0 else 0, self.width))

    def spread(self, i):
        return ((i // 4, lax.rem(i, 4)), (i,), ())[self.phase]

    def copy(self, src, dst, way, kind, peer):
        at = (self.entry, self.phase, way, kind)
        copy = push(src, dst, self.send.at[at], self.recv.at[at], {self.axis: peer})
        copy.start()
        self.sent.append(copy)
        return copy

    def load(self, index, dst, rows=None):
        src = self.src.at[self.view(pick(self.left, self.axis, index, self.full), rows)]
        copy = pltpu.make_async_copy(src, dst, self.own_sem.at[self.entry, len(self.loads)])
        copy.start()
        self.loads.append(copy)

    def begin(self, phase):
        self.phase, self.axis = phase, self.order[phase]
        self.full = (pl.ds(0, 4),) * (2 - phase)
        me, up, far, down = ring(self.axis)
        self.first, self.second, self.loads = [], [], []
        self.two_step = phase == 0 and self.halves is not None
        if self.two_step:
            self.ones, self.twos, self.near = self.bufs.pop(0), self.bufs.pop(0), self.bufs.pop(0)
            for way, peer in enumerate((up, down)):
                half = self.halves[way]
                src = self.src.at[self.view(pick(self.left, self.axis, far, self.full), half)]
                self.first.append(self.copy(src, self.ones.at[way], way, 0, peer))
            for way, peer in enumerate((up, down)):
                half = self.halves[1 - way]
                src = self.src.at[self.view(pick(self.left, self.axis, peer, self.full), half)]
                dst = self.twos.at[(way,) + self.full + (half,)]
                self.second.append(self.copy(src, dst, way, 1, peer))
            for way, peer in enumerate((up, down)):
                self.load(peer, self.near.at[way], self.halves[way])
        else:
            self.threes = self.bufs.pop(0)
            for step, peer in enumerate((up, far, down)):
                src = self.src.at[self.view(pick(self.left, self.axis, peer, self.full))]
                self.second.append(self.copy(src, self.threes.at[step], step, 0, peer))
        if phase == 0:
            self.own = self.bufs.pop(0)
            self.load(me, self.own)
        self.acc = self.bufs.pop(0) if phase < 2 else self.out

    def middle(self):
        _, up, _, down = ring(self.axis)
        for way, peer in enumerate((up, down)):
            self.first[way].wait_recv()
            self.loads[way].wait()

            def add(i, carry, way=way):
                there = (way,) + self.spread(i)
                total = self.ones[there].astype(F32) + self.near[there].astype(F32)
                self.ones[there] = total.astype(BF16)
                return carry

            lax.fori_loop(0, 16, add, 0)
            dst = self.twos.at[(way,) + self.full + (self.halves[way],)]
            self.second.append(self.copy(self.ones.at[way], dst, way, 2, peer))

    def finish(self):
        me = lax.axis_index(self.axis)
        for copy in self.second:
            copy.wait_recv()
        if self.phase == 0:
            self.loads[-1].wait()
        buf, slots = (self.twos, (0, 1)) if self.two_step else (self.threes, (0, 1, 2))

        def total(i, carry):
            there = self.spread(i)
            if self.phase == 0:
                whole = self.own[there].astype(F32)
            else:
                whole = self.src[self.view(pick(self.left, self.axis, me, there))].astype(F32)
            for slot in slots:
                whole = whole + buf[(slot,) + there].astype(F32)
            if self.phase < 2:
                self.acc[there] = whole.astype(self.acc.dtype)
            else:
                first = 0 if self.band is None else self.band[0]
                self.acc[pl.ds(first, self.band_rows), pl.ds(self.start, self.width)] = whole
            return carry

        lax.fori_loop(0, 4 ** (2 - self.phase), total, 0)
        self.src = self.acc
        self.left = tuple(name for name in self.left if name != self.axis)

    def drain(self):
        for copy in self.sent:
            copy.wait_send()


def scatter_buffers(rows, width, halved):
    bufs = []
    for phase in range(3):
        cube = (4,) * (2 - phase)
        if phase == 0 and halved:
            bufs.append(pltpu.VMEM((2,) + cube + (rows // 2, width), BF16))
            bufs.append(pltpu.VMEM((2,) + cube + (rows, width), BF16))
            bufs.append(pltpu.VMEM((2,) + cube + (rows // 2, width), BF16))
        else:
            bufs.append(pltpu.VMEM((3,) + cube + (rows, width), BF16))
        if phase == 0:
            bufs.append(pltpu.VMEM(cube + (rows, width), BF16))
        if phase < 2:
            bufs.append(pltpu.VMEM(cube + (rows, width), BF16))
    return bufs


class Gather:
    def __init__(self, entry, out, order, cols, send, recv, done=(), ring_rounds=(), band=None):
        self.band = (0, out.shape[3]) if band is None else band
        self.entry, self.out, self.order, self.cols = entry, out, order, pl.ds(*cols)
        self.send, self.recv, self.sent = send, recv, []
        self.done, self.ring_rounds = done, ring_rounds

    def spot(self, origin, rows=None):
        rows = pl.ds(*self.band) if rows is None else rows
        return self.out.at[part_of(self.done, self.axis, origin, rows, self.cols)]

    def copy(self, src, dst, step, way, peer):
        at = (self.entry, self.phase, step, way)
        copy = push(src, dst, self.send.at[at], self.recv.at[at], {self.axis: peer})
        copy.start()
        self.sent.append(copy)
        return copy

    def begin(self, phase, src=None):
        self.phase, self.axis = phase, self.order[phase]
        me, up, far, down = ring(self.axis)
        here = self.spot(me)
        src = here if src is None else src.at[:, self.cols]
        peers = (up, down) if phase in self.ring_rounds else (up, far, down)
        self.copies = [self.copy(src, here, 0, way, peer) for way, peer in enumerate(peers)]

    def middle(self):
        _, up, _, down = ring(self.axis)
        half = self.out.shape[3] // 2
        first, self.copies = self.copies, []
        for way, (peer, origin) in enumerate(((up, down), (down, up))):
            first[way].wait_recv()
            spot = self.spot(origin, pl.ds(way * half, half))
            self.copies.append(self.copy(spot, spot, 1, way, peer))

    def hold(self):
        for copy in self.copies:
            copy.wait_recv()

    def finish(self):
        self.hold()
        self.done = self.done + (self.axis,)

    def drain(self):
        for copy in self.sent:
            copy.wait_send()


class Rounds:
    def __init__(self, slots, send, recv, entry=0, order=("x", "y", "z")):
        self.slots, self.send, self.recv, self.sent = slots, send, recv, []
        self.entry, self.order = entry, order

    def begin(self, phase, rows):
        self.phase, axis = phase, self.order[phase]
        me = lax.axis_index(axis)
        for at, value in rows:
            self.slots[phase, me, at] = value
        self.copies = []
        for step, peer in enumerate(ring(axis)[1:]):
            spot = self.slots.at[phase, me]
            at = (self.entry, phase, step)
            copy = push(spot, spot, self.send.at[at], self.recv.at[at], {axis: peer})
            copy.start()
            self.copies.append(copy)

    def finish(self):
        for copy in self.copies:
            copy.wait_recv()
        self.sent += self.copies

    def drain(self):
        for copy in self.sent:
            copy.wait_send()


class Prefix(Rounds):
    def start(self, pair, backward):
        self.backward, self.cur, self.head = backward, pair, None
        self.share(0)

    def share(self, phase):
        self.begin(phase, [(slice(0, 1), self.cur[0]), (slice(1, 2), self.cur[1])])

    def step(self):
        self.finish()
        me = lax.axis_index(self.order[self.phase])
        run = (jnp.ones_like(self.cur[0]), jnp.zeros_like(self.cur[1]))
        mine = run
        for j in (3, 2, 1, 0) if self.backward else (0, 1, 2, 3):
            take = me == j
            mine = (jnp.where(take, run[0], mine[0]), jnp.where(take, run[1], mine[1]))
            fac, val = self.slots[self.phase, j, 0:1], self.slots[self.phase, j, 1:2]
            run = (run[0] * fac, val + fac * run[1])
        self.cur = run
        if self.head is None:
            self.head = mine
        else:
            self.head = (mine[0] * self.head[0], self.head[1] + self.head[0] * mine[1])
        if self.phase < 2:
            self.share(self.phase + 1)
        return self.head


class Total(Rounds):
    def start(self, value):
        self.begin(0, [(slice(None), value)])

    def step(self):
        self.finish()
        at = self.slots
        k = self.phase
        value = (at[k, 0] + at[k, 1]) + (at[k, 2] + at[k, 3])
        if k + 1 < len(self.order):
            self.begin(k + 1, [(slice(None), value)])
        return value


def axis_peers():
    return [{axis: ring(axis)[step]} for axis in AXES for step in (1, 2, 3)]


def along_seq(distance):
    place = lax.axis_index("z") * 16 + lax.axis_index("y") * 4 + lax.axis_index("x")
    place = lax.rem(place + distance + 64, 64)
    return {"z": place // 16, "y": lax.rem(place // 4, 4), "x": lax.rem(place, 4)}


CHUNKS = ((0, 384), (384, 512), (896, 384))
SUM_ORDERS = (
    (("x", "y", "z"), ("y", "z", "x"), ("z", "x", "y")),
    (("z", "y", "x"), ("x", "z", "y"), ("y", "x", "z")),
    (("y", "z", "x"), ("x", "y", "z"), ("z", "x", "y")),
)
ROW_HALVES = (pl.ds(0, 16), pl.ds(16, 16))
BANDS = ((0, 16), (16, 16), (32, 16))


def gelu_parts(x):
    inner = GELU_C * (x + GELU_A * x * x * x)
    t = jnp.tanh(inner)
    slope = GELU_C * (1.0 + 3.0 * GELU_A * x * x)
    return 0.5 * x * (1.0 + t), 0.5 * (1.0 + t) + 0.5 * x * (1.0 - t * t) * slope


FAR, UP, DOWN, ME = 0, 1, 2, 3


class RingSum:
    def __init__(self, part, got, one, two, send, recv, sib_send, sib_recv):
        self.part, self.got, self.one, self.two = part, got, one, two
        self.send, self.recv, self.sib_send, self.sib_recv = send, recv, sib_send, sib_recv
        self.core, self.sums, self.sent = lax.axis_index("mp"), {}, []

    def across(self, *slots):
        for slot in slots:
            copy = push(
                self.part.at[slot, 1 - self.core],
                self.got.at[slot],
                self.sib_send.at[slot],
                self.sib_recv.at[slot],
                {"mp": 1 - self.core},
            )
            copy.start()
            self.sums[slot] = copy

    def add(self, dst, src):
        dst[...] = (dst[...].astype(F32) + src[...].astype(F32)).astype(dst.dtype)

    def collect(self, slot):
        self.sums[slot].wait_recv()
        self.add(self.got.at[slot], self.part.at[slot, self.core])

    def far(self):
        self.collect(FAR)
        half = self.one.shape[1]
        _, up, _, down = ring("x")
        self.first = []
        for way, peer in enumerate((up, down)):
            piece = self.got.at[FAR, pl.ds(way * half, half)]
            at = (0, way)
            copy = push(piece, self.one.at[way], self.send.at[at], self.recv.at[at], {"x": peer})
            copy.start()
            self.first.append(copy)

    def near(self):
        half = self.one.shape[1]
        _, up, _, down = ring("x")
        self.second = []
        for way, (peer, slot) in enumerate(((up, UP), (down, DOWN))):
            self.collect(slot)
            self.first[way].wait_recv()
            self.add(self.got.at[slot, pl.ds(way * half, half)], self.one.at[way])
            at = (1, way)
            copy = push(self.got.at[slot], self.two.at[way], self.send.at[at], self.recv.at[at], {"x": peer})
            copy.start()
            self.second.append(copy)

    def total(self):
        self.sums[ME].wait_recv()
        total = self.got[ME].astype(F32) + self.part[ME, self.core].astype(F32)
        for way in range(2):
            self.second[way].wait_recv()
            total = total + self.two[way].astype(F32)
        return total

    def drain(self):
        for copy in self.first + self.second + list(self.sums.values()):
            copy.wait_send()


def ring_sum_scratch(rows, width):
    return [
        pltpu.VMEM((4, rows, width), BF16),
        pltpu.VMEM((2, rows // 2, width), BF16),
        pltpu.VMEM((2, rows, width), BF16),
        DMA((2, 2)),
        DMA((2, 2)),
        DMA((4,)),
        DMA((4,)),
    ]


def mlp_kernel(
    nm_ref, go_ref, hidden_ref, inv_ref, gain_ref, go_hbm, w_hbm,
    grad_hidden_ref, low_ref, term_ref, dw_ref, opart_out,
    go, w, gathered, npart, opart, mlp_in, ggu, gmi, low_half,
    load_sem, wsend, wrecv, gsend, grecv, gsib_send, gsib_recv, core_sem, *sum_refs,
):
    rows, width = nm_ref.shape
    half = rows // 2
    units = mlp_in.shape[1]
    me, up, far, down = ring("x")
    core = lax.axis_index("mp")
    other = {"mp": 1 - core}
    loads = [pltpu.make_async_copy(nm_ref, gathered.at[ME, core], load_sem.at[0])]
    wide = w.shape[4] // 2
    full, every = pl.ds(0, 4), pl.ds(0, w.shape[3])
    last = (("z", 0), ("y", wide))

    def weight_set(axis, index, at, cols):
        return ((index, full) if axis == "z" else (full, index)) + (full, at, pl.ds(cols, wide))

    for e, (axis, cols) in enumerate(last):
        here, ahead, _, behind = ring(axis)
        for k, index in enumerate((here, ahead, behind)):
            spot = weight_set(axis, index, every, cols)
            loads.append(pltpu.make_async_copy(w_hbm.at[spot], w.at[spot], load_sem.at[1 + 3 * e + k]))
    for slot, chip in ((FAR, far), (UP, up), (DOWN, down), (ME, me)):
        at = pl.ds(slot * 2 * rows, 2 * rows)
        loads.append(pltpu.make_async_copy(go_hbm.at[chip], go.at[at], load_sem.at[7 + slot]))
    for load in loads:
        load.start()
    peers = [{"x": up}, {"x": down}, other]
    for axis in ("y", "z"):
        peers += [{axis: ring(axis)[1]}, {axis: ring(axis)[3]}]
    greet(peers)
    top, low = pl.ds(0, half), pl.ds(half, half)
    first = []
    for way, (peer, slot) in enumerate(((up, DOWN), (down, UP))):
        spot = gathered.at[slot, core]
        copy = push(nm_ref, spot, gsend.at[0, way], grecv.at[0, way], {"x": peer})
        copy.start()
        first.append(copy)
    across = [push(nm_ref, gathered.at[ME, core], gsib_send.at[0], gsib_recv.at[0], other)]
    across[0].start()
    rest = []
    for e, (axis, cols) in enumerate(last):
        _, ahead, _, behind = ring(axis)
        deep = w.shape[3] // 2
        for way, (peer, origin) in enumerate(((ahead, behind), (behind, ahead))):
            spot = weight_set(axis, origin, pl.ds(way * deep, deep), cols)
            copy = push(w_hbm.at[spot], w.at[spot], wsend.at[e, way], wrecv.at[e, way], {axis: peer})
            copy.start()
            rest.append(copy)
    second = []
    for way, (peer, slot, piece) in enumerate(((up, DOWN, top), (down, UP, low))):
        first[way].wait_recv()
        spot = gathered.at[slot, core]
        copy = push(
            spot.at[piece], gathered.at[FAR, core, piece], gsend.at[1, way], grecv.at[1, way], {"x": peer}
        )
        copy.start()
        second.append(copy)
        copy = push(spot, spot, gsib_send.at[1 + way], gsib_recv.at[1 + way], other)
        copy.start()
        across.append(copy)
    for copy in rest:
        copy.wait_recv()
    for load in loads:
        load.wait()

    def tile(j, start=0):
        return pl.ds(pl.multiple_of(start + j * 256, 256), 256)

    def columns(at):
        return w[:, :, :, :, at].reshape(width, 256)

    def shard_tile(i, at):
        return w[i // 2, pl.ds(2 * lax.rem(i, 2), 2), :, :, at].reshape(256, -1)

    def grad_tile(j, carry):
        gmi[:, tile(j)] = dot(go[...], columns(tile(j, 2 * units)))
        return carry

    lax.fori_loop(0, units // 256, grad_tile, 0)
    for way, piece in enumerate((top, low)):
        second[way].wait_recv()
        spot = gathered.at[FAR, core, piece]
        copy = push(spot, spot, gsib_send.at[3 + way], gsib_recv.at[3 + way], other)
        copy.start()
        across.append(copy)

    def tokens_step(slot):
        at = pl.ds(slot * 2 * rows, 4 * rows)

        def hidden_tile(j, carry):
            tokens_in = gathered[slot : slot + 2].reshape(4 * rows, width)
            gate = dot(tokens_in, columns(tile(j)))
            up_lin = dot(tokens_in, columns(tile(j, units)))
            grad = gmi[at, tile(j)]
            act, slope = gelu_parts(gate)
            mlp_in[at, tile(j)] = (act * up_lin).astype(BF16)
            ggu[at, tile(j)] = (slope * (grad * up_lin)).astype(BF16)
            ggu[at, tile(j, units)] = (grad * act).astype(BF16)
            return carry

        lax.fori_loop(0, units // 256, hidden_tile, 0)

        def back_tile(j, carry):
            back = dot_t(ggu[at], shard_tile(j, pl.ds(0, 2 * units)))
            npart[slot : slot + 2, :, :, tile(j)] = back.astype(BF16).reshape(2, 2, rows, 256)
            return carry

        lax.fori_loop(0, width // 256, back_tile, 0)

    def out_tile(j, carry):
        part = dot_t(mlp_in[...], shard_tile(j, pl.ds(2 * units, units)))
        opart[:, :, :, tile(j)] = part.astype(BF16).reshape(4, 2, rows, 256)
        return carry

    def weight_grads(lower, upper):
        def step(i, carry):
            left = gathered[:, :, :, tile(i)].reshape(8 * rows, 256)
            dw_ref[tile(i), pl.ds(0, 2 * units)] = outer(left, ggu[...]).astype(BF16)
            dw_ref[tile(i), pl.ds(2 * units, units)] = outer(go[:, tile(i)], mlp_in[...]).astype(BF16)
            return carry

        lax.fori_loop(lower, upper, step, 0)

    sums = RingSum(npart, *sum_refs)
    for copy in across:
        copy.wait_recv()
    tokens_step(FAR)
    sums.across(FAR, UP)
    sums.far()
    tokens_step(DOWN)
    sums.across(DOWN, ME)
    sums.near()
    lax.fori_loop(0, width // 256, out_tile, 0)
    save = pltpu.make_async_copy(opart, opart_out, load_sem.at[11])
    save.start()
    weight_grads(0, 5)
    grad_normed = sums.total()
    hat = hidden_ref[...] * inv_ref[...]
    grad_hat = grad_normed * gain_ref[...]
    inner = jnp.mean(grad_hat * hat, axis=-1, keepdims=True)
    grad_hidden = go_ref[...].astype(F32) + inv_ref[...] * (grad_hat - hat * inner)
    grad_hidden_ref[...] = grad_hidden
    term_ref[...] = jnp.sum(grad_normed * hat, axis=0, keepdims=True)
    low_half[...] = grad_hidden.astype(BF16)
    low_ref[core] = low_half[...]
    swap = push(low_half, low_ref.at[core], core_sem.at[0], core_sem.at[1], other)
    swap.start()
    weight_grads(5, 8)
    swap.wait()
    save.wait()
    sums.drain()
    for copy in first + second + across + rest:
        copy.wait_send()


def mlp(normed, grad_out, hidden, inverse, gain, grad_out_all, weights, cid):
    rows, width = normed.shape
    units = weights.shape[4] // 3

    def block(dtype, *shape):
        return pltpu.VMEM(shape, dtype)

    return pl.pallas_call(
        mlp_kernel,
        out_shape=[
            jax.ShapeDtypeStruct((rows, width), F32),
            jax.ShapeDtypeStruct((2, rows, width), BF16),
            jax.ShapeDtypeStruct((1, width), F32),
            jax.ShapeDtypeStruct((width, 3 * units), BF16),
            jax.ShapeDtypeStruct((4, 2, rows, width), BF16),
        ],
        in_specs=[VM] * 5 + [ANY] * 2,
        out_specs=[VM] * 4 + [HBM],
        scratch_shapes=[
            block(BF16, 8 * rows, width),
            block(BF16, *weights.shape),
            block(BF16, 4, 2, rows, width),
            block(BF16, 4, 2, rows, width),
            block(BF16, 4, 2, rows, width),
            block(BF16, 8 * rows, units),
            block(BF16, 8 * rows, 2 * units),
            block(F32, 8 * rows, units),
            block(BF16, rows, width),
        ]
        + [DMA((12,)), DMA((2, 2)), DMA((2, 2)), DMA((2, 2)), DMA((2, 2)), DMA((5,)), DMA((5,)), DMA((2,))]
        + ring_sum_scratch(rows, width),
        compiler_params=params(cid, 60),
    )(normed, grad_out, hidden, inverse, gain, grad_out_all.reshape(4, 2 * rows, width), weights)


def lanes(n):
    return pl.ds(pl.multiple_of(n * BLOCK, BLOCK), BLOCK)


def minus_expm1(x):
    series = jnp.ones_like(x)
    for k in (9, 8, 7, 6, 5, 4, 3, 2):
        series = 1.0 + x * (1.0 / k) * series
    return jnp.where(x > -0.4, -x * series, 1.0 - jnp.exp(x))


CONV_W, CONV_B, RATES, BIAS, CONV_STATE, H_INIT, SLOPE = 0, 4, 5, 6, 8, 11, 12


def rec_forward_kernel(*refs):
    (
        tokens_ref, gain_ref, gain_mlp_ref, conv_w_ref, conv_b_ref, rates_ref, slope_ref, bias_ref, conv_state_ref,
        h_init_ref, starts_ref, valid_ref, lin_in, gate_in, back_in, mlp0, mlp1, mlp2, cot_ref, g_hbm,
        lin_out, gate_out, back_out, mlp_out, ext_out, act_out, mixed_out, reset_out, input_out, f_out, states_out,
        branch_out, normed_out, go_all, inv_ref, rms_ref, hidden_ref, nm_ref, inv_mlp_ref, rms_mlp_ref, go_ref, v_ref,
        wl, wg, wb, ext, gate_lin, mixed_v, reset_v, input_v, f_v, states, branch_v, normed, tail_in, driven, cf_v,
        part, part_low, part_in, g_v, rms_v, slots, mask_ref,
        tail_sem, load_sem, save_sem, own_sem, move_send, move_recv, send, recv, small_send, small_recv, core_sem,
        go_send, go_recv, go_sib_send, go_sib_recv,
    ) = refs
    count, width = tokens_ref.shape
    rec = f_v.shape[1]
    blocks = rec // BLOCK
    half = count // 2
    core = lax.axis_index("mp")
    other = {"mp": 1 - core}
    here = tuple(lax.axis_index(name) for name in AXES)
    load = pltpu.make_async_copy(g_hbm, g_v, load_sem)
    load.start()
    owns = [
        pltpu.make_async_copy(lin_in, wl.at[here], own_sem.at[0]),
        pltpu.make_async_copy(gate_in, wg.at[here], own_sem.at[1]),
        pltpu.make_async_copy(back_in, wb.at[here], own_sem.at[2]),
    ]
    units = mlp_out.shape[4] // 3
    every = pl.ds(0, lin_in.shape[0])

    def quarter(k, chip):
        return (mlp0, mlp1, mlp2)[k].at[every, pl.ds(pl.multiple_of(chip * units, units), units)]

    spots = [mlp_out.at[here + (every, pl.ds(k * units, units))] for k in range(3)]
    owns += [pltpu.make_async_copy(quarter(k, here[2]), spots[k], own_sem.at[3 + k]) for k in range(3)]
    for own in owns:
        own.start()
    greet(axis_peers() + [other, along_seq(1), along_seq(-1)])
    tail_copy = push(tokens_ref.at[pl.ds(count - 16, 16)], tail_in, tail_sem.at[0], tail_sem.at[1], along_seq(1))
    tail_copy.start()
    lin = [Gather(e, wl, ORDERS[e], CHUNKS[e], send, recv, ring_rounds=(2,)) for e in range(3)]
    gate = [
        Gather(3 + e, wg, ORDERS[(e + 1) % 3], CHUNKS[e], send, recv, ring_rounds=(1, 2)) for e in range(3)
    ]
    back = [
        Gather(6 + e, wb, ORDERS[(2, 1, 0)[e]], CHUNKS[e], send, recv, ring_rounds=(1, 2)) for e in range(3)
    ]
    rest = gate + back
    wide = mlp_out.shape[4] // 2
    mlp_flows = [
        Gather(9 + e, mlp_out, order, (e * wide, wide), send, recv, done=("x",), ring_rounds=(1,))
        for e, order in enumerate((("y", "z"), ("z", "y")))
    ]

    def each(group, name, *args):
        for flow in group:
            getattr(flow, name)(*args)

    each(lin, "begin", 0, lin_in)
    moves = []
    for step, peer in enumerate(ring("x")[1:]):
        for k in range(3):
            copy = push(quarter(k, peer), spots[k], move_send.at[step, k], move_recv.at[step, k], {"x": peer})
            copy.start()
            moves.append(copy)
    each(gate, "begin", 0, gate_in)
    each(back, "begin", 0, back_in)

    v_ref[CONV_W : CONV_W + CONV] = conv_w_ref[...]
    v_ref[BIAS : BIAS + 2] = bias_ref[...]
    v_ref[CONV_STATE : CONV_STATE + EDGE] = conv_state_ref[...]
    for at, ref in ((CONV_B, conv_b_ref), (RATES, rates_ref), (SLOPE, slope_ref), (H_INIT, h_init_ref)):
        v_ref[at : at + 1] = ref[...].reshape(1, rec)
    v_ref[SLOPE + 1 :] = jnp.zeros((15 - SLOPE, rec), F32)
    square = (count, count)
    diagonal = lax.broadcasted_iota(jnp.int32, square, 0) == lax.broadcasted_iota(jnp.int32, square, 1)
    for k, row in enumerate((1.0 - starts_ref[...].astype(F32), valid_ref[...].astype(F32))):
        spread = jnp.where(diagonal, jnp.broadcast_to(row.reshape(1, count), square), 0.0)
        mask_ref[:, k : k + 1] = jnp.sum(spread, axis=1, keepdims=True)

    def norm(values):
        mean_sq = jnp.mean(values * values, axis=-1, keepdims=True)
        inverse = lax.rsqrt(mean_sq + EPSILON)
        return values * inverse, inverse, jnp.sqrt(mean_sq + EPSILON)

    def norm_step(i, carry):
        at = pl.ds(pl.multiple_of(i * 64, 64), 64)
        hat, inverse, rms = norm(tokens_ref[at].astype(F32))
        inv_ref[at] = inverse
        rms_ref[at] = rms
        normed[pl.ds(pl.multiple_of(16 + i * 64, 16), 64)] = (hat * gain_ref[...]).astype(BF16)
        return carry

    lax.fori_loop(0, count // 64, norm_step, 0)
    for own in owns:
        own.wait()
    each(lin, "finish")
    each(lin, "begin", 1)
    each(rest, "finish")
    tail_copy.wait_recv()
    normed[0:16] = (norm(tail_in[...].astype(F32))[0] * gain_ref[...]).astype(BF16)
    saves = []

    def save(src, dst):
        copy = pltpu.make_async_copy(src, dst, save_sem.at[len(saves)])
        copy.start()
        saves.append(copy)

    save(normed.at[pl.ds(16, count)], normed_out)
    each(lin, "finish")
    each(lin, "begin", 2)
    each(rest, "begin", 1)
    each(lin, "middle")
    each(rest, "middle")
    for copy in moves:
        copy.wait_recv()
    each(mlp_flows, "begin", 0)
    each(rest, "finish")
    each(rest, "begin", 2)
    mine = pl.ds(pl.multiple_of(core * half, half), half)
    go_ref[...] = (cot_ref[mine].astype(F32) * mask_ref[mine, 1:2]).astype(BF16)
    load.wait()
    each(lin, "finish")
    save(wl, lin_out)
    is_first = (here[0] + here[1] + here[2]) == 0

    def rec_step(n, carry):
        at = lanes(n)
        ext[:, at] = dot(normed[...], wl[:, :, :, :, at].reshape(width, BLOCK))

        @pl.when(is_first)
        def _():
            ext[16 - EDGE : 16, at] = v_ref[CONV_STATE : CONV_STATE + EDGE, at]

        total = v_ref[CONV_B : CONV_B + 1, at] + jnp.zeros((count, BLOCK), F32)
        for k in range(CONV):
            total = total + v_ref[CONV_W + k : CONV_W + k + 1, at] * ext[pl.ds(16 - EDGE + k, count), at]
        mixed = total.astype(BF16)
        mixed_v[:, at] = mixed
        reset = jax.nn.sigmoid(dot(mixed, g_v[0, n]) + v_ref[BIAS : BIAS + 1, at])
        gated = jax.nn.sigmoid(dot(mixed, g_v[1, n]) + v_ref[BIAS + 1 : BIAS + 2, at])
        reset_v[:, at] = reset
        input_v[:, at] = gated
        log_decay = -8.0 * v_ref[RATES : RATES + 1, at] * reset
        f_v[:, at] = jnp.exp(log_decay) * mask_ref[:, 0:1]
        driven[:, at] = jnp.sqrt(minus_expm1(2.0 * log_decay)) * gated * mixed.astype(F32)
        return carry

    lax.fori_loop(0, blocks, rec_step, 0)
    for src, dst in ((ext, ext_out), (mixed_v, mixed_out), (reset_v, reset_out), (input_v, input_out), (f_v, f_out)):
        save(src, dst)

    def group(i, carry):
        base = pl.multiple_of(i * 8, 8)
        f, d = f_v[pl.ds(base, 8)], driven[pl.ds(base, 8)]
        cf, cd = carry
        cfs, cds = [], []
        for r in range(8):
            cf = cf * f[r : r + 1]
            cd = cd * f[r : r + 1] + d[r : r + 1]
            cfs.append(cf)
            cds.append(cd)
        cf_v[pl.ds(base, 8)] = jnp.concatenate(cfs, axis=0)
        states[pl.ds(pl.multiple_of(base + 8, 8), 8)] = jnp.concatenate(cds, axis=0)
        return cf, cd

    zero = jnp.zeros((1, rec), F32)
    ends = lax.fori_loop(0, count // 8, group, (zero + 1.0, zero))
    prefix = Prefix(slots, small_send, small_recv)
    prefix.start(ends, False)
    prefix.step()
    prefix.step()
    each(rest, "middle")
    each(mlp_flows, "finish")
    each(mlp_flows, "begin", 1)
    x_here, x_up, x_far, x_down = ring("x")
    spot = go_all.at[x_here, core]
    save(go_ref, spot)
    go_first = []
    for way, peer in enumerate((x_up, x_down)):
        copy = push(go_ref, spot, go_send.at[0, way], go_recv.at[0, way], {"x": peer})
        copy.start()
        go_first.append(copy)
    go_across = [push(go_ref, spot, go_sib_send.at[0], go_sib_recv.at[0], other)]
    go_across[0].start()
    head = prefix.step()
    carry_in = head[1] + head[0] * v_ref[H_INIT : H_INIT + 1]
    each(gate, "finish")
    save(wg, gate_out)

    def gate_step(n, carry):
        gate_lin[:, lanes(n)] = dot(normed[16:], wg[:, :, :, :, lanes(n)].reshape(width, BLOCK))
        return carry

    lax.fori_loop(0, blocks, gate_step, 0)
    save(gate_lin, act_out)
    states[0:8] = jnp.broadcast_to(carry_in, (8, rec))

    def branch_step(n, carry):
        at = lanes(n)
        value = states[8:, at] + cf_v[:, at] * states[0:1, at]
        states[8:, at] = value
        branch_v[:, at] = (gelu_parts(gate_lin[:, at])[0] * value).astype(BF16)
        return carry

    go_second = []
    for way, (peer, origin) in enumerate(((x_up, x_down), (x_down, x_up))):
        go_first[way].wait_recv()
        spot = go_all.at[origin, core]
        piece = spot.at[pl.ds(way * (half // 2), half // 2)]
        copy = push(piece, piece, go_send.at[1, way], go_recv.at[1, way], {"x": peer})
        copy.start()
        go_second.append(copy)
        copy = push(spot, spot, go_sib_send.at[1 + way], go_sib_recv.at[1 + way], other)
        copy.start()
        go_across.append(copy)
    lax.fori_loop(0, blocks, branch_step, 0)
    save(states, states_out)
    save(branch_v, branch_out)
    each(back, "finish")
    save(wb, back_out)

    def out_step(i, carry):
        at = pl.ds(pl.multiple_of(i * 256, 256), 256)
        rows = wb[i // 2, pl.ds(2 * lax.rem(i, 2), 2)].reshape(256, rec)
        value = dot_t(branch_v[...], rows)
        part[0, :, at] = value[:half]
        part[1, :, at] = value[half:]
        return carry

    lax.fori_loop(0, width // 256, out_step, 0)
    part_low[...] = part[1 - core].astype(BF16)
    part_copy = push(part_low, part_in, core_sem.at[0], core_sem.at[1], other)
    part_copy.start()
    for way in range(2):
        go_second[way].wait_recv()
        piece = go_all.at[x_far, core, pl.ds(way * (half // 2), half // 2)]
        copy = push(piece, piece, go_sib_send.at[3 + way], go_sib_recv.at[3 + way], other)
        copy.start()
        go_across.append(copy)
    part_copy.wait_recv()
    hidden = tokens_ref[mine].astype(F32) + (part[core] + part_in[...].astype(F32))
    hidden_ref[...] = hidden
    hat, inverse, rms = norm(hidden)
    inv_mlp_ref[...] = inverse
    rms_v[...] = jnp.broadcast_to(rms, (half, 128))
    rms_mlp_ref[core] = rms_v[...]
    rms_copy = push(rms_v, rms_mlp_ref.at[core], core_sem.at[2], core_sem.at[3], other)
    rms_copy.start()
    nm_ref[...] = (hat * gain_mlp_ref[...]).astype(BF16)
    each(mlp_flows, "hold")
    rms_copy.wait()
    for copy in go_across:
        copy.wait()
    for copy in go_first + go_second:
        copy.wait_send()
    for copy in moves:
        copy.wait_send()
    for copy in saves:
        copy.wait()
    each(lin, "drain")
    each(rest, "drain")
    each(mlp_flows, "drain")
    prefix.drain()
    part_copy.wait_send()
    tail_copy.wait_send()


def rec_forward(tokens, gain_rec, gain_mlp, vectors, masks, lin, gate, back, mlp_weights, cotangent, gates, cid):
    count, width = tokens.shape
    rows, rec = lin.shape
    half = count // 2

    def cube(last):
        return (4, 4, 4, rows, last)

    def sds(shape, dtype):
        return jax.ShapeDtypeStruct(shape, dtype)

    saved = [
        (cube(rec), BF16),
        (cube(rec), BF16),
        (cube(rec), BF16),
        (cube(3 * mlp_weights[0].shape[1] // 4), BF16),
        ((count + 16, rec), F32),
        ((count, rec), F32),
        ((count, rec), BF16),
        ((count, rec), F32),
        ((count, rec), F32),
        ((count, rec), F32),
        ((count + 8, rec), F32),
        ((count, rec), BF16),
        ((count, width), BF16),
        ((4, 2, half, width), BF16),
    ]
    small = [
        ((count, 1), F32),
        ((count, 1), F32),
        ((half, width), F32),
        ((half, width), BF16),
        ((half, 1), F32),
        ((2, half, 128), F32),
        ((half, width), BF16),
        ((16, rec), F32),
    ]
    scratch = saved[:3] + saved[4:12] + [((count + 16, width), BF16), ((16, width), BF16)]
    scratch += [((count, rec), F32), ((count, rec), F32), ((2, half, width), F32)]
    scratch += [((half, width), BF16), ((half, width), BF16), (gates.shape, BF16), ((half, 128), F32), ((3, 4, 2, rec), F32), ((count, 2), F32)]
    return pl.pallas_call(
        rec_forward_kernel,
        out_shape=[sds(*one) for one in saved + small],
        in_specs=[VM] * 19 + [ANY],
        out_specs=[HBM] * len(saved) + [VM] * len(small),
        scratch_shapes=[pltpu.VMEM(*one) for one in scratch]
        + [
            DMA((2,)),
            DMA,
            DMA((13,)),
            DMA((6,)),
            DMA((3, 3)),
            DMA((3, 3)),
            DMA((11, 3, 2, 3)),
            DMA((11, 3, 2, 3)),
            DMA((1, 3, 3)),
            DMA((1, 3, 3)),
            DMA((4,)),
            DMA((2, 2)),
            DMA((2, 2)),
            DMA((5,)),
            DMA((5,)),
        ],
        compiler_params=params(cid, 60),
    )(tokens, gain_rec[None], gain_mlp[None], *vectors, *masks, lin, gate, back, *mlp_weights, cotangent, gates)


G_BIAS, G_LAM, G_CONV_W, G_CONV_B, G_H, G_STATE = 0, 2, 3, 7, 8, 9
GATE_ROWS = 48


def shard_rows(ref, i, value):
    value = value.reshape(2, 4, 32, value.shape[1])
    ref[i // 2, pl.ds(2 * lax.rem(i, 2), 2)] = value


def rec_back_kernel(
    gh_ref, branch_ref, normed_ref, gate_ref, states_ref, f_ref, v_ref, hidden_ref,
    wb_hbm, ext_hbm, mixed_hbm, reset_hbm, input_hbm, g_hbm, wg_hbm, opart_hbm, wl_hbm,
    small_ref, part_ref, gates_out, result_ref, dw_out_hbm, dw_gate_hbm, dw_lin_hbm,
    wb, ext, mixed_v, reset_v, input_v, g_v, wg, opart, gate_low, low, cb, al, gm, dw_out, dw_gate, gg,
    tail, edge, edge_in, slots, result_half,
    *refs,
):
    bufs, refs = refs[:18], refs[18:]
    load_sem, save_sem, small_send, small_recv, edge_sem, own_sem, send, recv, core_sem = refs[:9]
    sum_refs = refs[9:]
    count, rec = gate_ref.shape
    half = count // 2
    width = gh_ref.shape[1]
    blocks = rec // BLOCK
    pairs = (
        (wb_hbm, wb), (ext_hbm, ext), (mixed_hbm, mixed_v), (reset_hbm, reset_v), (input_hbm, input_v), (g_hbm, g_v),
        (wg_hbm, wg), (opart_hbm, opart),
    )
    loads = [pltpu.make_async_copy(src, dst, load_sem.at[k]) for k, (src, dst) in enumerate(pairs)]
    for load in loads:
        load.start()
    saves = []

    def save(src, dst):
        copy = pltpu.make_async_copy(src, dst, save_sem.at[len(saves)])
        copy.start()
        saves.append(copy)

    ahead, behind = along_seq(1), along_seq(-1)
    other = {"mp": 1 - lax.axis_index("mp")}
    greet(axis_peers() + [ahead, behind, other])
    place = lax.axis_index("z") * 16 + lax.axis_index("y") * 4 + lax.axis_index("x")
    is_first = jnp.where(place == 0, 1.0, 0.0)
    has_next = jnp.where(place == 63, 0.0, 1.0)

    def weight_grad(ref, left, right):
        def step(i, carry):
            cols = pl.ds(pl.multiple_of(i * 256, 256), 256)
            shard_rows(ref, i, outer(left[:, cols], right[...]).astype(BF16))
            return carry

        lax.fori_loop(0, left.shape[1] // 256, step, 0)

    loads[0].wait()

    def branch_step(n, carry):
        grad = dot(gh_ref[...], wb[:, lanes(n)])
        act, slope = gelu_parts(gate_ref[:, lanes(n)])
        gate_low[:, lanes(n)] = (slope * (grad * states_ref[8:, lanes(n)])).astype(BF16)
        al[:, lanes(n)] = grad * act
        return carry

    lax.fori_loop(0, blocks, branch_step, 0)
    loads.append(pltpu.make_async_copy(wl_hbm, wb, load_sem.at[8]))
    loads[-1].start()
    loads[7].wait()
    sums = RingSum(opart, *sum_refs)
    sums.across(FAR, UP, DOWN, ME)

    def group(i, carry):
        base = pl.multiple_of(count - 8 - i * 8, 8)
        f, d = f_ref[pl.ds(base, 8)], al[pl.ds(base, 8)]
        follow, cf, cd = carry
        cfs, cds = [None] * 8, [None] * 8
        for r in (7, 6, 5, 4, 3, 2, 1, 0):
            cf = cf * follow
            cd = cd * follow + d[r : r + 1]
            cfs[r], cds[r] = cf, cd
            follow = f[r : r + 1]
        cb[pl.ds(base, 8)] = jnp.concatenate(cfs, axis=0)
        al[pl.ds(base, 8)] = jnp.concatenate(cds, axis=0)
        return follow, cf, cd

    zero = jnp.zeros((1, rec), F32)
    follow, cf, cd = lax.fori_loop(0, count // 8, group, (zero + 1.0, zero + 1.0, zero))
    prefix = Prefix(slots, small_send, small_recv)
    prefix.start((follow * cf, follow * cd), True)
    weight_grad(dw_out, gh_ref, branch_ref)
    save(dw_out, dw_out_hbm)
    prefix.step()
    sums.far()
    weight_grad(dw_gate, normed_ref, gate_low)
    save(dw_gate, dw_gate_hbm)
    prefix.step()
    for load in loads[1:7] + loads[8:]:
        load.wait()

    def part_tile(i, carry):
        at = pl.ds(pl.multiple_of(i * 256, 256), 256)
        value = dot_t(gate_low[...], wg[at, :])
        part_ref[0, :, at] = value[:half]
        part_ref[1, :, at] = value[half:]
        return carry

    lax.fori_loop(0, width // 256, part_tile, 0)
    later = prefix.step()[1]
    sums.near()
    al[...] = al[...] + cb[...] * later

    def grads_step(n, carry):
        at = lanes(n)
        adjoint = al[:, at]
        factors, reset, gated = f_ref[:, at], reset_v[:, at], input_v[:, at]
        mixed_low = mixed_v[:, at]
        mixed = mixed_low.astype(F32)
        rates = v_ref[RATES : RATES + 1, at]
        log_decay = -8.0 * rates * reset
        decays = jnp.exp(log_decay)
        scale_in = jnp.sqrt(minus_expm1(2.0 * log_decay))
        grad_log = adjoint * states_ref[pl.ds(7, count), at] * factors
        grad_log = grad_log - adjoint * gated * mixed * decays * decays / scale_in
        small_ref[G_LAM : G_LAM + 1, at] = (
            8.0 * jnp.sum(grad_log * reset, axis=0, keepdims=True) * v_ref[SLOPE : SLOPE + 1, at]
        )
        small_ref[G_H : G_H + 1, at] = is_first * factors[0:1] * adjoint[0:1]
        grad_reset = (grad_log * (-8.0 * rates) * reset * (1.0 - reset)).astype(BF16)
        grad_input = (adjoint * scale_in * mixed * gated * (1.0 - gated)).astype(BF16)
        for g, grad in enumerate((grad_reset, grad_input)):
            small_ref[G_BIAS + g : G_BIAS + g + 1, at] = jnp.sum(
                grad.astype(F32), axis=0, keepdims=True
            )
            b = g * blocks + n
            rows = pl.ds(pl.multiple_of(16 * lax.rem(b, 3), 16), 16)
            gg[:, :, b // 3, rows, :] = outer(mixed_low, grad).astype(BF16).reshape(4, 4, 16, BLOCK)
        grad_mixed = adjoint * scale_in * gated
        grad_mixed = grad_mixed + dot_t(grad_reset, g_v[0, n]) + dot_t(grad_input, g_v[1, n])
        gm[0:8] = jnp.zeros((8, BLOCK), F32)
        gm[8 : 8 + count] = grad_mixed
        gm[8 + count :] = jnp.zeros((8, BLOCK), F32)
        small_ref[G_CONV_B : G_CONV_B + 1, at] = jnp.sum(grad_mixed, axis=0, keepdims=True)
        total = jnp.zeros((count, BLOCK), F32)
        front = jnp.zeros((8, BLOCK), F32)
        for k in range(CONV):
            small_ref[G_CONV_W + k : G_CONV_W + k + 1, at] = jnp.sum(
                grad_mixed * ext[pl.ds(16 - EDGE + k, count), at], axis=0, keepdims=True
            )
            weight = v_ref[CONV_W + k : CONV_W + k + 1, at]
            total = total + weight * gm[pl.ds(8 + EDGE - k, count)]
            front = front + weight * gm[pl.ds(8 - k, 8)]
        low[:, at] = total.astype(BF16)
        tail[:, at] = total[count - 16 :]
        edge[:, at] = front
        small_ref[G_STATE : G_STATE + EDGE, at] = is_first * front[:EDGE]
        small_ref[G_STATE + EDGE :, at] = jnp.zeros((16 - G_STATE - EDGE, BLOCK), F32)
        return carry

    for x, j in ((3, 1), (3, 2)):
        gg[:, :, x, 16 * j : 16 * j + 16, :] = jnp.zeros((4, 4, 16, BLOCK), BF16)
    lax.fori_loop(0, blocks, grads_step, 0)
    edge_copy = push(edge, edge_in, edge_sem.at[0], edge_sem.at[1], behind)
    edge_copy.start()
    gates = [
        Scatter(
            e, gg, (0, BLOCK), ORDERS[e], None, bufs[6 * e : 6 * e + 6], gates_out, own_sem, send, recv, BANDS[e]
        )
        for e in range(3)
    ]

    def each(name, *args):
        for flow in gates:
            getattr(flow, name)(*args)

    each("begin", 0)
    saves[0].wait()
    edge_copy.wait_recv()
    last = jnp.concatenate([tail[0:13], tail[13:16] + has_next * edge_in[0:EDGE]], axis=0)
    low[count - 16 :] = last.astype(BF16)
    weight_grad(dw_out, normed_ref, low)
    save(dw_out, dw_lin_hbm)
    each("finish")
    each("begin", 1)

    def rest_tile(i, carry):
        at = pl.ds(pl.multiple_of(i * 256, 256), 256)
        value = dot_t(low[...], wb[at, :])
        part_ref[0, :, at] = part_ref[0, :, at] + value[:half]
        part_ref[1, :, at] = part_ref[1, :, at] + value[half:]
        return carry

    lax.fori_loop(0, width // 256, rest_tile, 0)
    each("finish")
    each("begin", 2)
    core = lax.axis_index("mp")
    result_half[...] = (hidden_ref[...] + sums.total()).astype(BF16)
    result_ref[core] = result_half[...]
    result_copy = push(result_half, result_ref.at[core], core_sem.at[0], core_sem.at[1], other)
    result_copy.start()
    each("finish")
    result_copy.wait()
    for copy in saves[1:]:
        copy.wait()
    each("drain")
    sums.drain()
    prefix.drain()
    edge_copy.wait_send()


def rec_back(
    gh, branch, normed, gate_lin, states_ext, factors, vectors, hidden,
    w_back, ext, mixed, reset, gated, gates, w_gate, mlp_part, w_lin, cid,
):
    count, rec = gate_lin.shape
    half, width = hidden.shape

    def like(array):
        return pltpu.VMEM(array.shape, array.dtype)

    wide, low = pltpu.VMEM((count, rec), F32), pltpu.VMEM((count, rec), BF16)
    cube = (4, 4, 4, width // 64, rec)
    bufs = []
    for _ in range(3):
        bufs += scatter_buffers(GATE_ROWS // 3, BLOCK, False)
    return pl.pallas_call(
        rec_back_kernel,
        out_shape=[
            jax.ShapeDtypeStruct((16, rec), F32),
            jax.ShapeDtypeStruct((2, half, width), F32),
            jax.ShapeDtypeStruct((GATE_ROWS, BLOCK), F32),
            jax.ShapeDtypeStruct((2, half, width), BF16),
            jax.ShapeDtypeStruct(cube, BF16),
            jax.ShapeDtypeStruct(cube, BF16),
            jax.ShapeDtypeStruct(cube, BF16),
        ],
        in_specs=[VM] * 8 + [ANY] * 9,
        out_specs=[VM] * 4 + [HBM] * 3,
        scratch_shapes=[
            like(w_back), like(ext), like(mixed), like(reset), like(gated), like(gates), like(w_gate), like(mlp_part),
            low, low, wide, wide, pltpu.VMEM((count + 16, BLOCK), F32),
            pltpu.VMEM(cube, BF16), pltpu.VMEM(cube, BF16), pltpu.VMEM((4, 4, 4, GATE_ROWS, BLOCK), BF16),
            pltpu.VMEM((16, rec), F32), pltpu.VMEM((8, rec), F32), pltpu.VMEM((8, rec), F32),
            pltpu.VMEM((3, 4, 2, rec), F32), pltpu.VMEM((half, width), BF16),
        ]
        + bufs
        + [
            DMA((9,)),
            DMA((3,)),
            DMA((1, 3, 3)),
            DMA((1, 3, 3)),
            DMA((2,)),
            DMA((3, 3)),
            DMA((3, 3, 3, 3)),
            DMA((3, 3, 3, 3)),
            DMA((2,)),
        ]
        + ring_sum_scratch(half, width),
        compiler_params=params(cid, 61),
    )(
        gh, branch, normed, gate_lin, states_ext, factors, vectors, hidden,
        w_back, ext, mixed, reset, gated, gates, w_gate, mlp_part, w_lin,
    )


def rec_end_kernel(
    part, small_ref, gain_term_ref, gh_ref, tokens_in, inverse_ref, gain_ref, gates_in,
    dw0, dw1, dw2,
    total_ref, gains_ref, all_gates_ref, out0, out1, out2, tokens_hbm,
    *refs,
):
    bufs, refs = refs[: 9 * 8], refs[9 * 8 :]
    (
        part_low, part_in, tokens_v, gates_ref, ring_gains, gains0, small0, small1, small2,
        load_sem, own_sem, send, recv, gsend, grecv, small_send, small_recv, ring_send, ring_recv, core_sem,
    ) = refs
    half, width = gh_ref.shape
    core = lax.axis_index("mp")
    other = {"mp": 1 - core}
    x_here = lax.axis_index("x")
    greet(axis_peers() + [other] + [{"x": peer, "mp": 1 - core} for peer in ring("x")[1:]])
    small = [
        Total(slots, small_send, small_recv, e, ORDERS[e])
        for e, slots in enumerate((small0, small1, small2))
    ]
    for flow, (start, wide) in zip(small, CHUNKS):
        flow.start(small_ref[:, start : start + wide])
    part_low[...] = part[1 - core].astype(BF16)
    part_copy = push(part_low, part_in, core_sem.at[0], core_sem.at[1], other)
    part_copy.start()
    flows = [
        Scatter(
            e, (dw0, dw1, dw2)[e // 3], CHUNKS[e % 3], SUM_ORDERS[e // 3][e % 3], ROW_HALVES,
            bufs[8 * e : 8 * e + 8], (out0, out1, out2)[e // 3], own_sem, send, recv,
        )
        for e in range(9)
    ]
    one, two, three = flows[:3], flows[3:6], flows[6:]
    spread = [Gather(e, gates_ref, ORDERS[e], (0, BLOCK), gsend, grecv, band=BANDS[e]) for e in range(3)]

    def each(group, name, *args):
        for flow in group:
            getattr(flow, name)(*args)

    gates_ref[lax.axis_index("z"), lax.axis_index("y"), x_here] = gates_in[...].astype(BF16)
    each(spread, "begin", 0)
    each(one, "begin", 0)
    part_copy.wait_recv()
    grad_normed = part[core] + part_in[...].astype(F32)
    hat = tokens_in[...].astype(F32) * inverse_ref[...]
    gain_term = jnp.sum(grad_normed * hat, axis=0, keepdims=True)
    quarter = width // 4
    for k in range(4):
        cols = slice(k * quarter, (k + 1) * quarter)
        ring_gains[x_here, core, k : k + 1] = gain_term[:, cols]
        ring_gains[x_here, core, 4 + k : 5 + k] = gain_term_ref[:, cols]
    shares = []
    spot = ring_gains.at[x_here, core]
    group = [{"x": x, "mp": c} for x in ring("x") for c in (core, 1 - core)][1:]
    for k, peer in enumerate(group):
        copy = push(spot, spot, ring_send.at[k], ring_recv.at[k], peer)
        copy.start()
        shares.append(copy)
    each(two, "begin", 0)
    grad_hat = grad_normed * gain_ref[...]
    inner = jnp.mean(grad_hat * hat, axis=-1, keepdims=True)
    tokens_v[...] = gh_ref[...] + inverse_ref[...] * (grad_hat - hat * inner)
    token_copy = push(tokens_v, tokens_hbm.at[core], core_sem.at[2], core_sem.at[3], other)
    token_copy.start()
    token_save = pltpu.make_async_copy(tokens_v, tokens_hbm.at[core], load_sem.at[1])
    token_save.start()
    for flow in small:
        flow.step()
    each(spread, "finish")
    each(spread, "begin", 1)
    each(one, "middle")
    for copy in shares:
        copy.wait_recv()
    gains = Total(gains0, small_send, small_recv, 3, ("y", "z"))
    halves = [ring_gains[x, 0] + ring_gains[x, 1] for x in range(4)]
    gains.start((halves[0] + halves[1]) + (halves[2] + halves[3]))
    each(three, "begin", 0)
    each(two, "middle")
    for flow in small:
        flow.step()
    each(spread, "finish")
    each(spread, "begin", 2)
    gains.step()
    each(one, "finish")
    each(one, "begin", 1)
    each(three, "middle")
    each(two, "finish")
    each(two, "begin", 1)
    each(one, "finish")
    each(one, "begin", 2)
    for flow, (start, wide) in zip(small, CHUNKS):
        total_ref[:, start : start + wide] = flow.step()
    gains_ref[...] = gains.step()
    each(spread, "finish")

    def unpack(b, carry):
        at = pl.ds(pl.multiple_of(16 * lax.rem(b, 3), 16), 16)
        all_gates_ref[b] = gates_ref[:, :, b // 3, at, :].reshape(BLOCK, BLOCK).astype(F32)
        return carry

    lax.fori_loop(0, all_gates_ref.shape[0], unpack, 0)
    each(three, "finish")
    each(three, "begin", 1)
    each(two, "finish")
    each(two, "begin", 2)
    each(one, "finish")
    each(three, "finish")
    each(three, "begin", 2)
    each(two, "finish")
    each(three, "finish")
    for copy in (token_copy, token_save):
        copy.wait()
    each(flows + spread + small, "drain")
    gains.drain()
    for copy in shares + [part_copy]:
        copy.wait_send()


def rec_end(part, small, gain_term, grad_hidden, tokens, inverse, gain, gates, weights, cid):
    half, width = grad_hidden.shape
    rows, rec = weights[0].shape[3:]
    gate_blocks = 2 * rec // BLOCK

    def sds(*shape):
        return jax.ShapeDtypeStruct(shape, F32)

    bufs = []
    for e in range(9):
        bufs += scatter_buffers(rows, CHUNKS[e % 3][1], True)
    return pl.pallas_call(
        rec_end_kernel,
        out_shape=[
            sds(16, rec),
            sds(8, width // 4),
            sds(gate_blocks, BLOCK, BLOCK),
            sds(rows, rec),
            sds(rows, rec),
            sds(rows, rec),
            sds(2, half, width),
        ],
        in_specs=[VM] * 8 + [ANY] * 3,
        out_specs=[VM] * 6 + [HBM],
        scratch_shapes=bufs
        + [
            pltpu.VMEM((half, width), BF16),
            pltpu.VMEM((half, width), BF16),
            pltpu.VMEM((half, width), F32),
            pltpu.VMEM((4, 4, 4) + gates.shape, BF16),
            pltpu.VMEM((4, 2, 8, width // 4), F32),
            pltpu.VMEM((2, 4, 8, width // 4), F32),
        ]
        + [pltpu.VMEM((3, 4, 16, wide), F32) for _, wide in CHUNKS]
        + [
            DMA((2,)),
            DMA((9, 3)),
            DMA((9, 3, 3, 3)),
            DMA((9, 3, 3, 3)),
            DMA((3, 3, 1, 3)),
            DMA((3, 3, 1, 3)),
            DMA((4, 3, 3)),
            DMA((4, 3, 3)),
            DMA((7,)),
            DMA((7,)),
            DMA((4,)),
        ],
        compiler_params=params(cid, 60),
    )(part, small, gain_term, grad_hidden, tokens, inverse, gain, gates, *weights)


def mlp_end_kernel(in_ref, back, send, recv):
    x_here = lax.axis_index("x")
    peers = ring("x")[1:]
    greet([{"x": peer} for peer in peers])
    moves = []
    for step, peer in enumerate(peers):
        copy = push(in_ref.at[peer], back.at[x_here], send.at[step], recv.at[step], {"x": peer})
        copy.start()
        moves.append(copy)
    back[x_here] = in_ref[x_here]
    for copy in moves:
        copy.wait()


def mlp_end(quarters, cid):
    return pl.pallas_call(
        mlp_end_kernel,
        out_shape=jax.ShapeDtypeStruct(quarters.shape, quarters.dtype),
        in_specs=[VM],
        out_specs=VM,
        scratch_shapes=[DMA((3,)), DMA((3,))],
        compiler_params=params(cid, 61),
    )(quarters)


def finish_kernel(
    small_hbm, gains_hbm, out_hbm, gate_hbm, lin_hbm, back_hbm, result_in, tokens_in, gates_in,
    result_ref, tokens_ref, gates_ref, rec_ref, out_ref, mlp_ref, down_ref, bias_ref, lam_ref, conv_w_ref, conv_b_ref,
    gain_rec_ref, gain_mlp_ref, h_ref, state_ref,
    small_ref, gains_ref, out_sums, gate_sums, lin_sums, back, result_v, tokens_v, gates_v, sem, out_sem,
):
    pairs = (
        (result_in, result_v), (tokens_in, tokens_v), (gates_in, gates_v),
        (small_hbm, small_ref), (gains_hbm, gains_ref), (out_hbm, out_sums), (gate_hbm, gate_sums),
        (lin_hbm, lin_sums), (back_hbm, back),
    )
    loads = [pltpu.make_async_copy(src, dst, sem.at[k]) for k, (src, dst) in enumerate(pairs)]
    for load in loads:
        load.start()
    copies = []
    for k, (src, dst) in enumerate(((result_v, result_ref), (tokens_v, tokens_ref), (gates_v, gates_ref))):
        loads[k].wait()
        copies.append(pltpu.make_async_copy(src, dst, out_sem.at[k]))
        copies[k].start()
    for load in loads[3:]:
        load.wait()
    rec_ref[:, 0, :] = gate_sums[...]
    rec_ref[:, 1, :] = lin_sums[...]
    out_ref[...] = out_sums[...]
    units = down_ref.shape[1] // 4
    for q in range(4):
        value = back[q].astype(F32)
        at = pl.ds(q * units, units)
        for k in range(2):
            mlp_ref[:, k, at] = value[:, k * units : (k + 1) * units]
        down_ref[:, at] = value[:, 2 * units :]
    bias_ref[...] = small_ref[G_BIAS : G_BIAS + 2]
    lam_ref[...] = small_ref[G_LAM]
    conv_w_ref[...] = small_ref[G_CONV_W : G_CONV_W + CONV]
    conv_b_ref[...] = small_ref[G_CONV_B]
    h_ref[...] = small_ref[G_H]
    state_ref[...] = small_ref[G_STATE : G_STATE + EDGE]
    quarter = gains_ref.shape[1]
    for k in range(4):
        at = pl.ds(k * quarter, quarter)
        gain_rec_ref[at] = gains_ref[k]
        gain_mlp_ref[at] = gains_ref[4 + k]
    for copy in copies:
        copy.wait()


def finish(small, gains, sums, back, result, tokens, gates):
    rec = small.shape[1]
    rows = back.shape[1]
    units = back.shape[2] // 3
    width = gains.size // 2

    def sds(*shape):
        return jax.ShapeDtypeStruct(shape, F32)

    return pl.pallas_call(
        finish_kernel,
        out_shape=[
            jax.ShapeDtypeStruct(result.shape, result.dtype),
            sds(*tokens.shape),
            sds(*gates.shape),
            sds(rows, 2, rec),
            sds(rows, rec),
            sds(rows, 2, 4 * units),
            sds(rows, 4 * units),
            sds(2, rec),
            sds(rec),
            sds(CONV, rec),
            sds(rec),
            sds(width),
            sds(width),
            sds(rec),
            sds(EDGE, rec),
        ],
        in_specs=[HBM] * 9,
        out_specs=[HBM] * 3 + [VM] * 12,
        scratch_shapes=[pltpu.VMEM(a.shape, a.dtype) for a in (small, gains, *sums, back, result, tokens, gates)]
        + [DMA((9,)), DMA((3,))],
        compiler_params=pltpu.CompilerParams(vmem_limit_bytes=61 * MIB),
    )(small, gains, *sums, back, result, tokens, gates)


def body(
    tokens,
    cotangent,
    starts,
    valid,
    w_rec,
    w_out,
    w_mlp,
    w_down,
    lru_gates,
    lru_bias,
    lam,
    conv_w,
    conv_b,
    gain_rec,
    gain_mlp,
    h_init,
    conv_state,
):
    count, width = tokens.shape
    shard, _, rec = w_rec.shape
    hidden_units = w_mlp.shape[2] // 4
    half = count // 2
    core = lax.axis_index("mp")

    def my_half(array):
        return lax.dynamic_slice_in_dim(array, core * half, half, axis=0)

    (
        w_lin, w_gate, w_back, mlp_weights, ext, gate_lin, mixed, reset, gated, factors, states_ext, branch_in,
        normed_rec, grad_out_all, inverse_rec, rms_rec, hidden, normed_mlp, inverse_mlp, rms_half, grad_out, vectors,
    ) = rec_forward(
        tokens,
        gain_rec,
        gain_mlp,
        (conv_w, conv_b, jax.nn.softplus(-lam), jax.nn.sigmoid(-lam), lru_bias, conv_state, h_init),
        (starts, valid),
        w_rec[:, 1],
        w_rec[:, 0],
        w_out.T,
        (w_mlp[:, 0], w_mlp[:, 1], w_down.T),
        cotangent,
        lru_gates,
        0,
    )
    w_lin, w_gate, w_back = (w.reshape(width, rec) for w in (w_lin, w_gate, w_back))
    grad_hidden, grad_hidden_low, gain_mlp_term, mlp_terms, mlp_part = mlp(
        normed_mlp, grad_out, hidden, inverse_mlp, gain_mlp[None], grad_out_all, mlp_weights, 1
    )
    mlp_sums = lax.psum_scatter(mlp_terms, ("z", "y"), scatter_dimension=0, tiled=True)
    grad_hidden_low = grad_hidden_low.reshape(count, width)
    small, normed_part, gate_terms, result, *weight_terms = rec_back(
        grad_hidden_low,
        branch_in,
        normed_rec,
        gate_lin,
        states_ext,
        factors,
        vectors,
        hidden,
        w_back,
        ext,
        mixed,
        reset,
        gated,
        lru_gates,
        w_gate,
        mlp_part,
        w_lin,
        2,
    )
    small, gains, gate_blocks, out_sums, gate_sums, lin_sums, grad_tokens = rec_end(
        normed_part,
        small,
        gain_mlp_term,
        grad_hidden,
        my_half(tokens),
        my_half(inverse_rec),
        gain_rec[None],
        gate_terms,
        weight_terms,
        3,
    )
    back = mlp_end(mlp_sums.reshape(4, shard, 3 * hidden_units), 4)
    (
        result, grad_tokens, grad_gates, grad_w_rec, grad_out_t, grad_w_mlp, grad_down_t, grad_bias, grad_lam,
        grad_conv_w, conv_bias_gradient, grad_gain_rec, grad_gain_mlp, grad_h_init, grad_conv_state,
    ) = finish(
        small,
        gains,
        (out_sums, gate_sums, lin_sums),
        back,
        result.reshape(count, width),
        grad_tokens.reshape(count, width),
        gate_blocks.reshape(lru_gates.shape),
    )
    return (
        result,
        rms_rec[:, 0],
        rms_half[:, :, 0].reshape(count),
        grad_tokens,
        grad_w_rec,
        grad_out_t.T,
        grad_w_mlp,
        grad_down_t.T,
        grad_gates,
        grad_bias,
        grad_lam,
        grad_conv_w,
        conv_bias_gradient,
        grad_gain_rec,
        grad_gain_mlp,
        grad_h_init,
        grad_conv_state,
    )


def solution(mesh):
    cube = Mesh(mesh.devices.reshape(4, 4, 4, 2), ("z", "y", "x", "mp"))
    placed = (
        P(SEQ, None),
        P(SEQ, None),
        P(SEQ),
        P(SEQ),
        P(SEQ, None, "mp"),
        P("mp", SEQ),
        P(SEQ, None, "mp"),
        P("mp", SEQ),
        P(None, "mp", None, None),
        P(None, "mp"),
        P("mp"),
        P(None, "mp"),
        P("mp"),
        P(),
        P(),
        P("mp"),
        P(None, "mp"),
    )
    return jax.shard_map(
        body,
        mesh=cube,
        in_specs=placed,
        out_specs=(
            P(SEQ, None),
            P(SEQ),
            P(SEQ),
            P(SEQ, None),
            P(SEQ, None, "mp"),
            P("mp", SEQ),
            P(SEQ, None, "mp"),
            P("mp", SEQ),
            P(None, "mp", None, None),
            P(None, "mp"),
            P("mp"),
            P(None, "mp"),
            P("mp"),
            P(),
            P(),
            P("mp"),
            P(None, "mp"),
        ),
        check_vma=False,
    )
```

time: 463 us -> 392 us (0.85)
  Pallas kernels: 410 us -> 368 us
  local copies, waits for them, and re-layouts: 27.8 us -> 7.67 us
  other arithmetic: 9.71 us -> 1.99 us
    pallas_call x3 -> x5, Pallas kernels: 271 us -> 247 us  [the longest x1 99.4 us: rec_end(): pl.pallas_call(rec_end_kernel, out_shape=[sds(16, rec), sds(8, width // 4...]
    pallas_call x1, Pallas kernels: 138 us -> 121 us  [rec_forward(): pl.pallas_call(rec_forward_kernel, out_shape=[sds(*one) for one in saved...]
    unnamed x38 -> x8, local copies, waits for them, and re-layouts: 8.32 us -> 0.88 us
    slice x6 -> x2, local copies, waits for them, and re-layouts: 7.86 us -> 2.47 us  [the longest x1 1.79 us: body(): w_mlp[:, 1]]
  transfers between devices with their start and end apart: 2 -> 1, of which waited for: 0 -> 0; matrix products, arithmetic and copies ran while one was open for 4% -> 1% of each run, Pallas kernels for 55% -> 41%
where the time goes in v3:
time: 392 us
  Pallas kernels  368 us (94%)
  between operations  14.1 us (4%)
  local copies, waits for them, and re-layouts  7.67 us (2%)
    pallas_call x1, Pallas kernels, rec_forward(): pl.pallas_call(rec_forward_kernel, out_shape=[sds(*one) for one in saved...  121 us
    pallas_call x1, Pallas kernels, rec_end(): pl.pallas_call(rec_end_kernel, out_shape=[sds(16, rec), sds(8, width // 4...  99.4 us
    pallas_call x1, Pallas kernels, mlp(): pl.pallas_call(mlp_kernel, out_shape=[jax.ShapeDtypeStruct((rows, width),...  69.8 us
    pallas_call x1, Pallas kernels, rec_back(): pl.pallas_call(rec_back_kernel, out_shape=[jax.ShapeDtypeStruct((16, rec)...  60.7 us
    pallas_call x1, Pallas kernels, mlp_end(): pl.pallas_call(mlp_end_kernel, out_shape=jax.ShapeDtypeStruct(quarters.sh...  10.7 us
  transfers between devices with their start and end apart: 1, of which 0 were waited for; matrix products, arithmetic and copies ran while one was open for 1% of the time, Pallas kernels for 41%

profile of v3, /device:TPU:0, one launch (start us, length us, event | category | flops | bytes accessed | tf_op | source)
XLA Modules:
  0.0 392.1 jit_solution(14053777093348893262)
XLA Ops:
  7.2 0.0 reduce-scatter.2.cloned.1.call-start
  7.2 1.8 fusion
  9.0 1.3 fusion.1
  10.3 1.3 add_divide_fusion
  11.6 0.9 copy_bitcast_fusion
  12.5 0.7 copy_bitcast_fusion.2
  13.2 121.5 %shard_map.296 = (bf16[4,4,4,32,1280]{4,3,2,1,0:T(8,128)(2,1)}, bf16[4,4,4,32,1280]{4,3,2,1,0:T(8,128)(2,1)}, bf16[4,4,4,32,1280]{4,3,2,1,0:T(8,128)(2,1)}, bf16...) custom-call(bf16[256,2048]{1,0:T(8,128)(2,1)} %refs_0_.1, ...), custom_call_target="tpu_custom_call" | custom-call | tf_op jit(solution)/shard_map/pallas_call | solution.py:951
  134.7 69.8 %shard_map.297 = (f32[128,2048]{1,0:T(8,128)}, bf16[2,128,2048]{2,1,0:T(8,128)(2,1)}, f32[1,2048]{1,0:T(1,128)}, bf16[2048,2304]{1,0:T(8,128)(2,1)}, bf16[4,2,128,2048]{3,2,1,0:T(8,128)(2,1)}) custom-call(bf16[128,2048]{1,0:T(8,128)(2,1)} %get-tuple-element.73.nm_ref, bf16[128,2048]{1,0:T(8,128)(2,1)} %get-tuple-element.74.go_ref, ...), custom_call_target="tpu_custom_call" | custom-call | tf_op jit(solution)/shard_map/pallas_call | solution.py:603
  204.5 0.0 copy-start.2
  204.5 0.0 reduce-scatter.2.cloned.1.call-update
  204.5 0.9 copy-done.2
  205.4 0.7 reduce
  206.1 0.0 copy-start.3
  206.1 0.0 copy-start
  206.1 60.7 %shard_map.298 = (f32[16,1280]{1,0:T(8,128)}, f32[2,128,2048]{2,1,0:T(8,128)}, f32[48,256]{1,0:T(8,128)}, bf16[2,128,2048]{2,1,0:T(8,128)(2,1)}, bf16[4,4,4,32,1...) custom-call(bf16[256,2048]{1,0:T(8,128)(2,1)} %bitcast.30, ...), custom_call_target="tpu_custom_call" | custom-call | tf_op jit(solution)/shard_map/pallas_call | solution.py:1200
  266.8 0.0 copy-done.3
  266.8 0.6 constant_dynamic-slice_fusion.inverse_ref
  267.4 0.0 copy-done
  267.4 0.8 constant_dynamic-slice_fusion.1.tokens_in
  268.3 0.0 copy-start.1
  268.3 99.4 %shard_map.299 = (f32[16,1280]{1,0:T(8,128)}, f32[8,512]{1,0:T(8,128)}, f32[10,256,256]{2,1,0:T(8,128)}, f32[32,1280]{1,0:T(8,128)}, f32[32,1280]{1,0:T(8,128)},...) custom-call(f32[2,128,2048]{2,1,0:T(8,128)} %get-tuple-element.94.part, f32[16,1280]{1,0:T(8,128)} %get-tuple-element.95.small_ref, ...), custom_call_target="tpu_custom_call" | custom-call | tf_op jit(solution)/shard_map/pallas_call | solution.py:1369
  367.7 0.0 copy-done.1
  367.7 0.7 slice_reduce_fusion
  368.3 0.0 reduce-scatter.2.cloned.1.call-done
  368.3 10.7 %shard_map.300.back_hbm = bf16[4,32,2304]{2,1,0:T(8,128)(2,1)} custom-call(bf16[4,32,2304]{2,1,0:T(8,128)(2,1)} %bitcast.32), custom_call_target="tpu_custom_call" | custom-call | tf_op jit(solution)/shard_map/pallas_call | solution.py:1424
  379.0 6.3 %shard_map.301 = (bf16[256,2048]{1,0:T(8,128)(2,1)}, f32[256,2048]{1,0:T(8,128)}, f32[2,5,256,256]{3,2,1,0:T(8,128)}, f32[32,2,1280]{2,1,0:T(2,128)}, f32[32,128...) custom-call(f32[16,1280]{1,0:T(8,128)} %get-tuple-element.103.small_, ...), custom_call_target="tpu_custom_call" | custom-call | tf_op jit(solution)/shard_map/pallas_call | solution.py:1489
Async XLA Ops:
  7.2 361.2 %reduce-scatter.2.cloned.1.call-start = ((), (), s32[]{:S(2)}) async-start(), calls=%async_computation.1 | async-start | bytes 10027008 | tf_op jit(solution)/shard_map/reduce_scatter | solution.py:1565
  204.5 0.9 copy-start.2
  206.1 60.7 %copy-start.3 = (f32[256,1]{1,0:T(8,128)S(1)}, f32[256,1]{1,0:T(8,128)}, u32[]{:S(2)}) copy-start(f32[256,1]{1,0:T(8,128)} %get-tuple-element.98) | copy-start | bytes 3076
  206.1 61.4 %copy-start = (bf16[256,2048]{1,0:T(8,128)(2,1)S(1)}, bf16[256,2048]{1,0:T(8,128)(2,1)}, u32[]{:S(2)}) copy-start(bf16[256,2048]{1,0:T(8,128)(2,1)} %refs_0_.1) | copy-start | bytes 3145732
  268.3 99.4 %copy-start.1 = (f32[2,128,128]{2,1,0:T(8,128)S(1)}, f32[2,128,128]{2,1,0:T(8,128)}, u32[]{:S(2)}) copy-start(f32[2,128,128]{2,1,0:T(8,128)} %get-tuple-element.114) | copy-start | bytes 393220
Sparse Core Ops, SparseCore 0:
  204.6 98.1 reduce-scatter.1
